TPU v7x, 32 devices: a whole 2x2x4 slice. The times are simulated.
32 devices in a mesh: dp: 8 (over z, x), tensor: 4 (over y, core).
Axes of the slice: x: 2, y: 2, z: 4, core: 2. Of those that a mesh axis runs over, the one named last changes fastest.
Arguments:
- tokens: bfloat16 [8, 2048, 768], P('dp', 'tensor'), may hold values from -6 to 6
- segment_ids: int32 [8, 2048], P('dp'), may hold values from -1 to 5, as said below
- query_weight: bfloat16 [768, 768], P(None, 'tensor'), may hold values from -0.21875 to 0.21875
- key_weight: bfloat16 [768, 768], P(None, 'tensor'), may hold values from -0.21875 to 0.21875
- value_weight: bfloat16 [768, 768], P(None, 'tensor'), may hold values from -0.21875 to 0.21875
- output_weight: bfloat16 [768, 768], P('tensor'), may hold values from -3.5 to 3.5
- attn_gain: float32 [768], replicated, may hold values from 0.5 to 1.5
- attn_shift: float32 [768], replicated, may hold values from -3 to 3
- gate_weight: bfloat16 [768, 3072], P(None, 'tensor'), may hold values from -0.21875 to 0.21875
- up_weight: bfloat16 [768, 3072], P(None, 'tensor'), may hold values from -0.21875 to 0.21875
- down_weight: bfloat16 [3072, 768], P('tensor'), may hold values from -0.109375 to 0.109375
- mlp_gain: float32 [768], replicated, may hold values from 0.5 to 1.5
- mlp_shift: float32 [768], replicated, may hold values from -3 to 3
- cotangent: bfloat16 [8, 2048, 768], P('dp', 'tensor'), may hold values from -6 to 6
Outputs:
- encoded: bfloat16 [8, 2048, 768], P('dp', 'tensor')
- grad_tokens: float32 [8, 2048, 768], P('dp', 'tensor')
- grad_query: float32 [768, 768], P(None, 'tensor')
- grad_key: float32 [768, 768], P(None, 'tensor')
- grad_value: float32 [768, 768], P(None, 'tensor')
- grad_output: float32 [768, 768], P('tensor')
- grad_attn_gain: float32 [768], replicated
- grad_attn_shift: float32 [768], replicated
- grad_gate: float32 [768, 3072], P(None, 'tensor')
- grad_up: float32 [768, 3072], P(None, 'tensor')
- grad_down: float32 [3072, 768], P('tensor')
- grad_mlp_gain: float32 [768], replicated
- grad_mlp_shift: float32 [768], replicated
Inputs may be any that keep to these rules, and one draw needn't show every extreme that they name: `segment_ids`: each packed row holds documents 0 to 5 in this order, each one or more positions long, followed by one or more padding positions marked -1.
All inputs are finite; a program needn't handle non-finite values.
Results may differ from a plain program's by a relative error of at most 0.019.
Values may be sent and summed in bfloat16 or wider, within the bound.
No kernel may reach another device: no remote copies, remote signals or barrier semaphores. Data moves between devices by JAX's collectives and lax.ppermute only.
A program may use at most 128 MiB of HBM per device.

v0:
```python
import math

import jax
import jax.numpy as jnp
from jax import lax
from jax.sharding import PartitionSpec as P

HEAD_DIM = 64


EPSILON = 1e-05
ROPE_BASE = 1000.0
MASKED = -1000000000.0
query_block = 512


def positions(segments):
    places = jnp.arange(segments.shape[0], dtype=jnp.int32)
    before = jnp.concatenate([segments[:1] - 1, segments[:-1]])
    starts = lax.cummax(jnp.where(segments != before, places, 0), axis=0)
    return (places - starts).astype(jnp.float32)


def rotary_tables(segments):
    half_dim = HEAD_DIM // 2
    angle_rate = ROPE_BASE ** (-(jnp.arange(half_dim, dtype=jnp.float32) * 2.0 / HEAD_DIM))
    angles = positions(segments)[:, None] * angle_rate[None, :]
    return (jnp.cos(angles), jnp.sin(angles))


def rotate(tensor, cosine_table, sine_table):
    half_dim = tensor.shape[-1] // 2
    first_half = tensor[..., :half_dim]
    second_half = tensor[..., half_dim:]
    cosine_part = cosine_table[:, None, :]
    sine_part = sine_table[:, None, :]
    return jnp.concatenate(
        [
            first_half * cosine_part - second_half * sine_part,
            second_half * cosine_part + first_half * sine_part,
        ],
        axis=-1,
    )


def norm_parts(row_values):
    centred = row_values - jnp.mean(row_values, axis=-1, keepdims=True)
    inverse = lax.rsqrt(jnp.mean(centred * centred, axis=-1, keepdims=True) + EPSILON)
    return (centred * inverse, inverse)


def norm_back(grad_norm, normalized, inverse):
    return inverse * (
        grad_norm
        - jnp.mean(grad_norm, axis=-1, keepdims=True)
        - normalized * jnp.mean(grad_norm * normalized, axis=-1, keepdims=True)
    )


def contract_rows(left_side, right_side):
    return lax.dot_general(
        left_side, right_side, (((0,), (0,)), ((), ())), preferred_element_type=jnp.float32
    )


def contract_cols(left_side, right_side):
    return lax.dot_general(
        left_side, right_side, (((1,), (1,)), ((), ())), preferred_element_type=jnp.float32
    )


def local(
    tokens,
    segment_ids,
    query_weight,
    key_weight,
    value_weight,
    output_weight,
    attn_gain,
    attn_shift,
    gate_weight,
    up_weight,
    down_weight,
    mlp_gain,
    mlp_shift,
    cotangent,
):
    local_rows = tokens[0]
    segments = segment_ids[0]
    seq_length = segments.shape[0]
    head_width = query_weight.shape[1]
    local_heads = head_width // HEAD_DIM
    ff_local = gate_weight.shape[1]
    block_rows = min(query_block, seq_length)
    block_count = seq_length // block_rows
    score_scale = 1.0 / math.sqrt(HEAD_DIM)
    cosine_table, sine_table = rotary_tables(segments)
    joint_weight = jnp.concatenate([query_weight, key_weight, value_weight], axis=1)
    mixed_weight = jnp.concatenate([gate_weight, up_weight], axis=1)
    full_rows = lax.all_gather(local_rows, "tensor", axis=0, tiled=True)
    projected = jnp.dot(full_rows, joint_weight, preferred_element_type=jnp.float32)
    shaped = projected.reshape(seq_length, 3, local_heads, HEAD_DIM)
    queries = rotate(shaped[:, 0], cosine_table, sine_table).astype(jnp.bfloat16)
    key_rows = rotate(shaped[:, 1], cosine_table, sine_table).astype(jnp.bfloat16)
    value_rows = shaped[:, 2].astype(jnp.bfloat16)
    query_blocks = queries.reshape(block_count, block_rows, local_heads, HEAD_DIM)
    segment_blocks = segments.reshape(block_count, block_rows)

    def block_scores(query_part, segment_part):
        scores = (
            jnp.einsum("qhd,khd->hqk", query_part, key_rows, preferred_element_type=jnp.float32)
            * score_scale
        )
        allowed = (segment_part[:, None] == segments[None, :])[None]
        return jnp.where(allowed, scores, MASKED)

    def attend(block_pair):
        query_part, segment_part = block_pair
        scores = block_scores(query_part, segment_part)
        row_peak = jnp.max(scores, axis=-1, keepdims=True)
        shifted = jnp.exp(scores - row_peak)
        row_total = jnp.sum(shifted, axis=-1, keepdims=True)
        soft_weights = (shifted / row_total).astype(jnp.bfloat16)
        context_part = jnp.einsum(
            "hqk,khd->qhd", soft_weights, value_rows, preferred_element_type=jnp.float32
        )
        return (context_part.astype(jnp.bfloat16), (row_peak + jnp.log(row_total))[..., 0])

    context_blocks, log_totals = lax.map(attend, (query_blocks, segment_blocks))
    context = context_blocks.reshape(seq_length, head_width)
    attended = lax.psum_scatter(
        jnp.dot(context, output_weight, preferred_element_type=jnp.float32),
        "tensor",
        scatter_dimension=0,
        tiled=True,
    )
    first_norm, first_inverse = norm_parts(local_rows.astype(jnp.float32) + attended)
    normed = first_norm * attn_gain + attn_shift
    normed_low = normed.astype(jnp.bfloat16)
    normed_full = lax.all_gather(normed_low, "tensor", axis=0, tiled=True)
    mixed_proj = jnp.dot(normed_full, mixed_weight, preferred_element_type=jnp.float32)
    gate_pre = mixed_proj[:, :ff_local]
    up_pre = mixed_proj[:, ff_local:]
    gate_sigmoid = jax.nn.sigmoid(gate_pre)
    activated = gate_pre * gate_sigmoid
    hidden = (activated * up_pre).astype(jnp.bfloat16)
    mlp_rows = lax.psum_scatter(
        jnp.dot(hidden, down_weight, preferred_element_type=jnp.float32).astype(jnp.bfloat16),
        "tensor",
        scatter_dimension=0,
        tiled=True,
    ).astype(jnp.float32)
    second_norm, second_inverse = norm_parts(normed + mlp_rows)
    encoded = (second_norm * mlp_gain + mlp_shift).astype(jnp.bfloat16)
    grad_encoded = cotangent[0].astype(jnp.float32)
    grad_mlp_gain = jnp.sum(grad_encoded * second_norm, axis=0)
    grad_mlp_shift = jnp.sum(grad_encoded, axis=0)
    grad_second = norm_back(grad_encoded * mlp_gain, second_norm, second_inverse)
    grad_mlp_full = lax.all_gather(grad_second.astype(jnp.bfloat16), "tensor", axis=0, tiled=True)
    grad_down = contract_rows(hidden, grad_mlp_full)
    grad_hidden = contract_cols(grad_mlp_full, down_weight)
    grad_gate_low = (
        grad_hidden * up_pre * gate_sigmoid * (1.0 + gate_pre * (1.0 - gate_sigmoid))
    ).astype(jnp.bfloat16)
    grad_up_low = (grad_hidden * activated).astype(jnp.bfloat16)
    grad_mixed_low = jnp.concatenate([grad_gate_low, grad_up_low], axis=1)
    grad_mixed = contract_rows(normed_full, grad_mixed_low)
    grad_normed = grad_second + lax.psum_scatter(
        contract_cols(grad_mixed_low, mixed_weight).astype(jnp.bfloat16),
        "tensor",
        scatter_dimension=0,
        tiled=True,
    ).astype(jnp.float32)
    grad_attn_gain = jnp.sum(grad_normed * first_norm, axis=0)
    grad_attn_shift = jnp.sum(grad_normed, axis=0)
    grad_first = norm_back(grad_normed * attn_gain, first_norm, first_inverse)
    grad_attn_full = lax.all_gather(grad_first.astype(jnp.bfloat16), "tensor", axis=0, tiled=True)
    grad_output = contract_rows(context, grad_attn_full)
    grad_context = contract_cols(grad_attn_full, output_weight).astype(jnp.bfloat16)
    grad_context_blocks = grad_context.reshape(block_count, block_rows, local_heads, HEAD_DIM)

    def attend_back(carried, block_args):
        key_grad, value_grad = carried
        query_part, segment_part, log_part, grad_part = block_args
        scores = block_scores(query_part, segment_part)
        soft_weights = jnp.exp(scores - log_part[..., None])
        grad_soft = jnp.einsum(
            "qhd,khd->hqk", grad_part, value_rows, preferred_element_type=jnp.float32
        )
        inner_total = jnp.sum(soft_weights * grad_soft, axis=-1, keepdims=True)
        grad_scores = (soft_weights * (grad_soft - inner_total)).astype(jnp.bfloat16)
        grad_query_part = (
            jnp.einsum("hqk,khd->qhd", grad_scores, key_rows, preferred_element_type=jnp.float32)
            * score_scale
        )
        key_grad = (
            key_grad
            + jnp.einsum(
                "hqk,qhd->khd", grad_scores, query_part, preferred_element_type=jnp.float32
            )
            * score_scale
        )
        value_grad = value_grad + jnp.einsum(
            "hqk,qhd->khd",
            soft_weights.astype(jnp.bfloat16),
            grad_part,
            preferred_element_type=jnp.float32,
        )
        return ((key_grad, value_grad), grad_query_part)

    zero_grad = jnp.zeros((seq_length, local_heads, HEAD_DIM), jnp.float32)
    (key_grad, value_grad), query_grad = lax.scan(
        attend_back,
        (zero_grad, zero_grad),
        (query_blocks, segment_blocks, log_totals, grad_context_blocks),
    )
    query_grad = query_grad.reshape(seq_length, local_heads, HEAD_DIM)
    grad_projected = jnp.concatenate(
        [
            rotate(query_grad, cosine_table, -sine_table).reshape(seq_length, head_width),
            rotate(key_grad, cosine_table, -sine_table).reshape(seq_length, head_width),
            value_grad.reshape(seq_length, head_width),
        ],
        axis=1,
    ).astype(jnp.bfloat16)
    grad_joint = contract_rows(full_rows, grad_projected)
    grad_tokens = grad_first + lax.psum_scatter(
        contract_cols(grad_projected, joint_weight).astype(jnp.bfloat16),
        "tensor",
        scatter_dimension=0,
        tiled=True,
    ).astype(jnp.float32)
    grad_joint, grad_output, grad_mixed, grad_down = lax.psum(
        (grad_joint, grad_output, grad_mixed, grad_down), "dp"
    )
    grad_attn_gain, grad_attn_shift, grad_mlp_gain, grad_mlp_shift = lax.psum(
        (grad_attn_gain, grad_attn_shift, grad_mlp_gain, grad_mlp_shift), ("dp", "tensor")
    )
    return (
        encoded[None],
        grad_tokens[None],
        grad_joint[:, :head_width],
        grad_joint[:, head_width : 2 * head_width],
        grad_joint[:, 2 * head_width :],
        grad_output,
        grad_attn_gain,
        grad_attn_shift,
        grad_mixed[:, :ff_local],
        grad_mixed[:, ff_local:],
        grad_down,
        grad_mlp_gain,
        grad_mlp_shift,
    )


def solution(mesh):
    return jax.shard_map(
        local,
        mesh=mesh,
        in_specs=(
            P("dp", "tensor", None),
            P("dp", None),
            P(None, "tensor"),
            P(None, "tensor"),
            P(None, "tensor"),
            P("tensor", None),
            P(),
            P(),
            P(None, "tensor"),
            P(None, "tensor"),
            P("tensor", None),
            P(),
            P(),
            P("dp", "tensor", None),
        ),
        out_specs=(
            P("dp", "tensor", None),
            P("dp", "tensor", None),
            P(None, "tensor"),
            P(None, "tensor"),
            P(None, "tensor"),
            P("tensor", None),
            P(),
            P(),
            P(None, "tensor"),
            P(None, "tensor"),
            P("tensor", None),
            P(),
            P(),
        ),
        check_vma=False,
    )
```

profile of v0, /device:TPU:0, one launch (start us, length us, event | category | flops | bytes accessed | tf_op | source)
XLA Modules:
  0.0 960.3 jit_solution(13282478357112428750)
XLA Ops:
  17.9 23.0 %all-gather.12.cloned.1.call-done = bf16[1,2048,768]{2,1,0:T(8,128)(2,1)} async-done(((bf16[1,512,768]{2,1,0:T(8,128)(2,1)}), bf16[1,2048,768]{2,1,0:T(8,128)(2,1)}) %all-gather.12.cloned.1.call-update) | async-done | bytes 3145744 | tf_op jit(solution)/shard_map/all_gather | solution.py:100
  46.0 85.4 %while.27 = (s32[]{:T(128)}, bf16[4,512,3,64]{1,3,2,0:T(8,128)(2,1)}, f32[4,3,512]{2,1,0:T(4,128)}, s32[4,512]{1,0:T(4,128)S(1)}, s32[1,2048]{1,0:T(1,128)S(1)},...) while((s32[]{:T(128)}, ...), condition=%wide.region_5.6_spmd, body=%wide.region_2.5_spmd.sunk | while | flops 844200448 | bytes 43974772 | solution.py:129
  52.6 6.8 fusion.129
  59.4 7.3 fusion.130
  80.7 7.3 fusion.130
  102.1 7.3 fusion.130
  123.4 7.3 fusion.130
  138.5 58.5 %reduce-scatter.5.cloned.1.call-done = f32[512,768]{1,0:T(8,128)} async-done(((f32[2048,768]{1,0:T(8,128)}), f32[512,768]{1,0:T(8,128)}) %reduce-scatter.5.cloned.1.call-update) | async-done | bytes 1572880 | tf_op jit(solution)/shard_map/reduce_scatter | solution.py:131
  205.8 24.8 %all-gather.6.cloned.1.call-done = bf16[2048,768]{1,0:T(8,128)(2,1)} async-done(((bf16[512,768]{1,0:T(8,128)(2,1)}), bf16[2048,768]{1,0:T(8,128)(2,1)}) %all-gather.6.cloned.1.call-update) | async-done | bytes 3145744 | tf_op jit(solution)/shard_map/all_gather | solution.py:140
  230.6 8.2 fusion.80
  249.2 38.1 %reduce-scatter.7.cloned.1.call-done = bf16[512,768]{1,0:T(8,128)(2,1)} async-done(((bf16[2048,768]{1,0:T(8,128)(2,1)}), bf16[512,768]{1,0:T(8,128)(2,1)}) %reduce-scatter.7.cloned.1.call-update) | async-done | bytes 786448 | tf_op jit(solution)/shard_map/reduce_scatter | solution.py:147
  293.1 28.6 %all-gather.8.cloned.1.call-done = bf16[2048,768]{1,0:T(8,128)(2,1)} async-done(((bf16[512,768]{1,0:T(8,128)(2,1)}), bf16[2048,768]{1,0:T(8,128)(2,1)}) %all-gather.8.cloned.1.call-update) | async-done | bytes 3145744 | tf_op jit(solution)/shard_map/all_gather | solution.py:159
  321.7 7.9 multiply_convert_fusion.2
  332.2 8.3 fusion.44
  340.6 38.1 %reduce-scatter.9.cloned.1.call-done = bf16[512,768]{1,0:T(8,128)(2,1)} async-done(((bf16[2048,768]{1,0:T(8,128)(2,1)}), bf16[512,768]{1,0:T(8,128)(2,1)}) %reduce-scatter.9.cloned.1.call-update) | async-done | bytes 786448 | tf_op jit(solution)/shard_map/reduce_scatter | solution.py:168
  384.0 28.6 %all-gather.10.cloned.1.call-done = bf16[2048,768]{1,0:T(8,128)(2,1)} async-done(((bf16[512,768]{1,0:T(8,128)(2,1)}), bf16[2048,768]{1,0:T(8,128)(2,1)}) %all-gather.10.cloned.1.call-update) | async-done | bytes 3145744 | tf_op jit(solution)/shard_map/all_gather | solution.py:177
  416.4 171.2 %while.28 = (s32[]{:T(128)}, f32[2048,3,64]{0,2,1:T(8,128)}, f32[2048,3,64]{0,2,1:T(8,128)}, f32[4,512,3,64]{1,0,3,2:T(4,128)}, bf16[4,512,3,64]{1,3,2,0:T(8,128...) while((s32[]{:T(128)}, f32[2048,3,64]{0,2,1:T(8,128)}, ...), condition=%wide.region_19.20_spmd.clone, body=%wide.region_17.19_spmd.clone.sunk | while | flops 2063563264 | bytes 151972176 | solution.py:212
  456.7 8.6 dynamic_update_slice.20
  497.4 8.6 dynamic_update_slice.20
  538.1 8.6 dynamic_update_slice.20
  578.8 8.6 dynamic_update_slice.20
  606.6 8.4 fusion.42
  621.1 40.7 %all-reduce = (f32[768]{0:T(1024)}, f32[768]{0:T(1024)}, f32[768]{0:T(1024)}, f32[768]{0:T(1024)}) all-reduce(f32[768]{0:T(1024)S(1)} %copy-done.44, f32[768]{0:T(1024)S(1)} %copy-done.45, f32[768]{0:T(1024)S(1)} %copy-done.43, f32[768]{0:T(1024)S(1)} %convert_reduce_fusion), channel_id=1, replica_groups=mesh['dp'=8,'tensor'=4] {'dp','tensor'}, use_global_device_ids=true, to_apply=%region_24.25 | all-reduce | flops 3072 | bytes 24576 | tf_op jit(solution)/shard_map/psum | solution.py:236
  664.3 279.2 %all-reduce.4.cloned.1.call-done = (f32[768,576]{0,1:T(8,128)}, f32[192,768]{1,0:T(8,128)}, f32[768,1536]{1,0:T(8,128)}, f32[768,768]{1,0:T(8,128)}) async-done(((f32[768,576]{0,1:T(8,128)}, f32[192,768]{1,0:T(8,128)}, f32[768,1536]{1,0:T(8,128)}, f32[768,768]{1,0:T(8,128)}), (f32[768,576]{0,1:T(8,128)}, f32[192,768]{1,0:T(8,128)}, f32[768,1536]{1,0:T(8,128)}, ...) | async-done | bytes 9437200 | tf_op jit(solution)/shard_map/psum | solution.py:233
  (290 shorter events, 271.3 us)
Async XLA Ops:
  7.2 237.9 %copy-start = (bf16[768,768]{1,0:T(8,128)(2,1)S(1)}, bf16[768,768]{1,0:T(8,128)(2,1)}, u32[]{:S(2)}) copy-start(bf16[768,768]{1,0:T(8,128)(2,1)} %param.28) | copy-start | bytes 3538948
  7.2 33.7 %all-gather.12.cloned.1.call-start = ((), (), s32[]{:S(2)}) async-start(), calls=%async_computation.11 | async-start | bytes 3932160 | tf_op jit(solution)/shard_map/all_gather | solution.py:100
  7.9 189.1 %reduce-scatter.5.cloned.1.call-start = ((), (), s32[]{:S(2)}) async-start(), calls=%async_computation.4 | async-start | bytes 7864320 | tf_op jit(solution)/shard_map/reduce_scatter | solution.py:131
  16.0 28.8 %copy-start.36 = (bf16[768,576]{0,1:T(8,128)(2,1)}, bf16[768,576]{0,1:T(8,128)(2,1)S(1)}, u32[]{:S(2)}) copy-start(bf16[768,576]{0,1:T(8,128)(2,1)S(1)} %constant_dynamic-update-slice_fusion) | copy-start | bytes 2654212
  17.9 27.4 %copy-start.22 = (f32[2048,32]{0,1:T(8,128)}, f32[2048,32]{0,1:T(8,128)S(1)}, u32[]{:S(2)}) copy-start(f32[2048,32]{0,1:T(8,128)S(1)} %get-tuple-element.267) | copy-start | bytes 786436
  138.5 92.1 %all-gather.6.cloned.1.call-start = ((), (), s32[]{:S(2)}) async-start(), calls=%async_computation.5 | async-start | bytes 3932160 | tf_op jit(solution)/shard_map/all_gather | solution.py:140
  201.9 85.3 %reduce-scatter.7.cloned.1.call-start = ((), (), s32[]{:S(2)}) async-start(), calls=%async_computation.6 | async-start | bytes 3932160 | tf_op jit(solution)/shard_map/reduce_scatter | solution.py:147
  249.2 72.6 %all-gather.8.cloned.1.call-start = ((), (), s32[]{:S(2)}) async-start(), calls=%async_computation.7 | async-start | bytes 3932160 | tf_op jit(solution)/shard_map/all_gather | solution.py:159
  293.0 85.6 %reduce-scatter.9.cloned.1.call-start = ((), (), s32[]{:S(2)}) async-start(), calls=%async_computation.8 | async-start | bytes 3932160 | tf_op jit(solution)/shard_map/reduce_scatter | solution.py:168
  340.5 38.2 %copy-start.39 = (f32[512]{0:T(512)S(1)}, f32[512]{0:T(512)}, u32[]{:S(2)}) copy-start(f32[512]{0:T(512)} %copy-done.38) | copy-start | bytes 6148
  340.5 38.2 %copy-start.40 = (f32[768]{0:T(1024)S(1)}, f32[768]{0:T(1024)}, u32[]{:S(2)}) copy-start(f32[768]{0:T(1024)} %param.24) | copy-start | bytes 9220
  340.5 38.2 %copy-start.42 = (f32[512]{0:T(512)S(1)}, f32[512]{0:T(512)}, u32[]{:S(2)}) copy-start(f32[512]{0:T(512)} %copy-done.41) | copy-start | bytes 6148
  340.5 72.0 %all-gather.10.cloned.1.call-start = ((), (), s32[]{:S(2)}) async-start(), calls=%async_computation.9 | async-start | bytes 3932160 | tf_op jit(solution)/shard_map/all_gather | solution.py:177
  381.8 30.7 %copy-start.35 = (bf16[192,768]{1,0:T(8,128)(2,1)S(1)}, bf16[192,768]{1,0:T(8,128)(2,1)}, u32[]{:S(2)}) copy-start(bf16[192,768]{1,0:T(8,128)(2,1)} %param.23) | copy-start | bytes 884740
  383.9 277.9 %reduce-scatter.11.cloned.1.call-start = ((), (), s32[]{:S(2)}) async-start(), calls=%async_computation.10 | async-start | bytes 3932160 | tf_op jit(solution)/shard_map/reduce_scatter | solution.py:227
  452.8 12.5 %copy-start.5 = (bf16[2048,3,64]{0,2,1:T(8,128)(2,1)S(1)}, bf16[2048,3,64]{0,2,1:T(8,128)(2,1)}, u32[]{:S(2)}) copy-start(bf16[2048,3,64]{0,2,1:T(8,128)(2,1)} %copy-done.4) | copy-start | bytes 2359300 | tf_op jit(solution)/shard_map/while
  492.9 13.1 %copy-start.5 = (bf16[2048,3,64]{0,2,1:T(8,128)(2,1)S(1)}, bf16[2048,3,64]{0,2,1:T(8,128)(2,1)}, u32[]{:S(2)}) copy-start(bf16[2048,3,64]{0,2,1:T(8,128)(2,1)} %copy-done.4) | copy-start | bytes 2359300 | tf_op jit(solution)/shard_map/while
  492.9 13.1 %copy-start.17 = (bf16[4,512,3,64]{1,3,2,0:T(8,128)(2,1)S(1)}, bf16[4,512,3,64]{1,3,2,0:T(8,128)(2,1)}, u32[]{:S(2)}) copy-start(bf16[4,512,3,64]{1,3,2,0:T(8,128)(2,1)} %copy-done.16) | copy-start | bytes 2359300 | tf_op jit(solution)/shard_map/while
  533.6 13.1 %copy-start.5 = (bf16[2048,3,64]{0,2,1:T(8,128)(2,1)S(1)}, bf16[2048,3,64]{0,2,1:T(8,128)(2,1)}, u32[]{:S(2)}) copy-start(bf16[2048,3,64]{0,2,1:T(8,128)(2,1)} %copy-done.4) | copy-start | bytes 2359300 | tf_op jit(solution)/shard_map/while
  533.6 13.1 %copy-start.17 = (bf16[4,512,3,64]{1,3,2,0:T(8,128)(2,1)S(1)}, bf16[4,512,3,64]{1,3,2,0:T(8,128)(2,1)}, u32[]{:S(2)}) copy-start(bf16[4,512,3,64]{1,3,2,0:T(8,128)(2,1)} %copy-done.16) | copy-start | bytes 2359300 | tf_op jit(solution)/shard_map/while
  574.3 13.1 %copy-start.5 = (bf16[2048,3,64]{0,2,1:T(8,128)(2,1)S(1)}, bf16[2048,3,64]{0,2,1:T(8,128)(2,1)}, u32[]{:S(2)}) copy-start(bf16[2048,3,64]{0,2,1:T(8,128)(2,1)} %copy-done.4) | copy-start | bytes 2359300 | tf_op jit(solution)/shard_map/while
  574.3 13.1 %copy-start.17 = (bf16[4,512,3,64]{1,3,2,0:T(8,128)(2,1)S(1)}, bf16[4,512,3,64]{1,3,2,0:T(8,128)(2,1)}, u32[]{:S(2)}) copy-start(bf16[4,512,3,64]{1,3,2,0:T(8,128)(2,1)} %copy-done.16) | copy-start | bytes 2359300 | tf_op jit(solution)/shard_map/while
  598.7 344.8 %all-reduce.4.cloned.1.call-start = ((), (), s32[]{:S(2)}) async-start(), calls=%async_computation.12 | async-start | bytes 18874368 | tf_op jit(solution)/shard_map/psum | solution.py:233
  619.8 42.0 %copy-start.15 = (f32[512,768]{1,0:T(8,128)S(1)}, f32[512,768]{1,0:T(8,128)}, u32[]{:S(2)}) copy-start(f32[512,768]{1,0:T(8,128)} %get-tuple-element.232) | copy-start | bytes 4718596
  (57 other events, 218.0 us)
Sparse Core Ops, SparseCore 0:
  9.6 31.2 all-gather.11
  138.6 58.3 reduce-scatter.4
  202.1 28.5 all-gather.5
  249.3 37.9 reduce-scatter.6
  293.1 28.5 all-gather.7
  340.7 37.9 reduce-scatter.8
  384.0 28.5 all-gather.9
  598.8 38.5 reduce-scatter.10
  643.0 300.3 all-reduce.3
where the time goes:
time: 971 us; the launch traced here: 960 us
  waiting for transfers between devices  520 us (54%)
  matrix products  210 us (22%)
  other arithmetic  86.9 us (9%)
  local copies, waits for them, and re-layouts  76.5 us (8%)
  blocking collectives  40.7 us (4%)
  between operations  15.4 us (2%)
  loops' own time  10.8 us (1%)
    psum x1, waiting for transfers between devices, local(): lax.psum((grad_joint, grad_output, grad_mixed, grad_down), 'dp')  279 us
    reduce_scatter x1, waiting for transfers between devices, local(): lax.psum_scatter(jnp.dot(context, output_weight, preferred_element_type=j...  58.5 us
    psum x1, blocking collectives, local(): lax.psum((grad_attn_gain, grad_attn_shift, grad_mlp_gain, grad_mlp_shift)...  40.7 us
    reduce_scatter x1, waiting for transfers between devices, local(): lax.psum_scatter(contract_cols(grad_mixed_low, mixed_weight).astype(jnp.b...  38.1 us
    reduce_scatter x1, waiting for transfers between devices, local(): lax.psum_scatter(jnp.dot(hidden, down_weight, preferred_element_type=jnp....  38.1 us
    dynamic_update_slice x8, local copies, waits for them, and re-layouts, local(): lax.scan(attend_back, (zero_grad, zero_grad), (query_blocks, segment_bloc...  36.1 us
    dot_general x8, matrix products, block_scores(): jnp.einsum('qhd,khd->hqk', query_part, key_rows, preferred_element_type=j...  35.9 us
    dot_general x4, matrix products, attend(): jnp.einsum('hqk,khd->qhd', soft_weights, value_rows, preferred_element_ty...  29.3 us
  transfers between devices with their start and end apart: 9, of which 8 were waited for; matrix products, arithmetic and copies ran while one was open for 4% of the time, Pallas kernels for 0%

commit v1 on v0

v1 whole, which is shorter than its diff:
```python
import functools
import math

import jax
import jax.numpy as jnp
from jax import lax
from jax.experimental import pallas as pl
from jax.experimental.pallas import tpu as pltpu
from jax.sharding import PartitionSpec as P

HEAD_DIM = 64
EPSILON = 1e-05
ROPE_BASE = 1000.0
APART = -(2.0**30)
WIDE = 128
SEG_AT = HEAD_DIM
ROW_AT = HEAD_DIM + 8
VMEM = 48 * 2**20
bf16 = jnp.bfloat16
f32 = jnp.float32
NT = (((1,), (1,)), ((), ()))
TN = (((0,), (0,)), ((), ()))


def dot(a, b):
    return jnp.dot(a, b, preferred_element_type=f32)


def dot_nt(a, b):
    return lax.dot_general(a, b, NT, preferred_element_type=f32)


def dot_tn(a, b):
    return lax.dot_general(a, b, TN, preferred_element_type=f32)


def swap(value, axis, bit):
    size = lax.axis_size(axis)
    return lax.ppermute(value, axis, [(i, i ^ bit) for i in range(size)])


def gather_rows(block, axis):
    size = lax.axis_size(axis)
    held = {0: block}
    step = size // 2
    while step:
        keys = sorted(held)
        sent = held[keys[0]] if len(keys) == 1 else jnp.concatenate([held[k] for k in keys], axis=0)
        got = swap(sent, axis, step)
        rows = block.shape[0]
        for n, k in enumerate(keys):
            held[k ^ step] = got[n * rows : (n + 1) * rows]
        step //= 2
    return jnp.concatenate([held[k] for k in range(size)], axis=0)


def scatter_sum(blocks, axis):
    step = lax.axis_size(axis) // 2
    while step:
        got = swap(jnp.concatenate([b.astype(bf16) for b in blocks[step:]], axis=0), axis, step)
        rows = blocks[0].shape[0]
        blocks = [
            blocks[n].astype(f32) + got[n * rows : (n + 1) * rows].astype(f32) for n in range(step)
        ]
        step //= 2
    return blocks[0]


def exchange(blocks, axis):
    return [b if j == 0 else swap(b, axis, j) for j, b in enumerate(blocks)]


def sum_over(value, axis, order):
    me = lax.axis_index(axis)
    for bit in order:
        half = value.shape[0] // 2
        side = (me >> bit) & 1
        mine = lax.dynamic_slice_in_dim(value, side * half, half, 0)
        other = lax.dynamic_slice_in_dim(value, (1 - side) * half, half, 0)
        value = (mine.astype(f32) + swap(other, axis, 1 << bit).astype(f32)).astype(value.dtype)
    for bit in reversed(order):
        side = (me >> bit) & 1
        got = swap(value, axis, 1 << bit)
        value = jnp.where(
            side == 0, jnp.concatenate([value, got], 0), jnp.concatenate([got, value], 0)
        )
    return value


def small_sum(value, axis):
    step = lax.axis_size(axis) // 2
    while step:
        value = value + swap(value, axis, step)
        step //= 2
    return value


def project_kernel(heads, x_ref, w_ref, cos_ref, sin_ref, qf_ref, kf_ref, qa_ref, ka_ref, va_ref):
    proj = dot(x_ref[...], w_ref[...])
    cosine, sine = cos_ref[...], sin_ref[...]
    lane = lax.broadcasted_iota(jnp.int32, (proj.shape[0], WIDE), 1)
    first = lane < HEAD_DIM
    qf, kf = qf_ref[...], kf_ref[...]
    ones = jnp.where((lane >= HEAD_DIM) & (lane < HEAD_DIM + 3), 1.0, 0.0)
    for h in range(heads):
        at = [(part * heads + h) * WIDE for part in range(3)]
        q = proj[:, at[0] : at[0] + WIDE]
        k = proj[:, at[1] : at[1] + WIDE]
        v = proj[:, at[2] : at[2] + WIDE]
        q = q * cosine + pltpu.roll(q, HEAD_DIM, 1) * sine
        k = k * cosine + pltpu.roll(k, HEAD_DIM, 1) * sine
        qa_ref[h] = jnp.where(first, q * (1.0 / math.sqrt(HEAD_DIM)), qf).astype(bf16)
        ka_ref[h] = jnp.where(first, k, kf).astype(bf16)
        va_ref[h] = jnp.where(first, v, ones).astype(bf16)


def project(x, w, cosine, sine, qf, kf, heads, block=512):
    length, width = x.shape
    wide = jax.ShapeDtypeStruct((heads, length, WIDE), bf16)
    rows = lambda n: pl.BlockSpec((block, n), lambda i: (i, 0))
    out = pl.BlockSpec((heads, block, WIDE), lambda i: (0, i, 0))
    return pl.pallas_call(
        functools.partial(project_kernel, heads),
        grid=(length // block,),
        in_specs=[rows(width), pl.BlockSpec(w.shape, lambda i: (0, 0))] + [rows(WIDE)] * 4,
        out_specs=[out] * 3,
        out_shape=[wide] * 3,
        compiler_params=pltpu.CompilerParams(vmem_limit_bytes=VMEM),
        cost_estimate=pl.CostEstimate(
            flops=2 * length * width * w.shape[1], bytes_accessed=8 * 2**20, transcendentals=0
        ),
        name="project",
    )(x, w, cosine, sine, qf, kf)


def split3(value):
    high = value.astype(bf16).astype(f32)
    rest = value - high
    middle = rest.astype(bf16).astype(f32)
    return high, middle, rest - middle


def put_row(wide, at, value):
    lane = lax.broadcasted_iota(jnp.int32, wide.shape, 1)
    for n, part in enumerate(split3(value)):
        wide = jnp.where(lane == at + n, -part, wide)
    return wide


def attend_kernel(heads, qa_ref, ka_ref, va_ref, ctx_ref, qb_ref):
    parts = []
    for h in range(heads):
        qa = qa_ref[h]
        scores = dot_nt(qa, ka_ref[h])
        peak = jnp.max(scores, axis=1, keepdims=True)
        weights = jnp.exp(scores - peak).astype(bf16)
        summed = dot(weights, va_ref[h])
        total = summed[:, HEAD_DIM : HEAD_DIM + 1]
        parts.append(summed[:, :HEAD_DIM] / total)
        qb_ref[h] = put_row(qa.astype(f32), ROW_AT, peak + jnp.log(total)).astype(bf16)
    ctx_ref[...] = jnp.concatenate(parts, axis=1).astype(bf16)


def attend(qa, ka, va, block=256):
    heads, length, _ = qa.shape
    whole = pl.BlockSpec((heads, length, WIDE), lambda i: (0, 0, 0))
    part = pl.BlockSpec((heads, block, WIDE), lambda i: (0, i, 0))
    return pl.pallas_call(
        functools.partial(attend_kernel, heads),
        grid=(length // block,),
        in_specs=[part, whole, whole],
        out_specs=[pl.BlockSpec((block, heads * HEAD_DIM), lambda i: (i, 0)), part],
        out_shape=[
            jax.ShapeDtypeStruct((length, heads * HEAD_DIM), bf16),
            jax.ShapeDtypeStruct((heads, length, WIDE), bf16),
        ],
        compiler_params=pltpu.CompilerParams(vmem_limit_bytes=VMEM),
        cost_estimate=pl.CostEstimate(
            flops=4 * heads * length * length * 256,
            bytes_accessed=8 * 2**20,
            transcendentals=heads * length * length,
        ),
        name="attend",
    )(qa, ka, va)


def swap_halves(value, lane):
    half = HEAD_DIM // 2
    return jnp.where(
        lane < half, pltpu.roll(value, WIDE - half, 1), pltpu.roll(value, half, 1)
    )


def attend_back_kernel(
    head, block, qb_ref, ka_ref, va_ref, go_ref, ctx_ref, cos_ref, sin_ref, dq_ref, dkv_ref, doa, dqt
):
    j = pl.program_id(0)
    length = qb_ref.shape[1]
    cols = pl.ds(head * HEAD_DIM, HEAD_DIM)

    @pl.when(j == 0)
    def _():
        dqt[...] = jnp.zeros_like(dqt)
        for i in range(length // block):
            at = pl.ds(i * block, block)
            go = go_ref[at, cols].astype(f32)
            delta = jnp.sum(go * ctx_ref[at, cols].astype(f32), axis=1, keepdims=True)
            wide = jnp.concatenate([go, jnp.zeros_like(go)], axis=1)
            doa[at, :] = put_row(wide, HEAD_DIM, delta).astype(bf16)

    ka, va = ka_ref[0], va_ref[0]
    kt = ka.astype(f32).T[:HEAD_DIM].astype(bf16)
    dk = dv = None
    for i in range(length // block):
        at = pl.ds(i * block, block)
        qb, do = qb_ref[0, at, :], doa[at, :]
        weights = jnp.exp(dot_nt(ka, qb))
        grads = (weights * dot_nt(va, do)).astype(bf16)
        v_part = dot(weights.astype(bf16), do)
        k_part = dot(grads, qb)
        dk = k_part if i == 0 else dk + k_part
        dv = v_part if i == 0 else dv + v_part
        dqt[:, at] += dot(kt, grads)
    lane = lax.broadcasted_iota(jnp.int32, dk.shape, 1)
    rows = pl.ds(pl.multiple_of(j * ka.shape[0], ka.shape[0]), ka.shape[0])
    dk = dk * cos_ref[rows, :] - swap_halves(dk, lane) * sin_ref[rows, :]
    dkv_ref[...] = jnp.where(
        lane < HEAD_DIM, dk, pltpu.roll(jnp.where(lane < HEAD_DIM, dv, 0.0), HEAD_DIM, 1)
    ).astype(bf16)

    @pl.when(j == pl.num_programs(0) - 1)
    def _():
        for i in range(length // block):
            at = pl.ds(i * block, block)
            part = dqt[:, at]
            dq = jnp.concatenate([part, jnp.zeros_like(part)], axis=0).T
            lanes = lax.broadcasted_iota(jnp.int32, dq.shape, 1)
            dq = dq * cos_ref[at, :] - swap_halves(dq, lanes) * sin_ref[at, :]
            dq_ref[at, :] = (dq[:, :HEAD_DIM] * (1.0 / math.sqrt(HEAD_DIM))).astype(bf16)


def attend_back(head, qb, ka, va, go, ctx, cosine, sine, block_k=512, block_q=512):
    _, length, _ = qb.shape
    at_head = pl.BlockSpec((1, length, WIDE), lambda j: (head, 0, 0))
    part = pl.BlockSpec((1, block_k, WIDE), lambda j: (head, j, 0))
    full = lambda a: pl.BlockSpec(a.shape, lambda j: (0, 0))
    return pl.pallas_call(
        functools.partial(attend_back_kernel, head, block_q),
        grid=(length // block_k,),
        in_specs=[at_head, part, part, full(go), full(ctx), full(cosine), full(sine)],
        out_specs=[
            pl.BlockSpec((length, HEAD_DIM), lambda j: (0, 0)),
            pl.BlockSpec((block_k, WIDE), lambda j: (j, 0)),
        ],
        out_shape=[
            jax.ShapeDtypeStruct((length, HEAD_DIM), bf16),
            jax.ShapeDtypeStruct((length, WIDE), bf16),
        ],
        scratch_shapes=[pltpu.VMEM((length, WIDE), bf16), pltpu.VMEM((HEAD_DIM, length), f32)],
        compiler_params=pltpu.CompilerParams(vmem_limit_bytes=VMEM),
        cost_estimate=pl.CostEstimate(
            flops=10 * length * length * 256,
            bytes_accessed=4 * 2**20,
            transcendentals=length * length,
        ),
        name="attend_back",
    )(qb, ka, va, go, ctx, cosine, sine)


def positions(segments):
    places = jnp.arange(segments.shape[0], dtype=jnp.int32)
    before = jnp.concatenate([segments[:1] - 1, segments[:-1]])
    starts = lax.cummax(jnp.where(segments != before, places, 0), axis=0)
    return (places - starts).astype(f32)


def norm_parts(row_values):
    centred = row_values - jnp.mean(row_values, axis=-1, keepdims=True)
    inverse = lax.rsqrt(jnp.mean(centred * centred, axis=-1, keepdims=True) + EPSILON)
    return (centred * inverse, inverse)


def norm_back(grad_norm, normalized, inverse):
    return inverse * (
        grad_norm
        - jnp.mean(grad_norm, axis=-1, keepdims=True)
        - normalized * jnp.mean(grad_norm * normalized, axis=-1, keepdims=True)
    )


def relative_rows(value, blocks):
    me = lax.axis_index("tensor")
    rows = value.shape[0] // blocks
    return jnp.concatenate(
        [lax.dynamic_slice_in_dim(value, (me ^ j) * rows, rows, 0) for j in range(blocks)], axis=0
    )


def wide_weight(query_weight, key_weight, value_weight, heads):
    width = query_weight.shape[0]
    half = HEAD_DIM // 2

    def turned(weight):
        w = weight.reshape(width, heads, HEAD_DIM)
        swapped = jnp.concatenate([w[..., half:], w[..., :half]], axis=-1)
        return jnp.concatenate([w, swapped], axis=-1).reshape(width, heads * WIDE)

    v = value_weight.reshape(width, heads, HEAD_DIM)
    v = jnp.concatenate([v, jnp.zeros_like(v)], axis=-1).reshape(width, heads * WIDE)
    return jnp.concatenate([turned(query_weight), turned(key_weight), v], axis=1)


def local(
    tokens,
    segment_ids,
    query_weight,
    key_weight,
    value_weight,
    output_weight,
    attn_gain,
    attn_shift,
    gate_weight,
    up_weight,
    down_weight,
    mlp_gain,
    mlp_shift,
    cotangent,
):
    own = tokens[0]
    segments = segment_ids[0]
    head_width = query_weight.shape[1]
    heads = head_width // HEAD_DIM
    ff_local = gate_weight.shape[1]
    group = lax.axis_size("tensor")
    block = own.shape[0]
    bits = list(range(int(math.log2(lax.axis_size("dp")))))
    orders = [bits, bits[1:] + bits[:1]]

    x_full = gather_rows(own, "tensor")
    out_full = gather_rows(output_weight, "tensor")

    angle_rate = ROPE_BASE ** (-(jnp.arange(HEAD_DIM // 2, dtype=f32) * 2.0 / HEAD_DIM))
    angles = positions(segments)[:, None] * angle_rate[None, :]
    cosine, sine = jnp.cos(angles), jnp.sin(angles)
    blank = jnp.zeros((segments.shape[0], HEAD_DIM), f32)
    one_hot = (segments[:, None] + 1 == jnp.arange(8)[None, :]).astype(f32)
    table = jnp.concatenate(
        [cosine, cosine, blank, -sine, sine, blank]
        + [blank, APART * one_hot, blank[:, :56], blank, 1.0 - one_hot, blank[:, :3] + 1.0, blank[:, :53]],
        axis=1,
    )
    table = relative_rows(table, group)
    cos_wide, sin_wide, qf, kf = (table[:, n * WIDE : (n + 1) * WIDE] for n in range(4))

    joint_wide = wide_weight(query_weight, key_weight, value_weight, heads)
    qa, ka, va = project(x_full, joint_wide, cos_wide, sin_wide, qf, kf, heads)
    ctx, qb = attend(qa, ka, va)
    ctx_parts = exchange([ctx[j * block : (j + 1) * block] for j in range(group)], "tensor")
    ctx_own = jnp.concatenate(ctx_parts, axis=1)

    first_norm, first_inverse = norm_parts(own.astype(f32) + dot(ctx_own, out_full))
    normed = first_norm * attn_gain + attn_shift
    normed_full = gather_rows(normed.astype(bf16), "tensor")
    gate_pre = dot(normed_full, gate_weight)
    up_pre = dot(normed_full, up_weight)
    gate_sigmoid = jax.nn.sigmoid(gate_pre)
    activated = gate_pre * gate_sigmoid
    hidden = (activated * up_pre).astype(bf16)
    mlp = dot(hidden, down_weight)
    mlp_rows = scatter_sum([mlp[j * block : (j + 1) * block] for j in range(group)], "tensor")
    second_norm, second_inverse = norm_parts(normed + mlp_rows)
    encoded = (second_norm * mlp_gain + mlp_shift).astype(bf16)
    grad_encoded = cotangent[0].astype(f32)
    grad_second = norm_back(grad_encoded * mlp_gain, second_norm, second_inverse)
    grad_mlp_full = gather_rows(grad_second.astype(bf16), "tensor")

    grad_down = dot_tn(hidden, grad_mlp_full).astype(bf16)
    grad_down = sum_over(grad_down, "dp", orders[0])
    grad_hidden = dot_nt(grad_mlp_full, down_weight)
    grad_gate_low = (
        grad_hidden * up_pre * gate_sigmoid * (1.0 + gate_pre * (1.0 - gate_sigmoid))
    ).astype(bf16)
    grad_up_low = (grad_hidden * activated).astype(bf16)
    back = dot_nt(grad_gate_low, gate_weight) + dot_nt(grad_up_low, up_weight)
    grad_normed = grad_second + scatter_sum(
        [back[j * block : (j + 1) * block] for j in range(group)], "tensor"
    )
    grad_gate = sum_over(dot_tn(normed_full, grad_gate_low).astype(bf16), "dp", orders[1])
    grad_up = sum_over(dot_tn(normed_full, grad_up_low).astype(bf16), "dp", orders[0])

    grad_first = norm_back(grad_normed * attn_gain, first_norm, first_inverse)
    grad_attn_low = grad_first.astype(bf16)
    small = jnp.stack(
        [
            jnp.sum(grad_normed * first_norm, axis=0),
            jnp.sum(grad_normed, axis=0),
            jnp.sum(grad_encoded * second_norm, axis=0),
            jnp.sum(grad_encoded, axis=0),
        ]
    )
    small = small_sum(small_sum(small, "tensor"), "dp")

    grad_ctx_own = dot_nt(grad_attn_low, out_full).astype(bf16)
    grad_ctx = jnp.concatenate(
        exchange([grad_ctx_own[:, j * head_width : (j + 1) * head_width] for j in range(group)], "tensor"),
        axis=0,
    )
    grad_out = dot_tn(ctx_own, grad_attn_low)
    grad_out = scatter_sum(
        [grad_out[j * head_width : (j + 1) * head_width] for j in range(group)], "tensor"
    ).astype(bf16)
    grad_out = sum_over(grad_out, "dp", orders[0])

    grad_heads, parts = [], []
    for h in range(heads):
        dq, dkv = attend_back(h, qb, ka, va, grad_ctx, ctx, cos_wide, sin_wide)
        part = jnp.concatenate([dq, dkv], axis=1)
        parts.append(part)
        grad_heads.append(sum_over(dot_tn(x_full, part).astype(bf16), "dp", orders[h % 2]))
    columns = [
        jnp.concatenate([p[:, n * HEAD_DIM : (n + 1) * HEAD_DIM] for p in parts], axis=1)
        for n in range(3)
    ]
    back = (
        dot_nt(columns[0], query_weight)
        + dot_nt(columns[1], key_weight)
        + dot_nt(columns[2], value_weight)
    )
    grad_tokens = grad_first + scatter_sum(
        [back[j * block : (j + 1) * block] for j in range(group)], "tensor"
    )
    grad_joint = [
        jnp.concatenate([g[:, n * HEAD_DIM : (n + 1) * HEAD_DIM] for g in grad_heads], axis=1).astype(f32)
        for n in range(3)
    ]
    return (
        encoded[None],
        grad_tokens[None],
        *grad_joint,
        grad_out.astype(f32),
        small[0],
        small[1],
        grad_gate.astype(f32),
        grad_up.astype(f32),
        grad_down.astype(f32),
        small[2],
        small[3],
    )


def solution(mesh):
    rows, cols, lead = P("dp", "tensor", None), P(None, "tensor"), P("tensor", None)
    return jax.shard_map(
        local,
        mesh=mesh,
        in_specs=(
            rows, P("dp", None), cols, cols, cols, lead, P(), P(), cols, cols, lead, P(), P(), rows,
        ),
        out_specs=(
            rows, rows, cols, cols, cols, lead, P(), P(), cols, cols, lead, P(), P(),
        ),
        check_vma=False,
    )
```

time: 971 us -> 507 us (0.52)
  waiting for transfers between devices: 520 us -> 217 us
  matrix products: 210 us -> 54.8 us
  Pallas kernels: 0 us -> 73.2 us
  starting transfers between devices: 0.63 us -> 55.6 us
  local copies, waits for them, and re-layouts: 76.5 us -> 34.2 us
  blocking collectives: 40.7 us -> 0 us
  other arithmetic: 86.9 us -> 59.5 us
  between operations: 15.4 us -> 3.56 us
  loops' own time: 10.8 us -> 0 us
    psum x1 -> x0, waiting for transfers between devices: 279 us -> none  [local(): lax.psum((grad_joint, grad_output, grad_mixed, grad_down), 'dp')]
    ppermute x0 -> x69, waiting for transfers between devices: none -> 217 us  [swap(): return lax.ppermute(value, axis, [(i, i ^ bit) for i in range(size)])]
    dot_general x40 -> x18, matrix products: 210 us -> 54.8 us  [the longest x7 23.1 us: dot_nt(): return lax.dot_general(a, b, NT, preferred_element_type=f32)]
    reduce_scatter x4 -> x0, waiting for transfers between devices: 135 us -> none  [the longest x1 58.5 us: local(): lax.psum_scatter(jnp.dot(context, output_weight, preferred_element_type=j...]
    all_gather x4 -> x0, waiting for transfers between devices: 105 us -> none  [the longest x1 28.6 us: local(): lax.all_gather(grad_second.astype(jnp.bfloat16), 'tensor', axis=0, tiled=...]
    pallas_call x0 -> x5, Pallas kernels: none -> 73.2 us  [the longest x3 43.5 us: attend_back(): pl.pallas_call(functools.partial(attend_back_kernel, head, block_q), grid...]
    ppermute x0 -> x69, starting transfers between devices: none -> 55.6 us  [swap(): return lax.ppermute(value, axis, [(i, i ^ bit) for i in range(size)])]
    psum x1 -> x0, blocking collectives: 40.7 us -> none  [local(): lax.psum((grad_attn_gain, grad_attn_shift, grad_mlp_gain, grad_mlp_shift)...]
  transfers between devices with their start and end apart: 9 -> 69, of which waited for: 8 -> 44; matrix products, arithmetic and copies ran while one was open for 4% -> 22% of each run, Pallas kernels for 0% -> 15%
where the time goes in v1:
time: 507 us; the launch traced here: 498 us
  waiting for transfers between devices  217 us (43%)
  Pallas kernels  73.2 us (14%)
  other arithmetic  59.5 us (12%)
  starting transfers between devices  55.6 us (11%)
  matrix products  54.8 us (11%)
  local copies, waits for them, and re-layouts  34.2 us (7%)
    ppermute x69, waiting for transfers between devices, swap(): return lax.ppermute(value, axis, [(i, i ^ bit) for i in range(size)])  217 us
    ppermute x69, starting transfers between devices, swap(): return lax.ppermute(value, axis, [(i, i ^ bit) for i in range(size)])  55.6 us
    pallas_call x3, Pallas kernels, attend_back(): pl.pallas_call(functools.partial(attend_back_kernel, head, block_q), grid...  43.5 us
    dot_general x7, matrix products, dot_nt(): return lax.dot_general(a, b, NT, preferred_element_type=f32)  23.1 us
    pallas_call x1, Pallas kernels, attend(): pl.pallas_call(functools.partial(attend_kernel, heads), grid=(length // b...  22 us
    dot_general x4, matrix products, dot(): return jnp.dot(a, b, preferred_element_type=f32)  16.6 us
    dot_general x7, matrix products, dot_tn(): return lax.dot_general(a, b, TN, preferred_element_type=f32)  15.1 us
  transfers between devices with their start and end apart: 69, of which 44 were waited for; matrix products, arithmetic and copies ran while one was open for 22% of the time, Pallas kernels for 15%

profile of v1, /device:TPU:0, one launch (start us, length us, event | category | flops | bytes accessed | tf_op | source)
XLA Modules:
  0.0 497.8 jit_solution(1953235041325250123)
XLA Ops:
  10.4 5.5 %multiply_sine_fusion = (f32[2048,32]{1,0:T(8,128)}, f32[2048,32]{1,0:T(8,128)}, f32[2048,32]{1,0:T(8,128)S(1)}) fusion(f32[2048]{0:T(1024)S(1)} %fusion.59, f32[32]{0:T(128)S(1)} %negate_power_fusion), kind=kLoop, calls=%fused_computation.56 | loop fusion | flops 131072 | bytes 794752 | tf_op jit(solution)/shard_map/sin | solution.py:344
  15.9 6.4 %collective-permute-done = bf16[512,768]{1,0:T(8,128)(2,1)} collective-permute-done((bf16[512,768]{1,0:T(8,128)(2,1)}, bf16[512,768]{1,0:T(8,128)(2,1)}, u32[]{:S(2)}, u32[]{:S(2)}) %collective-permute-start) | collective-permute-done | bytes 786464 | tf_op jit(solution)/shard_map/ppermute | solution.py:39
  33.4 8.9 %concatenate.230 = f32[2048,512]{1,0:T(8,128)} concatenate(f32[2048,32]{1,0:T(8,128)S(1)} %get-tuple-element.97, f32[2048,32]{1,0:T(8,128)S(1)} %get-tuple-element.97, f32[2048,64]{1,0:T(8,128)S(1)} %broadcast_in_dim.11, f32[2048,32]{1,0:T(8,128)} %get-tuple-element.96, f32[2048,32]{1,0:T(8,128)} %get-tuple-element.95, f32[2048,128]{1,0:T(8,128)} %concatenate.229, ...), dimensions={1} | concatenate | bytes 8388608 | tf_op jit(solution)/shard_map/concatenate | solution.py:347
  51.3 7.4 %pad_maximum_fusion.1.x_ref = bf16[2048,768]{1,0:T(8,128)(2,1)} fusion(bf16[512,768]{1,0:T(8,128)(2,1)S(1)} %get-tuple-element.65, bf16[512,768]{1,0:T(8,128)(2,1)} %collective-permute-done, bf16[512,768]{1,0:T(8,128)(2,1)S(1)} %get-tuple-element.64, bf16[512,768]{1,0:T(8,128)(2,1)S(1)} %bitcast.72), kind=kLoop, calls=%fused_computation.11 | loop fusion | flops 12582912 | bytes 6291456 | tf_op jit(solution)/shard_map/concatenate | solution.py:54
  58.7 7.8 %project.1 = (bf16[3,2048,128]{2,1,0:T(8,128)(2,1)S(1)}, bf16[3,2048,128]{2,1,0:T(8,128)(2,1)}, bf16[3,2048,128]{2,1,0:T(8,128)(2,1)}) custom-call(bf16[2048,768]{1,0:T(8,128)(2,1)} %pad_maximum_fusion.1.x_ref, bf16[768,1152]{1,0:T(8,128)(2,1)} %pad_maximum_fusion.4.w_ref, f32[2048,128]{1,0:T(8,128)S(1)} %get-tuple-element.54.cos_ref, ...), custom_call_target="tpu_custom_call" | custom-call | flops 3623878656 | bytes 8388608 | tf_op jit(solution)/shard_map/project/pallas_call | solution.py:122
  67.8 22.0 %attend.1 = (bf16[2048,192]{1,0:T(8,128)(2,1)S(1)}, bf16[3,2048,128]{2,1,0:T(8,128)(2,1)S(1)}) custom-call(bf16[3,2048,128]{2,1,0:T(8,128)(2,1)S(1)} %get-tuple-element.24.qa_ref, bf16[3,2048,128]{2,1,0:T(8,128)(2,1)S(1)} %copy-done.4, bf16[3,2048,128]{2,1,0:T(8,128)(2,1)} %get-tuple-element.26.va_ref), custom_call_target="tpu_custom_call" | custom-call | flops 12884901888 | bytes 8388608 | tf_op jit(solution)/shard_map/attend/pallas_call | solution.py:168
  92.3 7.0 %collective-permute-done.3 = bf16[512,192]{1,0:T(8,128)(2,1)S(1)} collective-permute-done((bf16[512,192]{1,0:T(8,128)(2,1)S(1)}, bf16[512,192]{1,0:T(8,128)(2,1)S(1)}, u32[]{:S(2)}, u32[]{:S(2)}) %collective-permute-start.3) | collective-permute-done | bytes 196640 | tf_op jit(solution)/shard_map/ppermute | solution.py:39
  99.3 5.1 %collective-permute-done.4 = bf16[512,192]{1,0:T(8,128)(2,1)S(1)} collective-permute-done((bf16[512,192]{1,0:T(8,128)(2,1)S(1)}, bf16[512,192]{1,0:T(8,128)(2,1)S(1)}, u32[]{:S(2)}, u32[]{:S(2)}) %collective-permute-start.4) | collective-permute-done | bytes 196640 | tf_op jit(solution)/shard_map/ppermute | solution.py:39
  109.2 18.0 %collective-permute-done.7 = bf16[512,768]{1,0:T(8,128)(2,1)S(1)} collective-permute-done((bf16[512,768]{1,0:T(8,128)(2,1)S(1)}, bf16[512,768]{1,0:T(8,128)(2,1)S(1)}, u32[]{:S(2)}, u32[]{:S(2)}) %collective-permute-start.7) | collective-permute-done | bytes 786464 | tf_op jit(solution)/shard_map/ppermute | solution.py:39
  133.6 9.4 %multiply_convert_fusion.2 = (bf16[2048,768]{1,0:T(8,128)(2,1)S(1)}, f32[2048,768]{1,0:T(8,128)}) fusion(f32[2048,768]{1,0:T(8,128)S(1)} %fusion.74, bf16[768,768]{1,0:T(8,128)(2,1)S(1)} %copy-done.64, bf16[512,768]{1,0:T(8,128)(2,1)S(1)} %get-tuple-element.63, bf16[512,768]{1,0:T(8,128)(2,1)S(1)} %collective-permute-done.7, ...), kind=kOutput, calls=%fused_computation.3 | convolution fusion | flops 2437939200 | bytes 20054016 | tf_op jit(solution)/shard_map/dot_general | solution.py:26
  147.6 34.7 %collective-permute-done.9 = bf16[1024,768]{1,0:T(8,128)(2,1)S(1)} collective-permute-done((bf16[1024,768]{1,0:T(8,128)(2,1)S(1)}, bf16[1024,768]{1,0:T(8,128)(2,1)S(1)}, u32[]{:S(2)}, u32[]{:S(2)}) %collective-permute-start.9) | collective-permute-done | bytes 1572896 | tf_op jit(solution)/shard_map/ppermute | solution.py:39
  190.9 17.9 %collective-permute-done.11 = bf16[512,768]{1,0:T(8,128)(2,1)S(1)} collective-permute-done((bf16[512,768]{1,0:T(8,128)(2,1)S(1)}, bf16[512,768]{1,0:T(8,128)(2,1)S(1)}, u32[]{:S(2)}, u32[]{:S(2)}) %collective-permute-start.11) | collective-permute-done | bytes 786464 | tf_op jit(solution)/shard_map/ppermute | solution.py:39
  221.9 12.0 %multiply_convert_fusion = (bf16[2048,768]{1,0:T(8,128)(2,1)S(1)}, bf16[2048,768]{1,0:T(8,128)(2,1)}) fusion(f32[2048,768]{1,0:T(8,128)} %copy-done.70, f32[2048,768]{1,0:T(8,128)} %get-tuple-element.103, bf16[768,768]{1,0:T(8,128)(2,1)S(1)} %copy-done, bf16[512,768]{1,0:T(8,128)(2,1)S(1)} %get-tuple-element.61, bf16[512,768]{1,0:T(8,128)(2,1)S(1)} %copy-done.36, ...), kind=kOutput, calls=%fused_computation.1 | convolution fusion | flops 2448949248 | bytes 23199744 | tf_op jit(solution)/shard_map/dot_general | solution.py:30
  253.8 5.3 %collective-permute-done.51 = bf16[384,768]{1,0:T(8,128)(2,1)S(1)} collective-permute-done((bf16[384,768]{1,0:T(8,128)(2,1)S(1)}, bf16[384,768]{1,0:T(8,128)(2,1)S(1)}, u32[]{:S(2)}, u32[]{:S(2)}) %collective-permute-start.51) | collective-permute-done | bytes 589856 | tf_op jit(solution)/shard_map/ppermute | solution.py:39
  262.1 9.7 %collective-permute-done.64 = bf16[192,768]{1,0:T(8,128)(2,1)S(1)} collective-permute-done((bf16[192,768]{1,0:T(8,128)(2,1)S(1)}, bf16[192,768]{1,0:T(8,128)(2,1)S(1)}, u32[]{:S(2)}, u32[]{:S(2)}) %collective-permute-start.64) | collective-permute-done | bytes 294944 | tf_op jit(solution)/shard_map/ppermute | solution.py:39
  280.4 8.2 %collective-permute-done.65 = bf16[96,768]{1,0:T(8,128)(2,1)S(1)} collective-permute-done((bf16[96,768]{1,0:T(8,128)(2,1)S(1)}, bf16[96,768]{1,0:T(8,128)(2,1)S(1)}, u32[]{:S(2)}, u32[]{:S(2)}) %collective-permute-start.65) | collective-permute-done | bytes 147488 | tf_op jit(solution)/shard_map/ppermute | solution.py:39
  288.7 6.2 %collective-permute-done.59 = bf16[96,768]{1,0:T(8,128)(2,1)S(1)} collective-permute-done((bf16[96,768]{1,0:T(8,128)(2,1)S(1)}, bf16[96,768]{1,0:T(8,128)(2,1)S(1)}, u32[]{:S(2)}, u32[]{:S(2)}) %collective-permute-start.59) | collective-permute-done | bytes 147488 | tf_op jit(solution)/shard_map/ppermute | solution.py:39
  295.1 6.2 %collective-permute-done.66 = bf16[96,768]{1,0:T(8,128)(2,1)S(1)} collective-permute-done((bf16[96,768]{1,0:T(8,128)(2,1)S(1)}, bf16[96,768]{1,0:T(8,128)(2,1)S(1)}, u32[]{:S(2)}, u32[]{:S(2)}) %collective-permute-start.66) | collective-permute-done | bytes 147488 | tf_op jit(solution)/shard_map/ppermute | solution.py:39
  310.3 7.2 %collective-permute-done.67 = bf16[192,768]{1,0:T(8,128)(2,1)} collective-permute-done((bf16[192,768]{1,0:T(8,128)(2,1)S(1)}, bf16[192,768]{1,0:T(8,128)(2,1)}, u32[]{:S(2)}, u32[]{:S(2)}) %collective-permute-start.67) | collective-permute-done | bytes 294944 | tf_op jit(solution)/shard_map/ppermute | solution.py:39
  335.8 6.5 %collective-permute-done.62 = bf16[384,768]{1,0:T(8,128)(2,1)} collective-permute-done((bf16[384,768]{1,0:T(8,128)(2,1)}, bf16[384,768]{1,0:T(8,128)(2,1)}, u32[]{:S(2)}, u32[]{:S(2)}) %collective-permute-start.62) | collective-permute-done | bytes 589856 | tf_op jit(solution)/shard_map/ppermute | solution.py:39
  372.2 4.7 collective-permute-done.17
  377.1 14.2 %attend_back.3 = (bf16[2048,64]{1,0:T(8,128)(2,1)S(1)}, bf16[2048,128]{1,0:T(8,128)(2,1)S(1)}) custom-call(bf16[3,2048,128]{2,1,0:T(8,128)(2,1)} %copy-done.5, bf16[3,2048,128]{2,1,0:T(8,128)(2,1)} %get-tuple-element.25.ka_ref, bf16[3,2048,128]{2,1,0:T(8,128)(2,1)} %get-tuple-element.26.va_ref, bf16[2048,192]{1,0:T(8,128)(2,1)S(1)} %pad_maximum_fusion.12.go_ref, ...), custom_call_target="tpu_custom_call" | custom-call | flops 10737418240 | bytes 4194304 | tf_op jit(solution)/shard_map/attend_back/pallas_call | solution.py:247
  391.3 14.8 %attend_back.4 = (bf16[2048,64]{1,0:T(8,128)(2,1)S(1)}, bf16[2048,128]{1,0:T(8,128)(2,1)S(1)}) custom-call(bf16[3,2048,128]{2,1,0:T(8,128)(2,1)} %copy-done.5, bf16[3,2048,128]{2,1,0:T(8,128)(2,1)} %get-tuple-element.25.ka_ref, bf16[3,2048,128]{2,1,0:T(8,128)(2,1)} %get-tuple-element.26.va_ref, bf16[2048,192]{1,0:T(8,128)(2,1)S(1)} %pad_maximum_fusion.12.go_ref, ...), custom_call_target="tpu_custom_call" | custom-call | flops 10737418240 | bytes 4194304 | tf_op jit(solution)/shard_map/attend_back/pallas_call | solution.py:247
  406.1 14.5 %attend_back.5 = (bf16[2048,64]{1,0:T(8,128)(2,1)S(1)}, bf16[2048,128]{1,0:T(8,128)(2,1)S(1)}) custom-call(bf16[3,2048,128]{2,1,0:T(8,128)(2,1)} %copy-done.5, bf16[3,2048,128]{2,1,0:T(8,128)(2,1)} %get-tuple-element.25.ka_ref, bf16[3,2048,128]{2,1,0:T(8,128)(2,1)} %get-tuple-element.26.va_ref, bf16[2048,192]{1,0:T(8,128)(2,1)S(1)} %pad_maximum_fusion.12.go_ref, ...), custom_call_target="tpu_custom_call" | custom-call | flops 10737418240 | bytes 4194304 | tf_op jit(solution)/shard_map/attend_back/pallas_call | solution.py:247
  (429 shorter events, 234.7 us)
Async XLA Ops:
  0.7 21.7 %collective-permute-start = (bf16[512,768]{1,0:T(8,128)(2,1)}, bf16[512,768]{1,0:T(8,128)(2,1)}, u32[]{:S(2)}, u32[]{:S(2)}) collective-permute-start(bf16[512,768]{1,0:T(8,128)(2,1)} %bitcast.70), channel_id=1, source_target_pairs={{0,2},{1,3},{2,0},{3,1},{4,6},{5,7},{6,4},{7,5},{8,10},{9,11},{10,... | collective-permute-start | bytes 2359304 | tf_op jit(solution)/shard_map/ppermute | solution.py:39
  3.7 44.5 %collective-permute-start.5 = (bf16[192,768]{1,0:T(8,128)(2,1)}, bf16[192,768]{1,0:T(8,128)(2,1)}, u32[]{:S(2)}, u32[]{:S(2)}) collective-permute-start(bf16[192,768]{1,0:T(8,128)(2,1)} %param.19), channel_id=1, source_target_pairs={{0,2},{1,3},{2,0},{3,1},{4,6},{5,7},{6,4},{7,5},{8,10},{9,11},{10,... | collective-permute-start | bytes 884744 | tf_op jit(solution)/shard_map/ppermute | solution.py:39
  24.8 25.1 %collective-permute-start.1 = (bf16[1024,768]{1,0:T(8,128)(2,1)}, bf16[1024,768]{1,0:T(8,128)(2,1)}, u32[]{:S(2)}, u32[]{:S(2)}) collective-permute-start(bf16[1024,768]{1,0:T(8,128)(2,1)} %pad_maximum_fusion.5), channel_id=1, source_target_pairs={{0,1},{1,0},{2,3},{3,2},{4,5},{5,4},{6,7},{7,6},{8,9},{9,8},{10,11... | collective-permute-start | bytes 4718600 | tf_op jit(solution)/shard_map/ppermute | solution.py:39
  49.3 42.9 %collective-permute-start.6 = (bf16[384,768]{1,0:T(8,128)(2,1)S(1)}, bf16[384,768]{1,0:T(8,128)(2,1)S(1)}, u32[]{:S(2)}, u32[]{:S(2)}) collective-permute-start(bf16[384,768]{1,0:T(8,128)(2,1)S(1)} %pad_maximum_fusion.16), channel_id=1, source_target_pairs={{0,1},{1,0},{2,3},{3,2},{4,5},{5,4},{6,7},{7,6},{8,9},{9,8},{10,11... | collective-permute-start | bytes 1769480 | tf_op jit(solution)/shard_map/ppermute | solution.py:39
  107.5 19.6 %collective-permute-start.7 = (bf16[512,768]{1,0:T(8,128)(2,1)S(1)}, bf16[512,768]{1,0:T(8,128)(2,1)S(1)}, u32[]{:S(2)}, u32[]{:S(2)}) collective-permute-start(bf16[512,768]{1,0:T(8,128)(2,1)S(1)} %fusion.20), channel_id=1, source_target_pairs={{0,2},{1,3},{2,0},{3,1},{4,6},{5,7},{6,4},{7,5},{8,10},{9,11},{10,... | collective-permute-start | bytes 2359304 | tf_op jit(solution)/shard_map/ppermute | solution.py:39
  145.8 36.5 %collective-permute-start.9 = (bf16[1024,768]{1,0:T(8,128)(2,1)S(1)}, bf16[1024,768]{1,0:T(8,128)(2,1)S(1)}, u32[]{:S(2)}, u32[]{:S(2)}) collective-permute-start(bf16[1024,768]{1,0:T(8,128)(2,1)S(1)} %slice.418), channel_id=1, source_target_pairs={{0,2},{1,3},{2,0},{3,1},{4,6},{5,7},{6,4},{7,5},{8,10},{9,11},{10,... | collective-permute-start | bytes 4718600 | tf_op jit(solution)/shard_map/ppermute | solution.py:39
  189.1 19.6 %collective-permute-start.11 = (bf16[512,768]{1,0:T(8,128)(2,1)S(1)}, bf16[512,768]{1,0:T(8,128)(2,1)S(1)}, u32[]{:S(2)}, u32[]{:S(2)}) collective-permute-start(bf16[512,768]{1,0:T(8,128)(2,1)S(1)} %fusion.72), channel_id=1, source_target_pairs={{0,2},{1,3},{2,0},{3,1},{4,6},{5,7},{6,4},{7,5},{8,10},{9,11},{10,... | collective-permute-start | bytes 2359304 | tf_op jit(solution)/shard_map/ppermute | solution.py:39
  220.1 30.2 %collective-permute-start.63 = (bf16[384,768]{1,0:T(8,128)(2,1)S(1)}, bf16[384,768]{1,0:T(8,128)(2,1)S(1)}, u32[]{:S(2)}, u32[]{:S(2)}) collective-permute-start(bf16[384,768]{1,0:T(8,128)(2,1)S(1)} %constant_dynamic-slice_fusion.2), channel_id=1, source_target_pairs={{0,4},{4,0},{8,12},{12,8},{16,20},{20,16},{24,28},{28,24},{1,5},{5... | collective-permute-start | bytes 1769480 | tf_op jit(solution)/shard_map/ppermute | solution.py:39
  242.9 16.3 %collective-permute-start.51 = (bf16[384,768]{1,0:T(8,128)(2,1)S(1)}, bf16[384,768]{1,0:T(8,128)(2,1)S(1)}, u32[]{:S(2)}, u32[]{:S(2)}) collective-permute-start(bf16[384,768]{1,0:T(8,128)(2,1)S(1)} %constant_dynamic-slice_fusion.8), channel_id=1, source_target_pairs={{0,8},{4,12},{8,0},{12,4},{16,24},{20,28},{24,16},{28,20},{1,9},{5... | collective-permute-start | bytes 1769480 | tf_op jit(solution)/shard_map/ppermute | solution.py:39
  248.8 76.3 %collective-permute-start.13 = (bf16[1024,768]{1,0:T(8,128)(2,1)}, bf16[1024,768]{1,0:T(8,128)(2,1)}, u32[]{:S(2)}, u32[]{:S(2)}) collective-permute-start(bf16[1024,768]{1,0:T(8,128)(2,1)} %slice.417), channel_id=1, source_target_pairs={{0,2},{1,3},{2,0},{3,1},{4,6},{5,7},{6,4},{7,5},{8,10},{9,11},{10,... | collective-permute-start | bytes 4718600 | tf_op jit(solution)/shard_map/ppermute | solution.py:39
  250.5 21.3 %collective-permute-start.64 = (bf16[192,768]{1,0:T(8,128)(2,1)S(1)}, bf16[192,768]{1,0:T(8,128)(2,1)S(1)}, u32[]{:S(2)}, u32[]{:S(2)}) collective-permute-start(bf16[192,768]{1,0:T(8,128)(2,1)S(1)} %constant_dynamic-slice_fusion.1), channel_id=1, source_target_pairs={{0,8},{4,12},{8,0},{12,4},{16,24},{20,28},{24,16},{28,20},{1,9},{5... | collective-permute-start | bytes 884744 | tf_op jit(solution)/shard_map/ppermute | solution.py:39
  252.2 25.2 %collective-permute-start.58 = (bf16[192,768]{1,0:T(8,128)(2,1)S(1)}, bf16[192,768]{1,0:T(8,128)(2,1)S(1)}, u32[]{:S(2)}, u32[]{:S(2)}) collective-permute-start(bf16[192,768]{1,0:T(8,128)(2,1)S(1)} %constant_dynamic-slice_fusion.4), channel_id=1, source_target_pairs={{0,8},{4,12},{8,0},{12,4},{16,24},{20,28},{24,16},{28,20},{1,9},{5... | collective-permute-start | bytes 884744 | tf_op jit(solution)/shard_map/ppermute | solution.py:39
  259.4 19.5 %collective-permute-start.52 = (bf16[192,768]{1,0:T(8,128)(2,1)S(1)}, bf16[192,768]{1,0:T(8,128)(2,1)S(1)}, u32[]{:S(2)}, u32[]{:S(2)}) collective-permute-start(bf16[192,768]{1,0:T(8,128)(2,1)S(1)} %constant_dynamic-slice_fusion.7), channel_id=1, source_target_pairs={{0,16},{4,20},{8,24},{12,28},{16,0},{20,4},{24,8},{28,12},{1,17},{... | collective-permute-start | bytes 884744 | tf_op jit(solution)/shard_map/ppermute | solution.py:39
  271.9 16.7 %collective-permute-start.65 = (bf16[96,768]{1,0:T(8,128)(2,1)S(1)}, bf16[96,768]{1,0:T(8,128)(2,1)S(1)}, u32[]{:S(2)}, u32[]{:S(2)}) collective-permute-start(bf16[96,768]{1,0:T(8,128)(2,1)S(1)} %constant_dynamic-slice_fusion), channel_id=1, source_target_pairs={{0,16},{4,20},{8,24},{12,28},{16,0},{20,4},{24,8},{28,12},{1,17},{... | collective-permute-start | bytes 442376 | tf_op jit(solution)/shard_map/ppermute | solution.py:39
  277.4 17.5 %collective-permute-start.59 = (bf16[96,768]{1,0:T(8,128)(2,1)S(1)}, bf16[96,768]{1,0:T(8,128)(2,1)S(1)}, u32[]{:S(2)}, u32[]{:S(2)}) collective-permute-start(bf16[96,768]{1,0:T(8,128)(2,1)S(1)} %constant_dynamic-slice_fusion.3), channel_id=1, source_target_pairs={{0,16},{4,20},{8,24},{12,28},{16,0},{20,4},{24,8},{28,12},{1,17},{... | collective-permute-start | bytes 442376 | tf_op jit(solution)/shard_map/ppermute | solution.py:39
  279.0 22.4 %collective-permute-start.53 = (bf16[96,768]{1,0:T(8,128)(2,1)S(1)}, bf16[96,768]{1,0:T(8,128)(2,1)S(1)}, u32[]{:S(2)}, u32[]{:S(2)}) collective-permute-start(bf16[96,768]{1,0:T(8,128)(2,1)S(1)} %constant_dynamic-slice_fusion.6), channel_id=1, source_target_pairs={{0,4},{4,0},{8,12},{12,8},{16,20},{20,16},{24,28},{28,24},{1,5},{5... | collective-permute-start | bytes 442376 | tf_op jit(solution)/shard_map/ppermute | solution.py:39
  301.3 16.1 %collective-permute-start.67 = (bf16[192,768]{1,0:T(8,128)(2,1)S(1)}, bf16[192,768]{1,0:T(8,128)(2,1)}, u32[]{:S(2)}, u32[]{:S(2)}) collective-permute-start(bf16[192,768]{1,0:T(8,128)(2,1)S(1)} %maximum_select_fusion.12), channel_id=1, source_target_pairs={{0,8},{4,12},{8,0},{12,4},{16,24},{20,28},{24,16},{28,20},{1,9},{5... | collective-permute-start | bytes 884744 | tf_op jit(solution)/shard_map/ppermute | solution.py:39
  304.1 18.9 %collective-permute-start.61 = (bf16[192,768]{1,0:T(8,128)(2,1)S(1)}, bf16[192,768]{1,0:T(8,128)(2,1)}, u32[]{:S(2)}, u32[]{:S(2)}) collective-permute-start(bf16[192,768]{1,0:T(8,128)(2,1)S(1)} %maximum_select_fusion.11), channel_id=1, source_target_pairs={{0,8},{4,12},{8,0},{12,4},{16,24},{20,28},{24,16},{28,20},{1,9},{5... | collective-permute-start | bytes 884744 | tf_op jit(solution)/shard_map/ppermute | solution.py:39
  308.1 19.7 %collective-permute-start.55 = (bf16[192,768]{1,0:T(8,128)(2,1)S(1)}, bf16[192,768]{1,0:T(8,128)(2,1)S(1)}, u32[]{:S(2)}, u32[]{:S(2)}) collective-permute-start(bf16[192,768]{1,0:T(8,128)(2,1)S(1)} %maximum_select_fusion.10), channel_id=1, source_target_pairs={{0,16},{4,20},{8,24},{12,28},{16,0},{20,4},{24,8},{28,12},{1,17},{... | collective-permute-start | bytes 884744 | tf_op jit(solution)/shard_map/ppermute | solution.py:39
  325.1 17.3 %collective-permute-start.62 = (bf16[384,768]{1,0:T(8,128)(2,1)}, bf16[384,768]{1,0:T(8,128)(2,1)}, u32[]{:S(2)}, u32[]{:S(2)}) collective-permute-start(bf16[384,768]{1,0:T(8,128)(2,1)} %maximum_select_fusion.4), channel_id=1, source_target_pairs={{0,4},{4,0},{8,12},{12,8},{16,20},{20,16},{24,28},{28,24},{1,5},{5... | collective-permute-start | bytes 1769480 | tf_op jit(solution)/shard_map/ppermute | solution.py:39
  327.8 21.2 %collective-permute-start.14 = (bf16[512,768]{1,0:T(8,128)(2,1)}, bf16[512,768]{1,0:T(8,128)(2,1)}, u32[]{:S(2)}, u32[]{:S(2)}) collective-permute-start(bf16[512,768]{1,0:T(8,128)(2,1)} %fusion.14), channel_id=1, source_target_pairs={{0,1},{1,0},{2,3},{3,2},{4,5},{5,4},{6,7},{7,6},{8,9},{9,8},{10,11... | collective-permute-start | bytes 2359304 | tf_op jit(solution)/shard_map/ppermute | solution.py:39
  328.9 16.8 %collective-permute-start.56 = (bf16[384,768]{1,0:T(8,128)(2,1)}, bf16[384,768]{1,0:T(8,128)(2,1)}, u32[]{:S(2)}, u32[]{:S(2)}) collective-permute-start(bf16[384,768]{1,0:T(8,128)(2,1)} %maximum_select_fusion.3), channel_id=1, source_target_pairs={{0,8},{4,12},{8,0},{12,4},{16,24},{20,28},{24,16},{28,20},{1,9},{5... | collective-permute-start | bytes 1769480 | tf_op jit(solution)/shard_map/ppermute | solution.py:39
  368.6 91.4 %collective-permute-start.38 = (bf16[384,768]{1,0:T(8,128)(2,1)S(1)}, bf16[384,768]{1,0:T(8,128)(2,1)S(1)}, u32[]{:S(2)}, u32[]{:S(2)}) collective-permute-start(bf16[384,768]{1,0:T(8,128)(2,1)S(1)} %slice.419), channel_id=1, source_target_pairs={{0,2},{1,3},{2,0},{3,1},{4,6},{5,7},{6,4},{7,5},{8,10},{9,11},{10,... | collective-permute-start | bytes 1769480 | tf_op jit(solution)/shard_map/ppermute | solution.py:39
  433.4 47.2 %collective-permute-start.18 = (bf16[1024,768]{1,0:T(8,128)(2,1)S(1)}, bf16[1024,768]{1,0:T(8,128)(2,1)S(1)}, u32[]{:S(2)}, u32[]{:S(2)}) collective-permute-start(bf16[1024,768]{1,0:T(8,128)(2,1)S(1)} %slice.416), channel_id=1, source_target_pairs={{0,2},{1,3},{2,0},{3,1},{4,6},{5,7},{6,4},{7,5},{8,10},{9,11},{10,... | collective-permute-start | bytes 4718600 | tf_op jit(solution)/shard_map/ppermute | solution.py:39
  (116 other events, 898.3 us)

commit v2 on v1

v2 whole, which is shorter than its diff:
```python
import functools
import math

import jax
import jax.numpy as jnp
from jax import lax
from jax.experimental import pallas as pl
from jax.experimental.pallas import tpu as pltpu
from jax.sharding import PartitionSpec as P

HEAD_DIM = 64
EPSILON = 1e-05
ROPE_BASE = 1000.0
APART = -(2.0**30)
WIDE = 128
SEG_AT = HEAD_DIM
ROW_AT = HEAD_DIM + 8
VMEM = 48 * 2**20
bf16 = jnp.bfloat16
f32 = jnp.float32
NT = (((1,), (1,)), ((), ()))
TN = (((0,), (0,)), ((), ()))


def dot(a, b):
    return jnp.dot(a, b, preferred_element_type=f32)


def dot_nt(a, b):
    return lax.dot_general(a, b, NT, preferred_element_type=f32)


def dot_tn(a, b):
    return lax.dot_general(a, b, TN, preferred_element_type=f32)


def swap(value, axis, bit):
    size = lax.axis_size(axis)
    return lax.ppermute(value, axis, [(i, i ^ bit) for i in range(size)])


def after(value, *others):
    return lax.optimization_barrier((value, *others))[0]


def all_after(values, *others):
    return list(lax.optimization_barrier((tuple(values), others))[0])


def scatter_sum(blocks, axis):
    held = dict(enumerate(blocks))
    rows = blocks[0].shape[0]
    step = 1
    while step < len(blocks):
        sent = [k for k in held if k & step]
        got = [held.pop(k).astype(bf16) for k in sent]
        got = swap(got[0] if len(got) == 1 else jnp.concatenate(got, axis=0), axis, step)
        for n, k in enumerate(sent):
            held[k ^ step] = held[k ^ step] + got[n * rows : (n + 1) * rows].astype(f32)
        step *= 2
    return held[0]


def exchange(blocks, axis):
    return [b if j == 0 else swap(b, axis, j) for j, b in enumerate(blocks)]


def sum_steps(value, axis, order):
    me = lax.axis_index(axis)
    for bit in order:
        half = value.shape[0] // 2
        side = (me >> bit) & 1
        mine = lax.dynamic_slice_in_dim(value, side * half, half, 0)
        other = lax.dynamic_slice_in_dim(value, (1 - side) * half, half, 0)
        got = swap(other, axis, 1 << bit)
        deps = yield other
        if deps is not None:
            got = after(got, deps)
        value = (mine.astype(f32) + got.astype(f32)).astype(value.dtype)
    for bit in reversed(order):
        side = (me >> bit) & 1
        got = swap(value, axis, 1 << bit)
        deps = yield value
        if deps is not None:
            got = after(got, deps)
        value = jnp.where(
            side == 0, jnp.concatenate([value, got], 0), jnp.concatenate([got, value], 0)
        )
    return value


class Sum:
    def __init__(self, value, order):
        self.steps = sum_steps(value, "dp", order)
        self.result = None
        self.sent = next(self.steps)

    def advance(self, deps=None):
        if self.result is None:
            try:
                self.sent = self.steps.send(deps)
            except StopIteration as end:
                self.result = end.value

    def finish(self):
        while self.result is None:
            self.advance()
        return self.result


def small_sum(value, axis):
    step = lax.axis_size(axis) // 2
    while step:
        value = value + swap(value, axis, step)
        step //= 2
    return value


def project_kernel(heads, count, *refs):
    pieces, refs = refs[:count], refs[count:]
    w_ref, cos_ref, sin_ref, seg_ref = refs[:4]
    x_ref, qa_ref, ka_ref, va_ref = refs[-4:]
    rows = x_ref.shape[0]
    for n, piece in enumerate(pieces):

        @pl.when(pl.program_id(0) == n)
        def _(piece=piece):
            x_ref[...] = piece[...]

    proj = dot(x_ref[...], w_ref[...])
    cosine, sine = cos_ref[...], sin_ref[...]
    lane = lax.broadcasted_iota(jnp.int32, (rows, WIDE), 1)
    first = lane < HEAD_DIM
    same = lane == seg_ref[...] + (SEG_AT + 1)
    qf = jnp.where(same, APART, 0.0)
    kf = jnp.where((lane < ROW_AT + 3) & ~same, 1.0, 0.0)
    ones = jnp.where(lane < HEAD_DIM + 3, 1.0, 0.0)
    for h in range(heads):
        at = [(part * heads + h) * WIDE for part in range(3)]
        q = proj[:, at[0] : at[0] + WIDE]
        k = proj[:, at[1] : at[1] + WIDE]
        v = proj[:, at[2] : at[2] + WIDE]
        q = q * cosine + pltpu.roll(q, HEAD_DIM, 1) * sine
        k = k * cosine + pltpu.roll(k, HEAD_DIM, 1) * sine
        qa_ref[h] = jnp.where(first, q * (1.0 / math.sqrt(HEAD_DIM)), qf).astype(bf16)
        ka_ref[h] = jnp.where(first, k, kf).astype(bf16)
        va_ref[h] = jnp.where(first, v, ones).astype(bf16)


def project(pieces, start, w, cosine, sine, seg, heads, done=()):
    block, width = pieces[0].shape
    length = cosine.shape[0]
    rows = lambda n: pl.BlockSpec((block, n), lambda i: (start + i, 0))
    whole = lambda a: pl.BlockSpec(a.shape, lambda i: (0, 0))
    out = pl.BlockSpec((heads, block, WIDE), lambda i: (0, start + i, 0))
    given = len(pieces) + 4
    return pl.pallas_call(
        functools.partial(project_kernel, heads, len(pieces)),
        grid=(len(pieces),),
        in_specs=[whole(p) for p in pieces]
        + [whole(w), rows(WIDE), rows(WIDE), rows(1)]
        + [pl.BlockSpec(memory_space=pl.ANY)] * len(done),
        out_specs=[rows(width)] + [out] * 3,
        out_shape=[jax.ShapeDtypeStruct((length, width), bf16)]
        + [jax.ShapeDtypeStruct((heads, length, WIDE), bf16)] * 3,
        input_output_aliases={given + n: n for n in range(len(done))},
        compiler_params=pltpu.CompilerParams(vmem_limit_bytes=VMEM),
        cost_estimate=pl.CostEstimate(
            flops=2 * len(pieces) * block * width * w.shape[1], bytes_accessed=4 * 2**20, transcendentals=0
        ),
        name="project",
    )(*pieces, w, cosine, sine, seg, *done)


def split3(value):
    high = value.astype(bf16).astype(f32)
    rest = value - high
    middle = rest.astype(bf16).astype(f32)
    return high, middle, rest - middle


def put_row(wide, at, value):
    lane = lax.broadcasted_iota(jnp.int32, wide.shape, 1)
    for n, part in enumerate(split3(value)):
        wide = jnp.where(lane == at + n, -part, wide)
    return wide


def attend_kernel(heads, qa_ref, ka_ref, va_ref, *refs):
    ctx_ref, qb_ref = refs[-2:]
    parts = []
    for h in range(heads):
        qa = qa_ref[h]
        scores = dot_nt(qa, ka_ref[h])
        peak = jnp.max(scores, axis=1, keepdims=True)
        weights = jnp.exp(scores - peak).astype(bf16)
        summed = dot(weights, va_ref[h])
        total = summed[:, HEAD_DIM : HEAD_DIM + 1]
        parts.append(summed[:, :HEAD_DIM] / total)
        qb_ref[h] = put_row(qa.astype(f32), ROW_AT, peak + jnp.log(total)).astype(bf16)
    ctx_ref[...] = jnp.concatenate(parts, axis=1).astype(bf16)


def attend(qa, ka, va, start, count, done=(), block=256):
    heads, length, _ = qa.shape
    first = start // block
    whole = pl.BlockSpec((heads, length, WIDE), lambda i: (0, 0, 0))
    part = pl.BlockSpec((heads, block, WIDE), lambda i: (0, first + i, 0))
    return pl.pallas_call(
        functools.partial(attend_kernel, heads),
        grid=(count // block,),
        in_specs=[part, whole, whole] + [pl.BlockSpec(memory_space=pl.ANY)] * len(done),
        out_specs=[pl.BlockSpec((block, heads * HEAD_DIM), lambda i: (first + i, 0)), part],
        out_shape=[
            jax.ShapeDtypeStruct((length, heads * HEAD_DIM), bf16),
            jax.ShapeDtypeStruct((heads, length, WIDE), bf16),
        ],
        input_output_aliases={3 + n: n for n in range(len(done))},
        compiler_params=pltpu.CompilerParams(vmem_limit_bytes=VMEM),
        cost_estimate=pl.CostEstimate(
            flops=4 * heads * count * length * 256,
            bytes_accessed=8 * 2**20,
            transcendentals=heads * count * length,
        ),
        name="attend",
    )(qa, ka, va, *done)


def swap_halves(value, lane):
    half = HEAD_DIM // 2
    return jnp.where(
        lane < half, pltpu.roll(value, WIDE - half, 1), pltpu.roll(value, half, 1)
    )


def attend_back_kernel(head, block, qb_ref, ka_ref, va_ref, *refs):
    gos, refs = refs[:4], refs[4:]
    ctx_ref, cos_ref, sin_ref, dq_ref, dkv_ref, doa, dqt = refs
    j = pl.program_id(0)
    length = qb_ref.shape[1]
    cols = pl.ds(head * HEAD_DIM, HEAD_DIM)

    @pl.when(j == 0)
    def _():
        dqt[...] = jnp.zeros_like(dqt)
        for i in range(length // block):
            at = pl.ds(i * block, block)
            go = gos[i][:block, cols].astype(f32)
            delta = jnp.sum(go * ctx_ref[at, cols].astype(f32), axis=1, keepdims=True)
            wide = jnp.concatenate([go, jnp.zeros_like(go)], axis=1)
            doa[at, :] = put_row(wide, HEAD_DIM, delta).astype(bf16)

    ka, va = ka_ref[0], va_ref[0]
    kt = ka.astype(f32).T[:HEAD_DIM].astype(bf16)
    dk = dv = None
    for i in range(length // block):
        at = pl.ds(i * block, block)
        qb, do = qb_ref[0, at, :], doa[at, :]
        weights = jnp.exp(dot_nt(ka, qb))
        grads = (weights * dot_nt(va, do)).astype(bf16)
        v_part = dot(weights.astype(bf16), do)
        k_part = dot(grads, qb)
        dk = k_part if i == 0 else dk + k_part
        dv = v_part if i == 0 else dv + v_part
        dqt[:, at] += dot(kt, grads)
    lane = lax.broadcasted_iota(jnp.int32, dk.shape, 1)
    rows = pl.ds(pl.multiple_of(j * ka.shape[0], ka.shape[0]), ka.shape[0])
    dk = dk * cos_ref[rows, :] - swap_halves(dk, lane) * sin_ref[rows, :]
    dkv_ref[...] = jnp.where(
        lane < HEAD_DIM, dk, pltpu.roll(jnp.where(lane < HEAD_DIM, dv, 0.0), HEAD_DIM, 1)
    ).astype(bf16)

    @pl.when(j == pl.num_programs(0) - 1)
    def _():
        for i in range(length // block):
            at = pl.ds(i * block, block)
            part = dqt[:, at]
            dq = jnp.concatenate([part, jnp.zeros_like(part)], axis=0).T
            lanes = lax.broadcasted_iota(jnp.int32, dq.shape, 1)
            dq = dq * cos_ref[at, :] - swap_halves(dq, lanes) * sin_ref[at, :]
            dq_ref[at, :] = (dq[:, :HEAD_DIM] * (1.0 / math.sqrt(HEAD_DIM))).astype(bf16)


def attend_back(head, qb, ka, va, gos, ctx, cosine, sine, block_k=512):
    _, length, _ = qb.shape
    block_q = length // len(gos)
    at_head = pl.BlockSpec((1, length, WIDE), lambda j: (head, 0, 0))
    part = pl.BlockSpec((1, block_k, WIDE), lambda j: (head, j, 0))
    full = lambda a: pl.BlockSpec(a.shape, lambda j: (0, 0))
    return pl.pallas_call(
        functools.partial(attend_back_kernel, head, block_q),
        grid=(length // block_k,),
        in_specs=[at_head, part, part] + [full(a) for a in (*gos, ctx, cosine, sine)],
        out_specs=[
            pl.BlockSpec((length, HEAD_DIM), lambda j: (0, 0)),
            pl.BlockSpec((block_k, WIDE), lambda j: (j, 0)),
        ],
        out_shape=[
            jax.ShapeDtypeStruct((length, HEAD_DIM), bf16),
            jax.ShapeDtypeStruct((length, WIDE), bf16),
        ],
        scratch_shapes=[pltpu.VMEM((length, WIDE), bf16), pltpu.VMEM((HEAD_DIM, length), f32)],
        compiler_params=pltpu.CompilerParams(vmem_limit_bytes=VMEM),
        cost_estimate=pl.CostEstimate(
            flops=2**20,
            bytes_accessed=2**16,
            transcendentals=0,
        ),
        name="attend_back",
    )(qb, ka, va, *gos, ctx, cosine, sine)


ANY = pl.BlockSpec(memory_space=pl.ANY)
IN_VMEM = pl.BlockSpec(memory_space=pltpu.VMEM)


def start(source, target, sem):
    copy = pltpu.make_async_copy(source, target, sem)
    copy.start()
    return copy


def norm_parts(row_values):
    centred = row_values - jnp.mean(row_values, axis=-1, keepdims=True)
    inverse = lax.rsqrt(jnp.mean(centred * centred, axis=-1, keepdims=True) + EPSILON)
    return (centred * inverse, inverse)


def norm_back(grad_norm, normalized, inverse):
    return inverse * (
        grad_norm
        - jnp.mean(grad_norm, axis=-1, keepdims=True)
        - normalized * jnp.mean(grad_norm * normalized, axis=-1, keepdims=True)
    )


def mix_kernel(own_ref, *refs):
    parts, outs, refs = refs[:4], refs[4:8], refs[8:]
    gain_ref, shift_ref, norm_ref, inverse_ref, low_ref = refs
    total = own_ref[...].astype(f32)
    for part, out in zip(parts, outs):
        total = total + dot(part[...], out[...])
    norm, inverse = norm_parts(total)
    norm_ref[...] = norm
    inverse_ref[...] = jnp.broadcast_to(inverse, inverse_ref.shape)
    low_ref[...] = (norm * gain_ref[...] + shift_ref[...]).astype(bf16)


def mix(own, parts, outs, gain, shift, block=256):
    length, width = own.shape
    rows = lambda a: pl.BlockSpec((block, a.shape[1]), lambda i: (i, 0))
    whole = lambda a: pl.BlockSpec(a.shape, lambda i: (0, 0))
    shapes = [
        jax.ShapeDtypeStruct((length, width), f32),
        jax.ShapeDtypeStruct((length, WIDE), f32),
        jax.ShapeDtypeStruct((length, width), bf16),
    ]
    return pl.pallas_call(
        mix_kernel,
        grid=(length // block,),
        in_specs=[rows(own)] + [rows(p) for p in parts] + [whole(w) for w in outs] + [whole(gain), whole(shift)],
        out_specs=[rows(s) for s in shapes],
        out_shape=shapes,
        compiler_params=pltpu.CompilerParams(vmem_limit_bytes=VMEM),
        cost_estimate=pl.CostEstimate(flops=2 * length * width * width, bytes_accessed=6 * 2**20, transcendentals=0),
        name="mix",
    )(own, *parts, *outs, gain, shift)


def feed(low, gate, up):
    gate_pre, up_pre = dot(low, gate), dot(low, up)
    return gate_pre, up_pre


def hidden_of(gate_pre, up_pre):
    return (gate_pre * jax.nn.sigmoid(gate_pre) * up_pre).astype(bf16)


def feed_back(grad_hidden, gate_pre, up_pre):
    sigmoid = jax.nn.sigmoid(gate_pre)
    grad_gate = grad_hidden * up_pre * sigmoid * (1.0 + gate_pre * (1.0 - sigmoid))
    return grad_gate.astype(bf16), (grad_hidden * gate_pre * sigmoid).astype(bf16)


def shard_copies(n, firsts, shards, buffers, sem):
    refs = list(shards[3 * n : 3 * n + 3])
    hidden = refs[2].shape[0]
    for k in range(2):
        refs[k] = refs[k].at[:, pl.ds(firsts[2 * n + k] * hidden, hidden)]
    return [start(ref, buffer.at[n], sem.at[n, k]) for k, (ref, buffer) in enumerate(zip(refs, buffers))]


def shard_args(shards):
    args = [a for (gate, _), (up, _), down in shards for a in (gate, up, down)]
    return args, [first for (_, g), (_, u), _ in shards for first in (g, u)]


HALVES = 2


def halves(length):
    return [pl.ds(n * (length // HALVES), length // HALVES) for n in range(HALVES)]


def forward_kernel(firsts, last, low_ref, *refs):
    count = len(firsts) // 2
    shards, refs = refs[: 3 * count], refs[3 * count :]
    if last:
        before_ref, norm_ref, cot_ref, gain_ref, shift_ref, gain2_ref, shift2_ref = refs[:7]
        gates_ref, ups_ref, encoded_ref, second_ref, low2_ref, small_ref = refs[7:13]
        gate, up, down, gates, ups, sem, out_sem, total, before, norm1, cot_in, more_sem = refs[13:]
    else:
        gates_ref, ups_ref, total, gate, up, down, gates, ups, sem, out_sem = refs
    buffers = (gate, up, down)
    coming = [shard_copies(0, firsts, shards, buffers, sem)]
    if last:
        extra = [
            start(ref, buffer, more_sem.at[n])
            for n, (ref, buffer) in enumerate([(before_ref, before), (norm_ref, norm1), (cot_ref, cot_in)])
        ]
    going = []
    hidden = down.shape[1]
    for n in range(count):
        if n + 1 < count:
            coming.append(shard_copies(n + 1, firsts, shards, buffers, sem))
        for copy in coming[n]:
            copy.wait()
        for at in halves(low_ref.shape[0]):
            gate_pre, up_pre = feed(low_ref[at, :], gate[n], up[n])
            gates[n, at, :] = gate_pre.astype(bf16)
            ups[n, at, :] = up_pre.astype(bf16)
            part = dot(hidden_of(gate_pre, up_pre), down[n])
            total[at, :] = part if n == 0 else total[at, :] + part
        cols = pl.ds(n * hidden, hidden)
        going.append(start(gates.at[n], gates_ref.at[:, cols], out_sem.at[n, 0]))
        going.append(start(ups.at[n], ups_ref.at[:, cols], out_sem.at[n, 1]))
    if last:
        for copy in extra:
            copy.wait()
        normed = norm1[...] * gain_ref[...] + shift_ref[...]
        norm, inverse = norm_parts(normed + (before[...] + total[...]))
        cot = cot_in[...].astype(f32)
        encoded_ref[...] = (norm * gain2_ref[...] + shift2_ref[...]).astype(bf16)
        second = norm_back(cot * gain2_ref[...], norm, inverse)
        second_ref[...] = second
        low2_ref[...] = second.astype(bf16)
        small_ref[...] = jnp.concatenate(
            [jnp.sum(cot * norm, axis=0, keepdims=True), jnp.sum(cot, axis=0, keepdims=True)], axis=0
        )
    for copy in going:
        copy.wait()


def forward(low, shards, last=()):
    length, width = low.shape
    count, hidden = len(shards), shards[0][2].shape[0]
    args, firsts = shard_args(shards)
    shapes = [jax.ShapeDtypeStruct((length, hidden * count), bf16)] * 2
    out_specs = [ANY, ANY]
    scratch = [
        pltpu.VMEM((count, width, hidden), bf16),
        pltpu.VMEM((count, width, hidden), bf16),
        pltpu.VMEM((count, hidden, width), bf16),
        pltpu.VMEM((count, length, hidden), bf16),
        pltpu.VMEM((count, length, hidden), bf16),
        pltpu.SemaphoreType.DMA((count, 3)),
        pltpu.SemaphoreType.DMA((count, 2)),
    ]
    if last:
        shapes += [
            jax.ShapeDtypeStruct((length, width), bf16),
            jax.ShapeDtypeStruct((length, width), f32),
            jax.ShapeDtypeStruct((length, width), bf16),
            jax.ShapeDtypeStruct((2, width), f32),
        ]
        out_specs += [IN_VMEM] * 4
        wide = pltpu.VMEM((length, width), f32)
        scratch += [wide, wide, wide, pltpu.VMEM((length, width), bf16), pltpu.SemaphoreType.DMA((3,))]
    else:
        shapes.append(jax.ShapeDtypeStruct((length, width), f32))
        out_specs.append(IN_VMEM)
    return pl.pallas_call(
        functools.partial(forward_kernel, firsts, bool(last)),
        in_specs=[IN_VMEM] + [ANY] * len(args) + [ANY] * len(last[:3]) + [IN_VMEM] * len(last[3:]),
        out_specs=out_specs,
        out_shape=shapes,
        scratch_shapes=scratch,
        compiler_params=pltpu.CompilerParams(vmem_limit_bytes=VMEM),
        cost_estimate=pl.CostEstimate(
            flops=6 * length * width * hidden * count,
            bytes_accessed=12 * 2**20,
            transcendentals=length * hidden * count,
        ),
        name="feed_forward",
    )(low, *args, *last)


def backward_kernel(firsts, low2_ref, *refs):
    count = len(firsts) // 2
    shards, refs = refs[: 3 * count], refs[3 * count :]
    saved, refs = refs[:4], refs[4:]
    late_refs, refs = refs[:7], refs[7:]
    gain_ref, small_in_ref, first_ref, low_ref, ctx_ref = refs[:5]
    gate, up, down, gates, ups, total, second, norm1, inverse, outs, sem, saved_sem, late_sem = refs[5:]
    buffers = (gate, up, down)
    hidden = down.shape[1]

    def fetch(n):
        part, cols = n * 2 // count, pl.ds(n % (count // 2) * hidden, hidden)
        return shard_copies(n, firsts, shards, buffers, sem) + [
            start(ref.at[:, cols], buffer.at[n], saved_sem.at[n, k])
            for k, (ref, buffer) in enumerate(zip(saved[2 * part : 2 * part + 2], (gates, ups)))
        ]

    coming = [fetch(0)]
    late = []
    for n in range(count):
        if n + 1 < count:
            coming.append(fetch(n + 1))
        else:
            targets = [second, norm1, inverse] + [outs.at[k] for k in range(4)]
            late = [start(ref, target, late_sem.at[k]) for k, (ref, target) in enumerate(zip(late_refs, targets))]
        for copy in coming[n]:
            copy.wait()
        for at in halves(low2_ref.shape[0]):
            grad_hidden = dot_nt(low2_ref[at, :], down[n])
            grad_gate, grad_up = feed_back(grad_hidden, gates[n, at, :].astype(f32), ups[n, at, :].astype(f32))
            part = dot_nt(grad_gate, gate[n]) + dot_nt(grad_up, up[n])
            total[at, :] = part if n == 0 else total[at, :] + part
    for copy in late:
        copy.wait()
    normed_grad, norm = second[...] + total[...], norm1[...]
    first = norm_back(normed_grad * gain_ref[...], norm, inverse[:, :1])
    first_ref[...] = first
    low = first.astype(bf16)
    low_ref[...] = low
    small = jnp.concatenate(
        [
            jnp.sum(normed_grad * norm, axis=0, keepdims=True),
            jnp.sum(normed_grad, axis=0, keepdims=True),
            small_in_ref[...],
        ],
        axis=0,
    )
    width = outs.shape[1]
    small = jnp.concatenate([small[:, k * width : (k + 1) * width] for k in range(4)], axis=0)
    high = small.astype(bf16)
    small = jnp.concatenate([high, (small - high.astype(f32)).astype(bf16)], axis=0)
    length = low.shape[0]
    for k in range(4):
        ctx_ref[k, :length, :] = dot_nt(low, outs[k]).astype(bf16)
        ctx_ref[k, length:, :] = small


SMALL = 32


def backward(low2, shards, saved, second, norm, inverse, outs, gain, small):
    length, width = low2.shape
    count, hidden = len(shards), shards[0][2].shape[0]
    args, firsts = shard_args(shards)
    late = [second, norm, inverse, *outs]
    wide = pltpu.VMEM((length, width), f32)
    return pl.pallas_call(
        functools.partial(backward_kernel, firsts),
        in_specs=[IN_VMEM] + [ANY] * (len(args) + len(saved) + len(late)) + [IN_VMEM] * 2,
        out_specs=[IN_VMEM] * 3,
        out_shape=[
            jax.ShapeDtypeStruct((length, width), f32),
            jax.ShapeDtypeStruct((length, width), bf16),
            jax.ShapeDtypeStruct((4, length + SMALL, outs[0].shape[0]), bf16),
        ],
        scratch_shapes=[
            pltpu.VMEM((count, width, hidden), bf16),
            pltpu.VMEM((count, width, hidden), bf16),
            pltpu.VMEM((count, hidden, width), bf16),
            pltpu.VMEM((count, length, hidden), bf16),
            pltpu.VMEM((count, length, hidden), bf16),
            wide,
            wide,
            wide,
            pltpu.VMEM(inverse.shape, f32),
            pltpu.VMEM((4, *outs[0].shape), bf16),
            pltpu.SemaphoreType.DMA((count, 3)),
            pltpu.SemaphoreType.DMA((count, 2)),
            pltpu.SemaphoreType.DMA((len(late),)),
        ],
        compiler_params=pltpu.CompilerParams(vmem_limit_bytes=VMEM),
        cost_estimate=pl.CostEstimate(
            flops=6 * length * width * hidden * count,
            bytes_accessed=24 * 2**20,
            transcendentals=length * hidden * count,
        ),
        name="feed_back",
    )(low2, *args, *saved, *late, gain, small)


def weights_kernel(*refs):
    rows, grads, weights, refs = refs[:4], refs[4:8], refs[8:11], refs[11:]
    targets, refs = refs[:3], refs[3:]
    gate, up, down, low, low_t, low2, dgate, dup, hidden_t, result, sem, out_sem = refs
    block = rows[0].shape[0]
    at = [pl.ds(n * block, block) for n in range(4)]

    def fetch(n):
        return [
            start(rows[n], low.at[at[n], :], sem.at[n, 0]),
            start(grads[n], low2.at[at[n], :], sem.at[n, 1]),
        ]

    coming = [fetch(0)]
    own = [start(w, buffer, sem.at[4 + k, 0]) for k, (w, buffer) in enumerate(zip(weights, (gate, up, down)))]
    coming.append(fetch(1))
    for copy in own:
        copy.wait()
    for n in range(4):
        if n + 2 < 4:
            coming.append(fetch(n + 2))
        for copy in coming[n]:
            copy.wait()
        here = low[at[n], :]
        low_t[:, at[n]] = here.T
        gate_pre, up_pre = feed(here, gate[...], up[...])
        grad_hidden = dot_nt(low2[at[n], :], down[...])
        dgate[at[n], :], dup[at[n], :] = feed_back(grad_hidden, gate_pre, up_pre)
        hidden_t[:, at[n]] = hidden_of(gate_pre, up_pre).T
    going = []
    for k, (left, right) in enumerate([(low_t, dgate), (low_t, dup), (hidden_t, low2)]):
        result[k] = dot(left[...], right[...]).astype(bf16)
        going.append(start(result.at[k], targets[k], out_sem.at[k]))
    for copy in going:
        copy.wait()


def weight_grads(rows, grads, gate, up, down):
    block, width = rows[0].shape
    length, hidden = 4 * block, gate.shape[1]
    return pl.pallas_call(
        weights_kernel,
        in_specs=[ANY] * 11,
        out_specs=[ANY] * 3,
        out_shape=[
            jax.ShapeDtypeStruct((width, hidden), bf16),
            jax.ShapeDtypeStruct((width, hidden), bf16),
            jax.ShapeDtypeStruct((hidden, width), bf16),
        ],
        scratch_shapes=[
            pltpu.VMEM((width, hidden), bf16),
            pltpu.VMEM((width, hidden), bf16),
            pltpu.VMEM((hidden, width), bf16),
            pltpu.VMEM((length, width), bf16),
            pltpu.VMEM((width, length), bf16),
            pltpu.VMEM((length, width), bf16),
            pltpu.VMEM((length, hidden), bf16),
            pltpu.VMEM((length, hidden), bf16),
            pltpu.VMEM((hidden, length), bf16),
            pltpu.VMEM((3, width, hidden), bf16),
            pltpu.SemaphoreType.DMA((7, 2)),
            pltpu.SemaphoreType.DMA((3,)),
        ],
        compiler_params=pltpu.CompilerParams(vmem_limit_bytes=VMEM),
        cost_estimate=pl.CostEstimate(
            flops=12 * length * width * hidden, bytes_accessed=16 * 2**20, transcendentals=length * hidden
        ),
        name="feed_weights",
    )(*rows, *grads, gate, up, down)


def positions(segments):
    places = jnp.arange(segments.shape[0], dtype=jnp.int32)
    before = jnp.concatenate([segments[:1] - 1, segments[:-1]])
    starts = lax.cummax(jnp.where(segments != before, places, 0), axis=0)
    return (places - starts).astype(f32)


def relative_rows(value, blocks):
    me = lax.axis_index("tensor")
    rows = value.shape[0] // blocks
    return jnp.concatenate(
        [lax.dynamic_slice_in_dim(value, (me ^ j) * rows, rows, 0) for j in range(blocks)], axis=0
    )


def wide_weight(query_weight, key_weight, value_weight, heads):
    width = query_weight.shape[0]
    half = HEAD_DIM // 2

    def turned(weight):
        w = weight.reshape(width, heads, HEAD_DIM)
        swapped = jnp.concatenate([w[..., half:], w[..., :half]], axis=-1)
        return jnp.concatenate([w, swapped], axis=-1).reshape(width, heads * WIDE)

    v = value_weight.reshape(width, heads, HEAD_DIM)
    v = jnp.concatenate([v, jnp.zeros_like(v)], axis=-1).reshape(width, heads * WIDE)
    return jnp.concatenate([turned(query_weight), turned(key_weight), v], axis=1)


def local(
    tokens,
    segment_ids,
    query_weight,
    key_weight,
    value_weight,
    output_weight,
    attn_gain,
    attn_shift,
    gate_weight,
    up_weight,
    down_weight,
    mlp_gain,
    mlp_shift,
    cotangent,
):
    own = tokens[0]
    segments = segment_ids[0]
    head_width = query_weight.shape[1]
    heads = head_width // HEAD_DIM
    group = lax.axis_size("tensor")
    block = own.shape[0]
    dp = lax.axis_size("dp")
    bits = list(range(int(math.log2(dp))))
    orders = [bits, bits[1:] + bits[:1]]

    near = lambda a: swap(a, "tensor", 1)
    far = lambda a: swap(a, "tensor", 2)

    share = gate_weight.shape[0] // dp
    at = lax.axis_index("dp") * share
    mine = jnp.concatenate(
        [lax.dynamic_slice_in_dim(w, at, share, 0) for w in (gate_weight, up_weight)], axis=1
    )
    far_own = far(after(own, mine))
    mine = far(mine)
    near_own = near(own)
    near_weights = [near(w) for w in (gate_weight, up_weight, down_weight, output_weight)]

    angle_rate = ROPE_BASE ** (-(jnp.arange(HEAD_DIM // 2, dtype=f32) * 2.0 / HEAD_DIM))
    rates = jnp.concatenate([angle_rate, angle_rate, jnp.zeros(HEAD_DIM, f32)])
    signs = jnp.concatenate([-jnp.ones(HEAD_DIM // 2, f32), jnp.ones(HEAD_DIM // 2, f32), jnp.zeros(HEAD_DIM, f32)])
    angles = relative_rows(positions(segments), group)[:, None] * rates[None, :]
    cos_wide, sin_wide = jnp.cos(angles), jnp.sin(angles) * signs[None, :]
    seg = relative_rows(segments, group)[:, None]

    joint_wide = wide_weight(query_weight, key_weight, value_weight, heads)
    mine = after(mine, cos_wide)
    far_mixed = lax.all_gather(mine, "dp", axis=0, tiled=True)
    near_gate, near_up, near_down, near_out = all_after(near_weights, mine)
    tables = (joint_wide, cos_wide, sin_wide, seg, heads)
    near_half = project([after(own, near_gate, near_up, near_down, near_out), near_own], 0, *tables)
    far_own, _ = all_after([far_own, near_half[0]])
    both_own = near(far_own)
    far_out = far(after(output_weight, far_own))
    far_down = far(after(down_weight, far_own))
    x_full, qa, ka, va = project([far_own, both_own], 2, *tables, done=near_half)

    def send(value, j):
        return swap(value[j * block : (j + 1) * block], "tensor", j)

    half = attend(qa, ka, va, 2 * block, 2 * block)
    slices = [half[0][j * block : (j + 1) * block] for j in (2, 3)]
    far_out = after(far_out, half[0])
    ctx_far = [swap(c, "tensor", j) for c, j in zip(slices, (2, 3))]
    both_out = near(far_out)
    ctx, qb = attend(after(qa, far_out, *slices), ka, va, 0, 2 * block, done=half)
    far_mixed, far_down, both_out, *ctx_far = all_after([far_mixed, far_down, both_out, *ctx_far], ctx)
    ctx_parts = [ctx[:block], send(ctx, 1), *ctx_far]
    both_mixed, both_down = near(far_mixed), near(far_down)
    outs = [output_weight, near_out, far_out, both_out]
    sides = lambda a: ((a, 0), (a, 1))
    row = lambda a: a[None, :]

    first_norm, inverse, normed_low = mix(own, ctx_parts, outs, row(attn_gain), row(attn_shift))
    near_rows, far_rows = near(normed_low), far(normed_low)
    first_shards = [
        ((gate_weight, 0), (up_weight, 0), down_weight),
        ((near_gate, 0), (near_up, 0), near_down),
    ]
    gates_a, ups_a, half_way = forward(normed_low, first_shards)
    both_mixed, both_down = all_after([both_mixed, both_down], half_way)
    shards = first_shards + [(*sides(far_mixed), far_down), (*sides(both_mixed), both_down)]
    gates_b, ups_b, encoded, grad_second, grad_low, small = forward(
        normed_low,
        shards[2:],
        (half_way, first_norm, cotangent[0], row(attn_gain), row(attn_shift), row(mlp_gain), row(mlp_shift)),
    )
    near_rows, far_rows = all_after([near_rows, far_rows], grad_low)
    both_rows = near(far_rows)
    near_grads, far_grads = near(grad_low), far(grad_low)
    grad_first, grad_attn_low, grad_ctx = backward(
        after(grad_low, far_rows),
        shards,
        (gates_a, ups_a, gates_b, ups_b),
        grad_second,
        first_norm,
        inverse,
        outs,
        row(attn_gain),
        small,
    )
    near_grads, far_grads, both_rows = all_after([near_grads, far_grads, both_rows], grad_first)
    both_grads = near(far_grads)
    own_ctx, *sent_ctx = [grad_ctx[j] for j in range(group)]
    got_ctx = [swap(g, "tensor", j + 1) for j, g in enumerate(sent_ctx)]
    grad_out = [dot_tn(c, grad_attn_low) for c in ctx_parts]
    both_grads, *grad_out = all_after([both_grads, *grad_out])

    grad_gate, grad_up, grad_down = weight_grads(
        [after(normed_low, *sent_ctx), near_rows, far_rows, both_rows],
        [grad_low, near_grads, far_grads, both_grads],
        gate_weight,
        up_weight,
        down_weight,
    )
    grad_ctx = [own_ctx, *all_after(got_ctx, grad_down)]
    grad_gate = lax.psum(grad_gate, "dp")
    sums = [Sum(grad_up, orders[0]), Sum(grad_down, orders[1])]

    parts, grad_heads = [], []
    for h in range(heads):
        tied = all_after(grad_ctx, *[s.sent for s in sums])
        dq, dkv = attend_back(h, qb, ka, va, tied, ctx, cos_wide, sin_wide)
        part = jnp.concatenate([dq, dkv], axis=1)
        parts.append(part)
        for s in sums:
            s.advance(dq)
        grad_heads.append(dot_tn(part, x_full).astype(bf16))
        if h == 0:
            grad_out = scatter_sum(all_after(grad_out, dq), "tensor").astype(bf16)
            small = sum(g[block:].astype(f32) for g in all_after(grad_ctx, dq))
            small = (small[: SMALL // 2] + small[SMALL // 2 :]).reshape(4, 4, head_width)
            small = small.transpose(1, 0, 2).reshape(4, -1).astype(bf16)
        if h == heads - 2:
            most = jnp.concatenate([grad_out, *grad_heads, small], axis=0)
            sums.append(Sum(jnp.pad(most, ((0, -len(most) % (16 * dp)), (0, 0))), orders[0]))
    sums.append(Sum(grad_heads[-1], orders[1]))
    weights = [query_weight, key_weight, value_weight]
    columns = [
        jnp.concatenate([p[:, n * HEAD_DIM : (n + 1) * HEAD_DIM] for p in parts], axis=1)
        for n in range(3)
    ]
    back = [
        sum(dot_nt(c[j * block : (j + 1) * block], w) for c, w in zip(columns, weights))
        for j in range(group)
    ]
    grad_tokens = grad_first + scatter_sum(back, "tensor")
    while any(s.result is None for s in sums):
        for s in sums:
            s.advance()
    grad_up, grad_down, most, final = (s.result.astype(f32) for s in sums)
    grad_out, small = most[:head_width], most[heads * head_width : heads * head_width + 4]
    joint = jnp.concatenate([most[head_width : heads * head_width], final], axis=0)
    joint = joint.reshape(heads, 3, HEAD_DIM, -1)
    grad_joint = [joint[:, n].reshape(head_width, -1).T for n in range(3)]
    return (
        encoded[None],
        grad_tokens[None],
        *grad_joint,
        grad_out,
        small[0],
        small[1],
        grad_gate.astype(f32),
        grad_up,
        grad_down,
        small[2],
        small[3],
    )


def solution(mesh):
    rows, cols, lead = P("dp", "tensor", None), P(None, "tensor"), P("tensor", None)
    return jax.shard_map(
        local,
        mesh=mesh,
        in_specs=(
            rows, P("dp", None), cols, cols, cols, lead, P(), P(), cols, cols, lead, P(), P(), rows,
        ),
        out_specs=(
            rows, rows, cols, cols, cols, lead, P(), P(), cols, cols, lead, P(), P(),
        ),
        check_vma=False,
    )
```

time: 507 us -> 383 us (0.76)
  waiting for transfers between devices: 217 us -> 85.2 us
  Pallas kernels: 73.2 us -> 137 us
  matrix products: 54.8 us -> 21.5 us
  other arithmetic: 59.5 us -> 33.1 us
  between operations: 3.56 us -> 16 us
  starting transfers between devices: 55.6 us -> 48.2 us
    ppermute x69 -> x53, waiting for transfers between devices: 217 us -> 85.1 us  [swap(): return lax.ppermute(value, axis, [(i, i ^ bit) for i in range(size)])]
    pallas_call x2 -> x9, Pallas kernels: 29.7 us -> 94.2 us  [the longest x2 23.2 us: attend(): pl.pallas_call(functools.partial(attend_kernel, heads), grid=(count // bl...]
    dot_general x4 -> x0, matrix products: 16.6 us -> none  [dot(): return jnp.dot(a, b, preferred_element_type=f32)]
    unnamed x142 -> x124, local copies, waits for them, and re-layouts: 4.84 us -> 18.4 us
    concatenate x6 -> x0, local copies, waits for them, and re-layouts: 11.8 us -> none  [the longest x2 9.98 us: local(): jnp.concatenate([cosine, cosine, blank, -sine, sine, blank] + [blank, APA...]
    dot_general x7 -> x12, matrix products: 23.1 us -> 11.5 us  [dot_nt(): return lax.dot_general(a, b, NT, preferred_element_type=f32)]
    ppermute x69 -> x53, starting transfers between devices: 55.6 us -> 47.9 us  [swap(): return lax.ppermute(value, axis, [(i, i ^ bit) for i in range(size)])]
    concatenate x6 -> x9, other arithmetic: 12.3 us -> 5.7 us  [the longest x2 3.15 us: scatter_sum(): jnp.concatenate(got, axis=0)]
  transfers between devices with their start and end apart: 69 -> 55, of which waited for: 44 -> 18; matrix products, arithmetic and copies ran while one was open for 22% -> 17% of each run, Pallas kernels for 15% -> 36%
where the time goes in v2:
time: 383 us; the launch traced here: 378 us
  Pallas kernels  137 us (36%)
  waiting for transfers between devices  85.2 us (22%)
  starting transfers between devices  48.2 us (13%)
  local copies, waits for them, and re-layouts  36.8 us (10%)
  other arithmetic  33.1 us (9%)
  matrix products  21.5 us (6%)
  between operations  16 us (4%)
    ppermute x53, waiting for transfers between devices, swap(): return lax.ppermute(value, axis, [(i, i ^ bit) for i in range(size)])  85.1 us
    ppermute x53, starting transfers between devices, swap(): return lax.ppermute(value, axis, [(i, i ^ bit) for i in range(size)])  47.9 us
    pallas_call x3, Pallas kernels, attend_back(): pl.pallas_call(functools.partial(attend_back_kernel, head, block_q), grid...  43.1 us
    pallas_call x2, Pallas kernels, attend(): pl.pallas_call(functools.partial(attend_kernel, heads), grid=(count // bl...  23.2 us
    pallas_call x1, Pallas kernels, weight_grads(): pl.pallas_call(weights_kernel, in_specs=[ANY] * 11, out_specs=[ANY] * 3,...  21.1 us
    pallas_call x2, Pallas kernels, forward(): pl.pallas_call(functools.partial(forward_kernel, firsts, bool(last)), in_...  20.3 us
    unnamed x124, local copies, waits for them, and re-layouts  18.4 us
    pallas_call x1, Pallas kernels, backward(): pl.pallas_call(functools.partial(backward_kernel, firsts), in_specs=[IN_V...  15.1 us
  transfers between devices with their start and end apart: 55, of which 18 were waited for; matrix products, arithmetic and copies ran while one was open for 17% of the time, Pallas kernels for 36%

profile of v2, /device:TPU:0, one launch (start us, length us, event | category | flops | bytes accessed | tf_op | source)
XLA Modules:
  0.0 378.0 jit_solution(5415282582378960613)
XLA Ops:
  16.3 4.4 %fusion.7 = (f32[2048,128]{1,0:T(8,128)S(1)}, f32[2048,128]{1,0:T(8,128)S(1)}) fusion(f32[128]{0:T(128)} %constant.60.clone.1, f32[128]{0:T(128)S(1)} %pad_maximum_fusion.13, f32[2048]{0:T(1024)S(1)} %pad_maximum_fusion.12), kind=kLoop, calls=%fused_computation.26 | loop fusion | flops 524288 | bytes 2106368 | tf_op jit(solution)/shard_map/mul | solution.py:741
  36.2 5.6 %project.2 = (bf16[2048,768]{1,0:T(8,128)(2,1)}, bf16[3,2048,128]{2,1,0:T(8,128)(2,1)}, bf16[3,2048,128]{2,1,0:T(8,128)(2,1)}, bf16[3,2048,128]{2,1,0:T(8,128)(2,1)}) custom-call(bf16[512,768]{1,0:T(8,128)(2,1)} %bitcast.refs_0_.own_ref, bf16[512,768]{1,0:T(8,128)(2,1)} %collective-permute-done.6.refs_1_, bf16[768,1152]{1,0:T(8,128)(2,1)} %pad_maximum_fusion.refs_2_, ...), custom_call_target="tpu_custom_call" | custom-call | flops 1811939328 | bytes 4194304 | tf_op jit(solution)/shard_map/project/pallas_call | solution.py:157
  41.8 7.3 %collective-permute-done.refs_0_ = bf16[512,768]{1,0:T(8,128)(2,1)} collective-permute-done((bf16[512,768]{1,0:T(8,128)(2,1)}, bf16[512,768]{1,0:T(8,128)(2,1)}, u32[]{:S(2)}, u32[]{:S(2)}) %collective-permute-start) | collective-permute-done | bytes 786464 | tf_op jit(solution)/shard_map/ppermute | solution.py:39
  51.6 5.4 %project.3 = (bf16[2048,768]{1,0:T(8,128)(2,1)}, bf16[3,2048,128]{2,1,0:T(8,128)(2,1)}, bf16[3,2048,128]{2,1,0:T(8,128)(2,1)}, bf16[3,2048,128]{2,1,0:T(8,128)(2,1)}) custom-call(bf16[512,768]{1,0:T(8,128)(2,1)} %collective-permute-done.refs_0_, ...), custom_call_target="tpu_custom_call", output_to_operand_aliasing={{0}: (6, {}), {1}: (7, {}), {2}: (8, {}), {3}: (9, {})} | custom-call | flops 1811939328 | bytes 4194304 | tf_op jit(solution)/shard_map/project/pallas_call | solution.py:157
  59.9 11.6 %attend.2 = (bf16[2048,192]{1,0:T(8,128)(2,1)S(1)}, bf16[3,2048,128]{2,1,0:T(8,128)(2,1)S(1)}) custom-call(bf16[3,2048,128]{2,1,0:T(8,128)(2,1)S(1)} %copy-done.11, bf16[3,2048,128]{2,1,0:T(8,128)(2,1)S(1)} %copy-done, bf16[3,2048,128]{2,1,0:T(8,128)(2,1)} %get-tuple-element.125.va_ref), custom_call_target="tpu_custom_call" | custom-call | flops 6442450944 | bytes 8388608 | tf_op jit(solution)/shard_map/attend/pallas_call | solution.py:209
  73.6 11.6 %attend.3 = (bf16[2048,192]{1,0:T(8,128)(2,1)S(1)}, bf16[3,2048,128]{2,1,0:T(8,128)(2,1)S(1)}) custom-call(bf16[3,2048,128]{2,1,0:T(8,128)(2,1)S(1)} %copy-done.11, bf16[3,2048,128]{2,1,0:T(8,128)(2,1)S(1)} %copy-done, bf16[3,2048,128]{2,1,0:T(8,128)(2,1)} %get-tuple-element.125.va_ref, ...), custom_call_target="tpu_custom_call", output_to_operand_aliasing={{0}: (3, {}), {1}: (4, {})} | custom-call | flops 6442450944 | bytes 8388608 | tf_op jit(solution)/shard_map/attend/pallas_call | solution.py:209
  90.6 4.1 %collective-permute-done.13.refs_3_ = bf16[512,192]{1,0:T(8,128)(2,1)S(1)} collective-permute-done((bf16[512,192]{1,0:T(8,128)(2,1)S(1)}, bf16[512,192]{1,0:T(8,128)(2,1)S(1)}, u32[]{:S(2)}, u32[]{:S(2)}) %collective-permute-start.13) | collective-permute-done | bytes 196640 | tf_op jit(solution)/shard_map/ppermute | solution.py:39
  97.0 4.4 %collective-permute-done.9.refs_1_ = bf16[512,192]{1,0:T(8,128)(2,1)S(1)} collective-permute-done((bf16[512,192]{1,0:T(8,128)(2,1)S(1)}, bf16[512,192]{1,0:T(8,128)(2,1)S(1)}, u32[]{:S(2)}, u32[]{:S(2)}) %collective-permute-start.9) | collective-permute-done | bytes 196640 | tf_op jit(solution)/shard_map/ppermute | solution.py:39
  114.2 8.9 %feed_forward.2 = (bf16[512,1536]{1,0:T(8,128)(2,1)}, bf16[512,1536]{1,0:T(8,128)(2,1)}, f32[512,768]{1,0:T(8,128)}) custom-call(bf16[512,768]{1,0:T(8,128)(2,1)} %get-tuple-element.156.low_ref.refs_0_, bf16[768,768]{1,0:T(8,128)(2,1)} %refs_8_.1, bf16[768,768]{1,0:T(8,128)(2,1)} %refs_9_.1, bf16[768,768]{1,0:T(8,128)(2,1)S(1)} %copy-done.23, ...), custom_call_target="tpu_custom_call" | custom-call | flops 3623878656 | bytes 12582912 | tf_op jit(solution)/shard_map/feed_forward/pallas_call | solution.py:482
  123.2 11.4 %feed_forward.3 = (bf16[512,1536]{1,0:T(8,128)(2,1)}, bf16[512,1536]{1,0:T(8,128)(2,1)}, bf16[512,768]{1,0:T(8,128)(2,1)}, f32[512,768]{1,0:T(8,128)}, bf16[512,...) custom-call(bf16[512,768]{1,0:T(8,128)(2,1)} %get-tuple-element.156.low_ref.refs_0_, ...), custom_call_target="tpu_custom_call" | custom-call | flops 3623878656 | bytes 12582912 | tf_op jit(solution)/shard_map/feed_forward/pallas_call | solution.py:482
  135.8 15.1 %feed_back.1 = (f32[512,768]{1,0:T(8,128)}, bf16[512,768]{1,0:T(8,128)(2,1)S(1)}, bf16[4,544,192]{2,1,0:T(8,128)(2,1)S(1)}) custom-call(bf16[512,768]{1,0:T(8,128)(2,1)S(1)} %get-tuple-element.145.low2_ref.refs_4_, bf16[768,768]{1,0:T(8,128)(2,1)} %refs_8_.1, bf16[768,768]{1,0:T(8,128)(2,1)} %refs_9_.1, bf16[768,768]{1,0:T(8,128)(2,1)} %refs_10_.1, ...), custom_call_target="tpu_custom_call" | custom-call | flops 7247757312 | bytes 25165824 | tf_op jit(solution)/shard_map/feed_back/pallas_call | solution.py:564
  159.2 21.1 %feed_weights.1 = (bf16[768,768]{1,0:T(8,128)(2,1)}, bf16[768,768]{1,0:T(8,128)(2,1)}, bf16[768,768]{1,0:T(8,128)(2,1)}) custom-call(bf16[512,768]{1,0:T(8,128)(2,1)} %get-tuple-element.156.low_ref.refs_0_, bf16[512,768]{1,0:T(8,128)(2,1)} %collective-permute-done.16.refs_1_, bf16[512,768]{1,0:T(8,128)(2,1)} %collective-permute-done.17.refs_2_, ...), custom_call_target="tpu_custom_call" | custom-call | flops 14495514624 | bytes 16777216 | tf_op jit(solution)/shard_map/feed_weights/pallas_call | solution.py:638
  187.0 14.1 %attend_back.3 = (bf16[2048,64]{1,0:T(8,128)(2,1)S(1)}, bf16[2048,128]{1,0:T(8,128)(2,1)S(1)}) custom-call(bf16[3,2048,128]{2,1,0:T(8,128)(2,1)} %copy-done.1, bf16[3,2048,128]{2,1,0:T(8,128)(2,1)} %get-tuple-element.124.ka_ref, bf16[3,2048,128]{2,1,0:T(8,128)(2,1)} %get-tuple-element.125.va_ref, bf16[544,192]{1,0:T(8,128)(2,1)S(1)} %get-tuple-element.197.refs_0_, ...), custom_call_target="tpu_custom_call" | custom-call | flops 1048576 | bytes 65536 | tf_op jit(solution)/shard_map/attend_back/pallas_call | solution.py:290
  216.3 14.7 %attend_back.4 = (bf16[2048,64]{1,0:T(8,128)(2,1)S(1)}, bf16[2048,128]{1,0:T(8,128)(2,1)S(1)}) custom-call(bf16[3,2048,128]{2,1,0:T(8,128)(2,1)} %copy-done.1, bf16[3,2048,128]{2,1,0:T(8,128)(2,1)} %get-tuple-element.124.ka_ref, bf16[3,2048,128]{2,1,0:T(8,128)(2,1)} %get-tuple-element.125.va_ref, bf16[544,192]{1,0:T(8,128)(2,1)S(1)} %get-tuple-element.197.refs_0_, ...), custom_call_target="tpu_custom_call" | custom-call | flops 1048576 | bytes 65536 | tf_op jit(solution)/shard_map/attend_back/pallas_call | solution.py:290
  232.3 4.3 %collective-permute-done.27 = bf16[192,768]{1,0:T(8,128)(2,1)S(1)} collective-permute-done((bf16[192,768]{1,0:T(8,128)(2,1)S(1)}, bf16[192,768]{1,0:T(8,128)(2,1)S(1)}, u32[]{:S(2)}, u32[]{:S(2)}) %collective-permute-start.27) | collective-permute-done | bytes 294944 | tf_op jit(solution)/shard_map/ppermute | solution.py:39
  238.0 14.3 %attend_back.5 = (bf16[2048,64]{1,0:T(8,128)(2,1)S(1)}, bf16[2048,128]{1,0:T(8,128)(2,1)S(1)}) custom-call(bf16[3,2048,128]{2,1,0:T(8,128)(2,1)} %copy-done.1, bf16[3,2048,128]{2,1,0:T(8,128)(2,1)} %get-tuple-element.124.ka_ref, bf16[3,2048,128]{2,1,0:T(8,128)(2,1)} %get-tuple-element.125.va_ref, bf16[544,192]{1,0:T(8,128)(2,1)S(1)} %get-tuple-element.197.refs_0_, ...), custom_call_target="tpu_custom_call" | custom-call | flops 1048576 | bytes 65536 | tf_op jit(solution)/shard_map/attend_back/pallas_call | solution.py:290
  272.7 5.5 %collective-permute-done.39 = bf16[96,768]{1,0:T(8,128)(2,1)S(1)} collective-permute-done((bf16[96,768]{1,0:T(8,128)(2,1)S(1)}, bf16[96,768]{1,0:T(8,128)(2,1)S(1)}, u32[]{:S(2)}, u32[]{:S(2)}) %collective-permute-start.39) | collective-permute-done | bytes 147488 | tf_op jit(solution)/shard_map/ppermute | solution.py:39
  281.4 8.3 %collective-permute-done.40 = bf16[48,768]{1,0:T(8,128)(2,1)S(1)} collective-permute-done((bf16[48,768]{1,0:T(8,128)(2,1)S(1)}, bf16[48,768]{1,0:T(8,128)(2,1)S(1)}, u32[]{:S(2)}, u32[]{:S(2)}) %collective-permute-start.40) | collective-permute-done | bytes 73760 | tf_op jit(solution)/shard_map/ppermute | solution.py:39
  307.5 7.2 %collective-permute-done.43 = bf16[48,768]{1,0:T(8,128)(2,1)S(1)} collective-permute-done((bf16[48,768]{1,0:T(8,128)(2,1)S(1)}, bf16[48,768]{1,0:T(8,128)(2,1)S(1)}, u32[]{:S(2)}, u32[]{:S(2)}) %collective-permute-start.43) | collective-permute-done | bytes 73760 | tf_op jit(solution)/shard_map/ppermute | solution.py:39
  317.7 4.7 %collective-permute-done.34 = bf16[160,768]{1,0:T(8,128)(2,1)} collective-permute-done((bf16[160,768]{1,0:T(8,128)(2,1)S(1)}, bf16[160,768]{1,0:T(8,128)(2,1)}, u32[]{:S(2)}, u32[]{:S(2)}) %collective-permute-start.34) | collective-permute-done | bytes 245792 | tf_op jit(solution)/shard_map/ppermute | solution.py:39
  326.0 5.5 %collective-permute-done.35 = bf16[80,768]{1,0:T(8,128)(2,1)S(1)} collective-permute-done((bf16[80,768]{1,0:T(8,128)(2,1)S(1)}, bf16[80,768]{1,0:T(8,128)(2,1)S(1)}, u32[]{:S(2)}, u32[]{:S(2)}) %collective-permute-start.35) | collective-permute-done | bytes 122912 | tf_op jit(solution)/shard_map/ppermute | solution.py:39
  331.6 7.9 %collective-permute-done.36 = bf16[80,768]{1,0:T(8,128)(2,1)S(1)} collective-permute-done((bf16[80,768]{1,0:T(8,128)(2,1)S(1)}, bf16[80,768]{1,0:T(8,128)(2,1)S(1)}, u32[]{:S(2)}, u32[]{:S(2)}) %collective-permute-start.36) | collective-permute-done | bytes 122912 | tf_op jit(solution)/shard_map/ppermute | solution.py:39
  344.7 3.8 %collective-permute-done.37 = bf16[160,768]{1,0:T(8,128)(2,1)S(1)} collective-permute-done((bf16[160,768]{1,0:T(8,128)(2,1)S(1)}, bf16[160,768]{1,0:T(8,128)(2,1)S(1)}, u32[]{:S(2)}, u32[]{:S(2)}) %collective-permute-start.37) | collective-permute-done | bytes 245792 | tf_op jit(solution)/shard_map/ppermute | solution.py:39
  351.8 8.5 %collective-permute-done.52 = bf16[384,768]{1,0:T(8,128)(2,1)S(1)} collective-permute-done((bf16[384,768]{1,0:T(8,128)(2,1)S(1)}, bf16[384,768]{1,0:T(8,128)(2,1)S(1)}, u32[]{:S(2)}, u32[]{:S(2)}) %collective-permute-start.52) | collective-permute-done | bytes 589856 | tf_op jit(solution)/shard_map/ppermute | solution.py:39
  (336 shorter events, 152.2 us)
Async XLA Ops:
  7.2 88.9 %all-gather.2.cloned.1.call-start = ((), (), s32[]{:S(2)}) async-start(), calls=%async_computation | async-start | bytes 2654208 | tf_op jit(solution)/shard_map/all_gather | solution.py:746
  21.5 283.2 %all-reduce.4.cloned.1.call-start = ((), (), s32[]{:S(2)}) async-start(), calls=%async_computation.1 | async-start | bytes 2359296 | tf_op jit(solution)/shard_map/psum | solution.py:815
  49.1 22.4 %collective-permute-start.8 = (bf16[192,768]{1,0:T(8,128)(2,1)S(1)}, bf16[192,768]{1,0:T(8,128)(2,1)S(1)}, u32[]{:S(2)}, u32[]{:S(2)}) collective-permute-start(bf16[192,768]{1,0:T(8,128)(2,1)S(1)} %copy-done.12), channel_id=1, source_target_pairs={{0,2},{1,3},{2,0},{3,1},{4,6},{5,7},{6,4},{7,5},{8,10},{9,11},{10,... | collective-permute-start | bytes 884744 | tf_op jit(solution)/shard_map/ppermute | solution.py:39
  50.2 45.9 %collective-permute-start.10 = (bf16[768,768]{1,0:T(8,128)(2,1)S(1)}, bf16[768,768]{1,0:T(8,128)(2,1)}, u32[]{:S(2)}, u32[]{:S(2)}) collective-permute-start(bf16[768,768]{1,0:T(8,128)(2,1)S(1)} %copy-done.22), channel_id=1, source_target_pairs={{0,2},{1,3},{2,0},{3,1},{4,6},{5,7},{6,4},{7,5},{8,10},{9,11},{10,... | collective-permute-start | bytes 3538952 | tf_op jit(solution)/shard_map/ppermute | solution.py:39
  71.5 23.9 %collective-permute-start.11 = (bf16[192,768]{1,0:T(8,128)(2,1)S(1)}, bf16[192,768]{1,0:T(8,128)(2,1)S(1)}, u32[]{:S(2)}, u32[]{:S(2)}) collective-permute-start(bf16[192,768]{1,0:T(8,128)(2,1)S(1)} %collective-permute-done.8.refs_6_.refs_21_), channel_id=1, source_target_pairs={{0,1},{1,0},{2,3},{3,2},{4,5},{5,4},{6,7},{7,6},{8,9},{9,8},{10,11... | collective-permute-start | bytes 884744 | tf_op jit(solution)/shard_map/ppermute | solution.py:39
  72.9 21.8 %collective-permute-start.13 = (bf16[512,192]{1,0:T(8,128)(2,1)S(1)}, bf16[512,192]{1,0:T(8,128)(2,1)S(1)}, u32[]{:S(2)}, u32[]{:S(2)}) collective-permute-start(bf16[512,192]{1,0:T(8,128)(2,1)S(1)} %get-tuple-element.220), channel_id=1, source_target_pairs={{0,3},{1,2},{2,1},{3,0},{4,7},{5,6},{6,5},{7,4},{8,11},{9,10},{10,... | collective-permute-start | bytes 589832 | tf_op jit(solution)/shard_map/ppermute | solution.py:39
  96.1 27.0 %collective-permute-start.14 = (bf16[768,1536]{1,0:T(8,128)(2,1)}, bf16[768,1536]{1,0:T(8,128)(2,1)}, u32[]{:S(2)}, u32[]{:S(2)}) collective-permute-start(bf16[768,1536]{1,0:T(8,128)(2,1)} %all-gather.2.cloned.1.call-done.refs_0_.refs_1_.refs_6_.refs_7_), channel_id=1, source_target_pairs={{0,1},{1,0},{2,3},{3,2},{4,5},{5,4},{6,7},{7,6},{8,9},{9,8},{10,11... | collective-permute-start | bytes 7077896 | tf_op jit(solution)/shard_map/ppermute | solution.py:39
  96.3 26.7 %collective-permute-start.15 = (bf16[768,768]{1,0:T(8,128)(2,1)}, bf16[768,768]{1,0:T(8,128)(2,1)}, u32[]{:S(2)}, u32[]{:S(2)}) collective-permute-start(bf16[768,768]{1,0:T(8,128)(2,1)} %collective-permute-done.10.refs_2_.refs_8_), channel_id=1, source_target_pairs={{0,1},{1,0},{2,3},{3,2},{4,5},{5,4},{6,7},{7,6},{8,9},{9,8},{10,11... | collective-permute-start | bytes 3538952 | tf_op jit(solution)/shard_map/ppermute | solution.py:39
  111.6 24.1 %collective-permute-start.16 = (bf16[512,768]{1,0:T(8,128)(2,1)}, bf16[512,768]{1,0:T(8,128)(2,1)}, u32[]{:S(2)}, u32[]{:S(2)}) collective-permute-start(bf16[512,768]{1,0:T(8,128)(2,1)} %get-tuple-element.156.low_ref.refs_0_), channel_id=1, source_target_pairs={{0,1},{1,0},{2,3},{3,2},{4,5},{5,4},{6,7},{7,6},{8,9},{9,8},{10,11... | collective-permute-start | bytes 2359304 | tf_op jit(solution)/shard_map/ppermute | solution.py:39
  111.8 23.9 %collective-permute-start.17 = (bf16[512,768]{1,0:T(8,128)(2,1)}, bf16[512,768]{1,0:T(8,128)(2,1)}, u32[]{:S(2)}, u32[]{:S(2)}) collective-permute-start(bf16[512,768]{1,0:T(8,128)(2,1)} %get-tuple-element.156.low_ref.refs_0_), channel_id=1, source_target_pairs={{0,2},{1,3},{2,0},{3,1},{4,6},{5,7},{6,4},{7,5},{8,10},{9,11},{10,... | collective-permute-start | bytes 2359304 | tf_op jit(solution)/shard_map/ppermute | solution.py:39
  151.1 29.2 %collective-permute-start.18 = (bf16[544,192]{1,0:T(8,128)(2,1)S(1)}, bf16[544,192]{1,0:T(8,128)(2,1)S(1)}, u32[]{:S(2)}, u32[]{:S(2)}) collective-permute-start(bf16[544,192]{1,0:T(8,128)(2,1)S(1)} %get-tuple-element.216), channel_id=1, source_target_pairs={{0,1},{1,0},{2,3},{3,2},{4,5},{5,4},{6,7},{7,6},{8,9},{9,8},{10,11... | collective-permute-start | bytes 626696 | tf_op jit(solution)/shard_map/ppermute | solution.py:39
  151.5 28.9 %collective-permute-start.19 = (bf16[544,192]{1,0:T(8,128)(2,1)S(1)}, bf16[544,192]{1,0:T(8,128)(2,1)S(1)}, u32[]{:S(2)}, u32[]{:S(2)}) collective-permute-start(bf16[544,192]{1,0:T(8,128)(2,1)S(1)} %get-tuple-element.215), channel_id=1, source_target_pairs={{0,2},{1,3},{2,0},{3,1},{4,6},{5,7},{6,4},{7,5},{8,10},{9,11},{10,... | collective-permute-start | bytes 626696 | tf_op jit(solution)/shard_map/ppermute | solution.py:39
  153.6 26.7 %collective-permute-start.20 = (bf16[544,192]{1,0:T(8,128)(2,1)S(1)}, bf16[544,192]{1,0:T(8,128)(2,1)S(1)}, u32[]{:S(2)}, u32[]{:S(2)}) collective-permute-start(bf16[544,192]{1,0:T(8,128)(2,1)S(1)} %get-tuple-element.214), channel_id=1, source_target_pairs={{0,3},{1,2},{2,1},{3,0},{4,7},{5,6},{6,5},{7,4},{8,11},{9,10},{10,... | collective-permute-start | bytes 626696 | tf_op jit(solution)/shard_map/ppermute | solution.py:39
  183.0 25.5 %collective-permute-start.26 = (bf16[384,768]{1,0:T(8,128)(2,1)}, bf16[384,768]{1,0:T(8,128)(2,1)}, u32[]{:S(2)}, u32[]{:S(2)}) collective-permute-start(bf16[384,768]{1,0:T(8,128)(2,1)} %constant_dynamic-slice_fusion.10), channel_id=1, source_target_pairs={{0,8},{4,12},{8,0},{12,4},{16,24},{20,28},{24,16},{28,20},{1,9},{5... | collective-permute-start | bytes 1769480 | tf_op jit(solution)/shard_map/ppermute | solution.py:39
  185.5 23.0 %collective-permute-start.25 = (bf16[384,768]{1,0:T(8,128)(2,1)}, bf16[384,768]{1,0:T(8,128)(2,1)}, u32[]{:S(2)}, u32[]{:S(2)}) collective-permute-start(bf16[384,768]{1,0:T(8,128)(2,1)} %constant_dynamic-slice_fusion.11), channel_id=1, source_target_pairs={{0,4},{4,0},{8,12},{12,8},{16,20},{20,16},{24,28},{28,24},{1,5},{5... | collective-permute-start | bytes 1769480 | tf_op jit(solution)/shard_map/ppermute | solution.py:39
  211.5 25.1 %collective-permute-start.27 = (bf16[192,768]{1,0:T(8,128)(2,1)S(1)}, bf16[192,768]{1,0:T(8,128)(2,1)S(1)}, u32[]{:S(2)}, u32[]{:S(2)}) collective-permute-start(bf16[192,768]{1,0:T(8,128)(2,1)S(1)} %get-tuple-element.243), channel_id=1, source_target_pairs={{0,8},{4,12},{8,0},{12,4},{16,24},{20,28},{24,16},{28,20},{1,9},{5... | collective-permute-start | bytes 884744 | tf_op jit(solution)/shard_map/ppermute | solution.py:39
  211.9 24.7 %collective-permute-start.28 = (bf16[192,768]{1,0:T(8,128)(2,1)S(1)}, bf16[192,768]{1,0:T(8,128)(2,1)S(1)}, u32[]{:S(2)}, u32[]{:S(2)}) collective-permute-start(bf16[192,768]{1,0:T(8,128)(2,1)S(1)} %get-tuple-element.242), channel_id=1, source_target_pairs={{0,16},{4,20},{8,24},{12,28},{16,0},{20,4},{24,8},{28,12},{1,17},{... | collective-permute-start | bytes 884744 | tf_op jit(solution)/shard_map/ppermute | solution.py:39
  215.4 21.4 %collective-permute-start.30 = (bf16[192,768]{1,0:T(8,128)(2,1)S(1)}, bf16[192,768]{1,0:T(8,128)(2,1)S(1)}, u32[]{:S(2)}, u32[]{:S(2)}) collective-permute-start(bf16[192,768]{1,0:T(8,128)(2,1)S(1)} %add_convert_fusion.7), channel_id=1, source_target_pairs={{0,2},{1,3},{2,0},{3,1},{4,6},{5,7},{6,4},{7,5},{8,10},{9,11},{10,... | collective-permute-start | bytes 884744 | tf_op jit(solution)/shard_map/ppermute | solution.py:39
  261.5 37.7 %collective-permute-start.33 = (bf16[320,768]{1,0:T(8,128)(2,1)S(1)}, bf16[320,768]{1,0:T(8,128)(2,1)S(1)}, u32[]{:S(2)}, u32[]{:S(2)}) collective-permute-start(bf16[320,768]{1,0:T(8,128)(2,1)S(1)} %constant_dynamic-slice_fusion.5), channel_id=1, source_target_pairs={{0,4},{4,0},{8,12},{12,8},{16,20},{20,16},{24,28},{28,24},{1,5},{5... | collective-permute-start | bytes 1474568 | tf_op jit(solution)/shard_map/ppermute | solution.py:39
  268.9 79.9 %collective-permute-start.31 = (bf16[1024,768]{1,0:T(8,128)(2,1)}, bf16[1024,768]{1,0:T(8,128)(2,1)}, u32[]{:S(2)}, u32[]{:S(2)}) collective-permute-start(bf16[1024,768]{1,0:T(8,128)(2,1)} %pad_maximum_fusion.2), channel_id=1, source_target_pairs={{0,1},{1,0},{2,3},{3,2},{4,5},{5,4},{6,7},{7,6},{8,9},{9,8},{10,11... | collective-permute-start | bytes 4718600 | tf_op jit(solution)/shard_map/ppermute | solution.py:39
  278.6 20.6 %collective-permute-start.46 = (bf16[96,768]{1,0:T(8,128)(2,1)S(1)}, bf16[96,768]{1,0:T(8,128)(2,1)S(1)}, u32[]{:S(2)}, u32[]{:S(2)}) collective-permute-start(bf16[96,768]{1,0:T(8,128)(2,1)S(1)} %add_convert_fusion.12), channel_id=1, source_target_pairs={{0,16},{4,20},{8,24},{12,28},{16,0},{20,4},{24,8},{28,12},{1,17},{... | collective-permute-start | bytes 442376 | tf_op jit(solution)/shard_map/ppermute | solution.py:39
  299.2 24.3 %collective-permute-start.47 = (bf16[192,768]{1,0:T(8,128)(2,1)S(1)}, bf16[192,768]{1,0:T(8,128)(2,1)S(1)}, u32[]{:S(2)}, u32[]{:S(2)}) collective-permute-start(bf16[192,768]{1,0:T(8,128)(2,1)S(1)} %maximum_select_fusion.7), channel_id=1, source_target_pairs={{0,8},{4,12},{8,0},{12,4},{16,24},{20,28},{24,16},{28,20},{1,9},{5... | collective-permute-start | bytes 884744 | tf_op jit(solution)/shard_map/ppermute | solution.py:39
  299.4 23.0 %collective-permute-start.34 = (bf16[160,768]{1,0:T(8,128)(2,1)S(1)}, bf16[160,768]{1,0:T(8,128)(2,1)}, u32[]{:S(2)}, u32[]{:S(2)}) collective-permute-start(bf16[160,768]{1,0:T(8,128)(2,1)S(1)} %constant_dynamic-slice_fusion.4), channel_id=1, source_target_pairs={{0,8},{4,12},{8,0},{12,4},{16,24},{20,28},{24,16},{28,20},{1,9},{5... | collective-permute-start | bytes 737288 | tf_op jit(solution)/shard_map/ppermute | solution.py:39
  302.2 37.6 %collective-permute-start.51 = (bf16[192,768]{1,0:T(8,128)(2,1)S(1)}, bf16[192,768]{1,0:T(8,128)(2,1)}, u32[]{:S(2)}, u32[]{:S(2)}) collective-permute-start(bf16[192,768]{1,0:T(8,128)(2,1)S(1)} %maximum_select_fusion.8), channel_id=1, source_target_pairs={{0,16},{4,20},{8,24},{12,28},{16,0},{20,4},{24,8},{28,12},{1,17},{... | collective-permute-start | bytes 884744 | tf_op jit(solution)/shard_map/ppermute | solution.py:39
  (93 other events, 793.5 us)
Sparse Core Ops, SparseCore 0:
  21.6 52.8 all-gather.1
  205.0 98.3 all-reduce.3

commit v3 on v2

v3 whole, which is shorter than its diff:
```python
import functools
import math

import jax
import jax.numpy as jnp
from jax import lax
from jax.experimental import pallas as pl
from jax.experimental.pallas import tpu as pltpu
from jax.sharding import PartitionSpec as P

HEAD_DIM = 64
EPSILON = 1e-05
ROPE_BASE = 1000.0
APART = -(2.0**30)
WIDE = 128
SEGMENTS = 7
SEG_AT = HEAD_DIM
ROW_AT = HEAD_DIM + 8
VMEM = 60 * 2**20
VMEM_LESS = 44 * 2**20
SMALL_COST = pl.CostEstimate(flops=2**20, bytes_accessed=2**16, transcendentals=0)
bf16 = jnp.bfloat16
f32 = jnp.float32
NT = (((1,), (1,)), ((), ()))
TN = (((0,), (0,)), ((), ()))


def dot(a, b):
    return jnp.dot(a, b, preferred_element_type=f32)


def dot_nt(a, b):
    return lax.dot_general(a, b, NT, preferred_element_type=f32)


def dot_tn(a, b):
    return lax.dot_general(a, b, TN, preferred_element_type=f32)


def swap(value, axis, bit):
    size = lax.axis_size(axis)
    return lax.ppermute(value, axis, [(i, i ^ bit) for i in range(size)])


def after(value, *others):
    return lax.optimization_barrier((value, *others))[0]


def all_after(values, *others):
    return list(lax.optimization_barrier((tuple(values), others))[0])


def scatter_sum(blocks, axis):
    held = dict(enumerate(blocks))
    rows = blocks[0].shape[0]
    step = 1
    while step < len(blocks):
        sent = [k for k in held if k & step]
        got = [held.pop(k).astype(bf16) for k in sent]
        got = swap(got[0] if len(got) == 1 else jnp.concatenate(got, axis=0), axis, step)
        for n, k in enumerate(sent):
            held[k ^ step] = held[k ^ step] + got[n * rows : (n + 1) * rows].astype(f32)
        step *= 2
    return held[0]


def peers(axis, bits):
    me = lax.axis_index(axis)
    mine = sum(((me >> bit) & 1) << n for n, bit in enumerate(bits))
    far = [sum(((j >> n) & 1) << bit for n, bit in enumerate(bits)) for j in range(1 << len(bits))]
    return mine, far


def split_rows(value, axis, bits):
    mine, far = peers(axis, bits)
    rows = value.shape[0] // len(far)
    return [lax.dynamic_slice_in_dim(value, (mine ^ j) * rows, rows, 0) for j in range(len(far))]


def join_rows(parts, axis, bits):
    mine, _ = peers(axis, bits)

    def pick(p):
        value = parts[-1]
        for j in reversed(range(len(parts) - 1)):
            value = jnp.where(mine == p ^ j, parts[j], value)
        return value

    return jnp.concatenate([pick(p) for p in range(len(parts))], axis=0)


def sum_steps(parts, axis, groups):
    for n, bits in enumerate(groups):
        if n:
            parts = split_rows(value, axis, bits)
        _, far = peers(axis, bits)
        got = yield parts[1:], [swap(part, axis, step) for part, step in zip(parts[1:], far[1:])]
        value = sum((g.astype(f32) for g in got), parts[0].astype(f32)).astype(bf16)
    for bits in reversed(groups):
        _, far = peers(axis, bits)
        got = yield [value], [swap(value, axis, step) for step in far[1:]]
        value = join_rows([value, *got], axis, bits)
    return value


class Sum:
    def __init__(self, parts, groups):
        self.steps = sum_steps(parts, "dp", groups)
        self.result = None
        self.sent, self.got = next(self.steps)

    def take(self, got):
        if self.result is None:
            try:
                self.sent, self.got = self.steps.send(got)
            except StopIteration as end:
                self.result, self.sent, self.got = end.value, [], []


def take_round(sums, *others):
    got, others = lax.optimization_barrier(([s.got for s in sums], others))
    for s, g in zip(sums, got):
        s.take(g)
    return list(others)


def swap_halves(value, lane):
    half = HEAD_DIM // 2
    return jnp.where(
        lane < half, pltpu.roll(value, WIDE - half, 1), pltpu.roll(value, half, 1)
    )


def project_kernel(heads, start, count, me_ref, *refs):
    pieces, refs = refs[:count], refs[count:]
    weights, (seg_ref, rate_ref) = refs[:3], refs[3:5]
    x_ref, qa_ref, ka_ref, va_ref, cos_ref, sin_ref = refs[-6:]
    rows = x_ref.shape[0]
    step = pl.program_id(0)
    for n, piece in enumerate(pieces):

        @pl.when(step == n)
        def _(piece=piece):
            x_ref[...] = piece[...]

    x = x_ref[...]
    query, key, value = (dot_nt(x, w[...]) for w in weights)

    segs = seg_ref[...]
    order = jnp.where(segs < 0, SEGMENTS - 1, segs)
    first_place = jnp.zeros_like(order)
    for s in range(1, SEGMENTS):
        before = jnp.sum((order < s).astype(jnp.int32), axis=1, keepdims=True)
        first_place = jnp.where(order == s, before, first_place)
    places = lax.broadcasted_iota(jnp.int32, segs.shape, 1) - first_place

    def column(values):
        mine = me_ref[0] ^ (start + step)
        block = values[:, -rows:]
        for n in range(values.shape[1] // rows - 1):
            block = jnp.where(mine == n, values[:, n * rows : (n + 1) * rows], block)
        return jnp.broadcast_to(block.astype(f32), (WIDE, rows)).T

    angles = column(places) * rate_ref[...]
    seg = column(segs).astype(jnp.int32)
    lane = lax.broadcasted_iota(jnp.int32, (rows, WIDE), 1)
    cosine, sine = jnp.cos(angles), jnp.sin(angles)
    sine = jnp.where(lane < HEAD_DIM // 2, -sine, sine)
    cos_ref[...], sin_ref[...] = cosine, sine
    first = lane < HEAD_DIM
    same = lane == seg + (SEG_AT + 1)
    qf = jnp.where(same, APART, 0.0)
    kf = jnp.where((lane < ROW_AT + 3) & ~same, 1.0, 0.0)
    ones = jnp.where(lane < HEAD_DIM + 3, 1.0, 0.0)

    def part(values, h):
        at = h * HEAD_DIM
        if h % 2:
            return pltpu.roll(values[:, at - HEAD_DIM : at + HEAD_DIM], HEAD_DIM, 1)
        if h + 1 < heads:
            return values[:, at : at + WIDE]
        here = values[:, at : at + HEAD_DIM]
        return jnp.concatenate([here, jnp.zeros_like(here)], axis=1)

    for h in range(heads):
        q, k = part(query, h), part(key, h)
        q = q * cosine + swap_halves(q, lane) * sine
        k = k * cosine + swap_halves(k, lane) * sine
        qa_ref[h] = jnp.where(first, q * (1.0 / math.sqrt(HEAD_DIM)), qf).astype(bf16)
        ka_ref[h] = jnp.where(first, k, kf).astype(bf16)
        va_ref[h] = jnp.where(first, part(value, h), ones).astype(bf16)


def project(pieces, start, weights, segments, rates, heads, done=()):
    block, width = pieces[0].shape
    length = segments.shape[1]
    rows = lambda n: pl.BlockSpec((block, n), lambda i: (start + i, 0))
    whole = lambda a: pl.BlockSpec(a.shape, lambda i: (0, 0))
    out = pl.BlockSpec((heads, block, WIDE), lambda i: (0, start + i, 0))
    given = 1 + len(pieces) + 5
    me = lax.axis_index("tensor").astype(jnp.int32)[None]
    return pl.pallas_call(
        functools.partial(project_kernel, heads, start, len(pieces)),
        grid=(len(pieces),),
        in_specs=[pl.BlockSpec(memory_space=pltpu.SMEM)]
        + [whole(p) for p in pieces]
        + [whole(w) for w in weights]
        + [whole(segments), whole(rates)]
        + [pl.BlockSpec(memory_space=pl.ANY)] * len(done),
        out_specs=[rows(width)] + [out] * 3 + [rows(WIDE)] * 2,
        out_shape=[jax.ShapeDtypeStruct((length, width), bf16)]
        + [jax.ShapeDtypeStruct((heads, length, WIDE), bf16)] * 3
        + [jax.ShapeDtypeStruct((length, WIDE), f32)] * 2,
        input_output_aliases={given + n: n for n in range(len(done))},
        compiler_params=pltpu.CompilerParams(vmem_limit_bytes=VMEM),
        cost_estimate=SMALL_COST,
        name="project",
    )(me, *pieces, *weights, segments, rates, *done)


def split3(value):
    high = value.astype(bf16).astype(f32)
    rest = value - high
    middle = rest.astype(bf16).astype(f32)
    return high, middle, rest - middle


def put_row(wide, at, value):
    lane = lax.broadcasted_iota(jnp.int32, wide.shape, 1)
    for n, part in enumerate(split3(value)):
        wide = jnp.where(lane == at + n, -part, wide)
    return wide


def attend_kernel(heads, qa_ref, ka_ref, va_ref, *refs):
    ctx_ref, qb_ref = refs[-2:]
    parts = []
    for h in range(heads):
        qa = qa_ref[h]
        scores = dot_nt(qa, ka_ref[h])
        peak = jnp.max(scores, axis=1, keepdims=True)
        weights = jnp.exp(scores - peak).astype(bf16)
        summed = dot(weights, va_ref[h])
        total = summed[:, HEAD_DIM : HEAD_DIM + 1]
        parts.append(summed[:, :HEAD_DIM] / total)
        qb_ref[h] = put_row(qa.astype(f32), ROW_AT, peak + jnp.log(total)).astype(bf16)
    ctx_ref[...] = jnp.concatenate(parts, axis=1).astype(bf16)


def attend(qa, ka, va, start, count, done=(), block=256):
    heads, length, _ = qa.shape
    first = start // block
    whole = pl.BlockSpec((heads, length, WIDE), lambda i: (0, 0, 0))
    part = pl.BlockSpec((heads, block, WIDE), lambda i: (0, first + i, 0))
    return pl.pallas_call(
        functools.partial(attend_kernel, heads),
        grid=(count // block,),
        in_specs=[part, whole, whole] + [pl.BlockSpec(memory_space=pl.ANY)] * len(done),
        out_specs=[pl.BlockSpec((block, heads * HEAD_DIM), lambda i: (first + i, 0)), part],
        out_shape=[
            jax.ShapeDtypeStruct((length, heads * HEAD_DIM), bf16),
            jax.ShapeDtypeStruct((heads, length, WIDE), bf16),
        ],
        input_output_aliases={3 + n: n for n in range(len(done))},
        compiler_params=pltpu.CompilerParams(vmem_limit_bytes=VMEM_LESS),
        cost_estimate=SMALL_COST,
        name="attend",
    )(qa, ka, va, *done)


def attend_back_kernel(heads, qb_ref, ka_ref, va_ref, *refs):
    gos, refs = refs[:4], refs[4:]
    ctx_ref, cos_ref, sin_ref, dq_ref, dk_ref, dv_ref, doa, dqt = refs
    j, h = pl.program_id(0), pl.program_id(1)
    length = qb_ref.shape[1]
    block = length // 4
    at = [pl.ds(i * block, block) for i in range(4)]

    for head in range(heads):
        cols = pl.ds(head * HEAD_DIM, HEAD_DIM)

        @pl.when((j == 0) & (h == head))
        def _(cols=cols):
            for i in range(4):
                go = gos[i][:block, cols].astype(f32)
                delta = jnp.sum(go * ctx_ref[at[i], cols].astype(f32), axis=1, keepdims=True)
                wide = jnp.concatenate([go, jnp.zeros_like(go)], axis=1)
                doa[h, at[i], :] = put_row(wide, HEAD_DIM, delta).astype(bf16)

    @pl.when(j == 0)
    def _():
        dqt[h] = jnp.zeros(dqt.shape[1:], f32)

    ka, va = ka_ref[h], va_ref[h]
    kt = ka.astype(f32).T[:HEAD_DIM].astype(bf16)
    dk = dv = None
    for i in range(4):
        qb, do = qb_ref[h, at[i], :], doa[h, at[i], :]
        weights = jnp.exp(dot_nt(ka, qb))
        grads = (weights * dot_nt(va, do)).astype(bf16)
        v_part = dot(weights.astype(bf16), do)
        k_part = dot(grads, qb)
        dk = k_part if i == 0 else dk + k_part
        dv = v_part if i == 0 else dv + v_part
        dqt[h, :, at[i]] += dot(kt, grads)
    lane = lax.broadcasted_iota(jnp.int32, dk.shape, 1)
    rows = pl.ds(pl.multiple_of(j * ka.shape[0], ka.shape[0]), ka.shape[0])
    dk = dk * cos_ref[rows, :] - swap_halves(dk, lane) * sin_ref[rows, :]
    for head in range(heads):
        cols = pl.ds(head * HEAD_DIM, HEAD_DIM)

        @pl.when(h == head)
        def _(cols=cols):
            dk_ref[:, cols] = dk[:, :HEAD_DIM].astype(bf16)
            dv_ref[:, cols] = dv[:, :HEAD_DIM].astype(bf16)

        @pl.when((h == head) & (j == pl.num_programs(0) - 1))
        def _(cols=cols):
            for i in range(4):
                part = dqt[h, :, at[i]]
                dq = jnp.concatenate([part, jnp.zeros_like(part)], axis=0).T
                lanes = lax.broadcasted_iota(jnp.int32, dq.shape, 1)
                dq = dq * cos_ref[at[i], :] - swap_halves(dq, lanes) * sin_ref[at[i], :]
                dq_ref[at[i], cols] = (dq[:, :HEAD_DIM] * (1.0 / math.sqrt(HEAD_DIM))).astype(bf16)


def attend_back(qb, ka, va, gos, ctx, cosine, sine, block_k=512):
    heads, length, _ = qb.shape
    part = pl.BlockSpec((heads, block_k, WIDE), lambda j, h: (0, j, 0))
    full = lambda a: pl.BlockSpec(a.shape, lambda j, h, r=len(a.shape): (0,) * r)
    grad = jax.ShapeDtypeStruct((length, heads * HEAD_DIM), bf16)
    rows = pl.BlockSpec((block_k, heads * HEAD_DIM), lambda j, h: (j, 0))
    return pl.pallas_call(
        functools.partial(attend_back_kernel, heads),
        grid=(length // block_k, heads),
        in_specs=[full(qb), part, part] + [full(a) for a in (*gos, ctx, cosine, sine)],
        out_specs=[full(grad), rows, rows],
        out_shape=[grad] * 3,
        scratch_shapes=[pltpu.VMEM((heads, length, WIDE), bf16), pltpu.VMEM((heads, HEAD_DIM, length), f32)],
        compiler_params=pltpu.CompilerParams(vmem_limit_bytes=VMEM),
        cost_estimate=SMALL_COST,
        name="attend_back",
    )(qb, ka, va, *gos, ctx, cosine, sine)


ANY = pl.BlockSpec(memory_space=pl.ANY)
IN_VMEM = pl.BlockSpec(memory_space=pltpu.VMEM)


def start(source, target, sem):
    copy = pltpu.make_async_copy(source, target, sem)
    copy.start()
    return copy


def norm_parts(row_values):
    centred = row_values - jnp.mean(row_values, axis=-1, keepdims=True)
    inverse = lax.rsqrt(jnp.mean(centred * centred, axis=-1, keepdims=True) + EPSILON)
    return (centred * inverse, inverse)


def norm_back(grad_norm, normalized, inverse):
    return inverse * (
        grad_norm
        - jnp.mean(grad_norm, axis=-1, keepdims=True)
        - normalized * jnp.mean(grad_norm * normalized, axis=-1, keepdims=True)
    )


def mix_kernel(own_ref, *refs):
    parts, outs, refs = refs[:4], refs[4:8], refs[8:]
    gain_ref, shift_ref, norm_ref, inverse_ref, low_ref = refs
    total = own_ref[...].astype(f32)
    for part, out in zip(parts, outs):
        total = total + dot(part[...], out[...])
    norm, inverse = norm_parts(total)
    norm_ref[...] = norm
    inverse_ref[...] = jnp.broadcast_to(inverse, inverse_ref.shape)
    low_ref[...] = (norm * gain_ref[...] + shift_ref[...]).astype(bf16)


def mix(own, parts, outs, gain, shift, block=256):
    length, width = own.shape
    rows = lambda a: pl.BlockSpec((block, a.shape[1]), lambda i: (i, 0))
    whole = lambda a: pl.BlockSpec(a.shape, lambda i: (0, 0))
    shapes = [
        jax.ShapeDtypeStruct((length, width), f32),
        jax.ShapeDtypeStruct((length, WIDE), f32),
        jax.ShapeDtypeStruct((length, width), bf16),
    ]
    return pl.pallas_call(
        mix_kernel,
        grid=(length // block,),
        in_specs=[rows(own)] + [rows(p) for p in parts] + [whole(w) for w in outs] + [whole(gain), whole(shift)],
        out_specs=[rows(s) for s in shapes],
        out_shape=shapes,
        compiler_params=pltpu.CompilerParams(vmem_limit_bytes=VMEM),
        cost_estimate=SMALL_COST,
        name="mix",
    )(own, *parts, *outs, gain, shift)


def sigmoid(value):
    return 0.5 * jnp.tanh(0.5 * value) + 0.5


def feed(low, gate, up):
    gate_pre, up_pre = dot(low, gate), dot(low, up)
    return gate_pre, up_pre


def hidden_of(gate_pre, up_pre):
    return (gate_pre * sigmoid(gate_pre) * up_pre).astype(bf16)


def feed_back(grad_hidden, gate_pre, up_pre):
    part = sigmoid(gate_pre)
    active = gate_pre * part
    grad_gate = grad_hidden * up_pre * (part + active * (1.0 - part))
    return grad_gate.astype(bf16), (grad_hidden * active).astype(bf16)


def shard_copies(n, firsts, shards, buffers, sem):
    copies = []
    for k, buffer in enumerate(buffers):
        width = buffer.shape[2]
        source = shards[3 * n + k].at[:, pl.ds(firsts[3 * n + k] * width, width)]
        copies.append(start(source, buffer.at[n], sem.at[n, k]))
    return copies


def shard_args(shards):
    return [a for shard in shards for a, _ in shard], [first for shard in shards for _, first in shard]


HALVES = 2


def halves(length):
    return [pl.ds(n * (length // HALVES), length // HALVES) for n in range(HALVES)]


def forward_kernel(firsts, last, low_ref, *refs):
    count = len(firsts) // 3
    shards, refs = refs[: 3 * count], refs[3 * count :]
    if last:
        first_ref, then_ref, norm_ref, cot_ref, gain_ref, shift_ref, gain2_ref, shift2_ref = refs[:8]
        gates_ref, ups_ref, encoded_ref, second_ref, low2_ref, small_ref = refs[8:14]
        gate, up, down, gates, ups, sem, out_sem, total, before, then, norm1, cot_in, more_sem = refs[14:]
    else:
        gates_ref, ups_ref, total, gate, up, down, gates, ups, sem, out_sem = refs
    buffers = (gate, up, down)
    coming = [shard_copies(0, firsts, shards, buffers, sem)]
    if last:
        extra = [
            start(ref, buffer, more_sem.at[n])
            for n, (ref, buffer) in enumerate(
                [(first_ref, before), (then_ref, then), (norm_ref, norm1), (cot_ref, cot_in)]
            )
        ]
    going = []
    hidden = down.shape[1]
    for n in range(count):
        if n + 1 < count:
            coming.append(shard_copies(n + 1, firsts, shards, buffers, sem))
        for copy in coming[n]:
            copy.wait()
        for at in halves(low_ref.shape[0]):
            gate_pre, up_pre = feed(low_ref[at, :], gate[n], up[n])
            gates[n, at, :] = gate_pre.astype(bf16)
            ups[n, at, :] = up_pre.astype(bf16)
            part = dot(hidden_of(gate_pre, up_pre), down[n])
            total[at, :] = part if n == 0 else total[at, :] + part
        cols = pl.ds(n * hidden, hidden)
        going.append(start(gates.at[n], gates_ref.at[:, cols], out_sem.at[n, 0]))
        going.append(start(ups.at[n], ups_ref.at[:, cols], out_sem.at[n, 1]))
    if last:
        for copy in extra:
            copy.wait()
        normed = norm1[...] * gain_ref[...] + shift_ref[...]
        norm, inverse = norm_parts(normed + (before[...] + then[...] + total[...]))
        cot = cot_in[...].astype(f32)
        encoded_ref[...] = (norm * gain2_ref[...] + shift2_ref[...]).astype(bf16)
        second = norm_back(cot * gain2_ref[...], norm, inverse)
        second_ref[...] = second
        low2_ref[...] = second.astype(bf16)
        small_ref[...] = jnp.concatenate(
            [jnp.sum(cot * norm, axis=0, keepdims=True), jnp.sum(cot, axis=0, keepdims=True)], axis=0
        )
    for copy in going:
        copy.wait()


def forward(low, shards, last=()):
    length, width = low.shape
    count, hidden = len(shards), shards[0][2][0].shape[0]
    args, firsts = shard_args(shards)
    shapes = [jax.ShapeDtypeStruct((length, hidden * count), bf16)] * 2
    out_specs = [ANY, ANY]
    scratch = [
        pltpu.VMEM((count, width, hidden), bf16),
        pltpu.VMEM((count, width, hidden), bf16),
        pltpu.VMEM((count, hidden, width), bf16),
        pltpu.VMEM((count, length, hidden), bf16),
        pltpu.VMEM((count, length, hidden), bf16),
        pltpu.SemaphoreType.DMA((count, 3)),
        pltpu.SemaphoreType.DMA((count, 2)),
    ]
    if last:
        shapes += [
            jax.ShapeDtypeStruct((length, width), bf16),
            jax.ShapeDtypeStruct((length, width), f32),
            jax.ShapeDtypeStruct((length, width), bf16),
            jax.ShapeDtypeStruct((2, width), f32),
        ]
        out_specs += [IN_VMEM] * 4
        wide = pltpu.VMEM((length, width), f32)
        scratch += [wide] * 4 + [pltpu.VMEM((length, width), bf16), pltpu.SemaphoreType.DMA((4,))]
    else:
        shapes.append(jax.ShapeDtypeStruct((length, width), f32))
        out_specs.append(IN_VMEM)
    return pl.pallas_call(
        functools.partial(forward_kernel, firsts, bool(last)),
        in_specs=[IN_VMEM] + [ANY] * len(args) + [ANY] * len(last[:4]) + [IN_VMEM] * len(last[4:]),
        out_specs=out_specs,
        out_shape=shapes,
        scratch_shapes=scratch,
        compiler_params=pltpu.CompilerParams(vmem_limit_bytes=VMEM),
        cost_estimate=SMALL_COST,
        name="feed_forward",
    )(low, *args, *last)


def backward_kernel(firsts, where, low2_ref, *refs):
    count = len(firsts) // 3
    shards, refs = refs[: 3 * count], refs[3 * count :]
    pairs = where[-1][0] + 1
    saved, refs = refs[: 2 * pairs], refs[2 * pairs :]
    late_refs, refs = refs[:7], refs[7:]
    gain_ref, small_in_ref, first_ref, low_ref, *ctx_refs = refs[:8]
    gate, up, down, gates, ups, total, second, norm1, inverse, outs, sem, saved_sem, late_sem = refs[8:]
    buffers = (gate, up, down)
    hidden = down.shape[1]

    def fetch(n):
        part, cols = where[n][0], pl.ds(where[n][1] * hidden, hidden)
        return shard_copies(n, firsts, shards, buffers, sem) + [
            start(ref.at[:, cols], buffer.at[n], saved_sem.at[n, k])
            for k, (ref, buffer) in enumerate(zip(saved[2 * part : 2 * part + 2], (gates, ups)))
        ]

    coming = [fetch(0)]
    late = []
    for n in range(count):
        if n + 1 < count:
            coming.append(fetch(n + 1))
        else:
            targets = [second, norm1, inverse] + [outs.at[k] for k in range(4)]
            late = [start(ref, target, late_sem.at[k]) for k, (ref, target) in enumerate(zip(late_refs, targets))]
        for copy in coming[n]:
            copy.wait()
        for at in halves(low2_ref.shape[0]):
            grad_hidden = dot_nt(low2_ref[at, :], down[n])
            grad_gate, grad_up = feed_back(grad_hidden, gates[n, at, :].astype(f32), ups[n, at, :].astype(f32))
            part = dot_nt(grad_gate, gate[n]) + dot_nt(grad_up, up[n])
            total[at, :] = part if n == 0 else total[at, :] + part
    for copy in late:
        copy.wait()
    normed_grad, norm = second[...] + total[...], norm1[...]
    first = norm_back(normed_grad * gain_ref[...], norm, inverse[:, :1])
    first_ref[...] = first
    low = first.astype(bf16)
    low_ref[...] = low
    small = jnp.concatenate(
        [
            jnp.sum(normed_grad * norm, axis=0, keepdims=True),
            jnp.sum(normed_grad, axis=0, keepdims=True),
            small_in_ref[...],
        ],
        axis=0,
    )
    width = outs.shape[1]
    small = jnp.concatenate([small[:, k * width : (k + 1) * width] for k in range(4)], axis=0)
    high = small.astype(bf16)
    small = jnp.concatenate([high, (small - high.astype(f32)).astype(bf16)], axis=0)
    length = low.shape[0]
    for k in range(4):
        ctx_refs[k][:length, :] = dot_nt(low, outs[k]).astype(bf16)
        ctx_refs[k][length:, :] = small


SMALL = 32


def backward(low2, shards, saved, second, norm, inverse, outs, gain, small):
    length, width = low2.shape
    count, hidden = len(shards), shards[0][2][0].shape[0]
    args, firsts = shard_args(shards)
    where = [(n, k) for n, (gates, _) in enumerate(saved) for k in range(gates.shape[1] // hidden)]
    saved = [a for pair in saved for a in pair]
    late = [second, norm, inverse, *outs]
    wide = pltpu.VMEM((length, width), f32)
    return pl.pallas_call(
        functools.partial(backward_kernel, firsts, where),
        in_specs=[IN_VMEM] + [ANY] * (len(args) + len(saved) + len(late)) + [IN_VMEM] * 2,
        out_specs=[IN_VMEM] * 6,
        out_shape=[
            jax.ShapeDtypeStruct((length, width), f32),
            jax.ShapeDtypeStruct((length, width), bf16),
        ]
        + [jax.ShapeDtypeStruct((length + SMALL, outs[0].shape[0]), bf16)] * 4,
        scratch_shapes=[
            pltpu.VMEM((count, width, hidden), bf16),
            pltpu.VMEM((count, width, hidden), bf16),
            pltpu.VMEM((count, hidden, width), bf16),
            pltpu.VMEM((count, length, hidden), bf16),
            pltpu.VMEM((count, length, hidden), bf16),
            wide,
            wide,
            wide,
            pltpu.VMEM(inverse.shape, f32),
            pltpu.VMEM((4, *outs[0].shape), bf16),
            pltpu.SemaphoreType.DMA((count, 3)),
            pltpu.SemaphoreType.DMA((count, 2)),
            pltpu.SemaphoreType.DMA((len(late),)),
        ],
        compiler_params=pltpu.CompilerParams(vmem_limit_bytes=VMEM),
        cost_estimate=SMALL_COST,
        name="feed_back",
    )(low2, *args, *saved, *late, gain, small)


def weights_kernel(*refs):
    rows, grads, weights, refs = refs[:4], refs[4:8], refs[8:11], refs[11:]
    target, refs = refs[0], refs[1:]
    gate, up, down, low, low_t, low2, dgate, dup, hidden_t, result, sem, out_sem = refs
    block = rows[0].shape[0]
    at = [pl.ds(n * block, block) for n in range(4)]

    def fetch(n):
        return [
            start(rows[n], low.at[at[n], :], sem.at[n, 0]),
            start(grads[n], low2.at[at[n], :], sem.at[n, 1]),
        ]

    coming = [fetch(0)]
    own = [start(w, buffer, sem.at[4 + k, 0]) for k, (w, buffer) in enumerate(zip(weights, (gate, up, down)))]
    coming.append(fetch(1))
    for copy in own:
        copy.wait()
    for n in range(4):
        if n + 2 < 4:
            coming.append(fetch(n + 2))
        for copy in coming[n]:
            copy.wait()
        here = low[at[n], :]
        low_t[:, at[n]] = here.T
        gate_pre, up_pre = feed(here, gate[...], up[...])
        grad_hidden = dot_nt(low2[at[n], :], down[...])
        dgate[at[n], :], dup[at[n], :] = feed_back(grad_hidden, gate_pre, up_pre)
        hidden_t[:, at[n]] = hidden_of(gate_pre, up_pre).T
    going = []
    for k, (left, right) in enumerate([(low_t, dgate), (low_t, dup), (hidden_t, low2)]):
        result[k] = dot(left[...], right[...]).astype(bf16)
        rows_at = pl.ds(k * result.shape[1], result.shape[1])
        going.append(start(result.at[k], target.at[rows_at, :], out_sem.at[k]))
    for copy in going:
        copy.wait()


def weight_grads(rows, grads, gate, up, down):
    block, width = rows[0].shape
    length, hidden = 4 * block, gate.shape[1]
    return pl.pallas_call(
        weights_kernel,
        in_specs=[ANY] * 11,
        out_specs=ANY,
        out_shape=jax.ShapeDtypeStruct((3 * width, hidden), bf16),
        scratch_shapes=[
            pltpu.VMEM((width, hidden), bf16),
            pltpu.VMEM((width, hidden), bf16),
            pltpu.VMEM((hidden, width), bf16),
            pltpu.VMEM((length, width), bf16),
            pltpu.VMEM((width, length), bf16),
            pltpu.VMEM((length, width), bf16),
            pltpu.VMEM((length, hidden), bf16),
            pltpu.VMEM((length, hidden), bf16),
            pltpu.VMEM((hidden, length), bf16),
            pltpu.VMEM((3, width, hidden), bf16),
            pltpu.SemaphoreType.DMA((7, 2)),
            pltpu.SemaphoreType.DMA((3,)),
        ],
        compiler_params=pltpu.CompilerParams(vmem_limit_bytes=VMEM),
        cost_estimate=SMALL_COST,
        name="feed_weights",
    )(*rows, *grads, gate, up, down)


def local(
    tokens,
    segment_ids,
    query_weight,
    key_weight,
    value_weight,
    output_weight,
    attn_gain,
    attn_shift,
    gate_weight,
    up_weight,
    down_weight,
    mlp_gain,
    mlp_shift,
    cotangent,
):
    own = tokens[0]
    head_width = query_weight.shape[1]
    heads = head_width // HEAD_DIM
    group = lax.axis_size("tensor")
    block = own.shape[0]
    dp = lax.axis_size("dp")
    bits = list(range(int(math.log2(dp))))
    groups = [bits[:1]] + [bits[n : n + 2] for n in range(1, len(bits), 2)]

    near = lambda a: swap(a, "tensor", 1)
    far = lambda a: swap(a, "tensor", 2)

    share = gate_weight.shape[0] // dp
    at = lax.axis_index("dp") * share
    mine = jnp.concatenate(
        [lax.dynamic_slice_in_dim(w, at, share, 0) for w in (gate_weight, up_weight)], axis=1
    )
    far_own = far(own)
    near_own = near(own)
    near_weights = [near(w) for w in (gate_weight, up_weight, down_weight, output_weight)]
    angle_rate = ROPE_BASE ** (-(jnp.arange(HEAD_DIM // 2, dtype=f32) * 2.0 / HEAD_DIM))
    rates = jnp.concatenate([angle_rate, angle_rate, jnp.zeros(HEAD_DIM, f32)])[None, :]
    tables = ([w.T for w in (query_weight, key_weight, value_weight)], segment_ids, rates, heads)
    near_half = project([after(own, mine, *near_weights), near_own], 0, *tables)
    near_gate, near_up, near_down, near_out = near_weights
    far_own = after(far_own, near_half[0])
    both_own = near(far_own)
    mine = after(mine, far_own)
    far_mine = far(mine)
    x_full, qa, ka, va, cosine, sine = project([far_own, after(both_own, mine)], 2, *tables, done=near_half)
    far_mine = after(far_mine, qa)
    far_mixed = lax.all_gather(far_mine, "dp", axis=0, tiled=True)
    out_sent = after(output_weight, far_mine)
    far_out = far(out_sent)
    qa = after(qa, out_sent)

    def send(value, j):
        return swap(value[j * block : (j + 1) * block], "tensor", j)

    half = attend(qa, ka, va, 2 * block, 2 * block)
    far_out, *slices = all_after([far_out, *(half[0][j * block : (j + 1) * block] for j in (2, 3))], half[0])
    ctx_far = [swap(c, "tensor", j) for c, j in zip(slices, (2, 3))]
    both_out = near(far_out)
    ctx, qb = attend(after(qa, far_out, *slices), ka, va, 0, 2 * block, done=half)
    both_out, *ctx_far = all_after([both_out, *ctx_far], ctx)
    near_ctx = send(ctx, 1)
    down_sent = after(down_weight, *ctx_far)
    far_down = far(down_sent)
    ctx_parts = [ctx[:block], near_ctx, *ctx_far]
    outs = [output_weight, near_out, far_out, both_out]
    row = lambda a: a[None, :]

    first_norm, inverse, normed_low = mix(
        after(own, down_sent), ctx_parts, outs, row(attn_gain), row(attn_shift)
    )
    near_rows = near(normed_low)
    near_shards = [
        ((gate_weight, 0), (up_weight, 0), (down_weight, 0)),
        ((near_gate, 0), (near_up, 0), (near_down, 0)),
    ]
    *saved_a, half_way = forward(normed_low, near_shards)
    far_mixed, far_down = all_after([far_mixed, far_down], half_way)
    both_mixed, both_down = near(far_mixed), near(far_down)
    rows_sent = after(normed_low, far_down)
    far_rows = far(rows_sent)
    far_shard = [((far_mixed, 0), (far_mixed, 1), (far_down, 0))]
    *saved_b, more_way = forward(after(normed_low, rows_sent, far_mixed), far_shard)
    both_mixed, both_down = all_after([both_mixed, both_down], more_way)
    both_shard = [((both_mixed, 0), (both_mixed, 1), (both_down, 0))]
    shards = near_shards + far_shard + both_shard
    *saved_c, encoded, grad_second, grad_low, small = forward(
        normed_low,
        both_shard,
        (
            half_way,
            more_way,
            first_norm,
            cotangent[0],
            row(attn_gain),
            row(attn_shift),
            row(mlp_gain),
            row(mlp_shift),
        ),
    )
    near_rows, far_rows = all_after([near_rows, far_rows], grad_low)
    both_rows = near(far_rows)
    near_grads, far_grads = near(grad_low), far(grad_low)
    grad_first, grad_attn_low, own_ctx, *sent_ctx = backward(
        after(grad_low, far_rows),
        shards,
        (saved_a, saved_b, saved_c),
        grad_second,
        first_norm,
        inverse,
        outs,
        row(attn_gain),
        small,
    )
    near_grads, far_grads, both_rows = all_after([near_grads, far_grads, both_rows], grad_first)
    both_grads = near(far_grads)
    got_ctx = [swap(g, "tensor", j + 1) for j, g in enumerate(sent_ctx)]
    grad_feed = weight_grads(
        [after(normed_low, *sent_ctx), near_rows, far_rows, both_rows],
        [grad_low, near_grads, far_grads, both_grads],
        gate_weight,
        up_weight,
        down_weight,
    )
    grad_ctx = all_after(got_ctx, grad_feed)
    feed_part = lax.psum_scatter(after(grad_feed, *grad_ctx), "dp", scatter_dimension=0, tiled=True)
    grad_ctx = [own_ctx, *grad_ctx]
    grad_attn_low = after(grad_attn_low, grad_feed)
    sent = jnp.concatenate([dot_tn(ctx_parts[j], grad_attn_low) for j in (1, 3)], axis=0).astype(bf16)
    got = near(sent)
    kept = [dot_tn(ctx_parts[j], after(grad_attn_low, sent)) for j in (0, 2)]
    small = sum(g[block:].astype(f32) for g in grad_ctx)
    small = (small[: SMALL // 2] + small[SMALL // 2 :]).reshape(4, 4, head_width)
    small = small.transpose(1, 0, 2).reshape(4, -1).astype(bf16)
    got, *kept = all_after([got, *kept])
    sent = (kept[1] + got[head_width:].astype(f32)).astype(bf16)
    kept = kept[0] + got[:head_width].astype(f32)
    got = far(sent)

    dq, dk, dv = attend_back(qb, ka, va, all_after(grad_ctx, small, sent, kept), ctx, cosine, sine)
    grad_out = (kept + after(got, dq).astype(f32)).astype(bf16)
    joint = [dot_tn(g, x_full).astype(bf16) for g in (dq, dk, dv)]
    joint = jnp.concatenate([*joint, grad_out, small], axis=0)
    joint = jnp.pad(joint, ((0, -len(joint) % (8 * dp)), (0, 0)))
    sums = [Sum(split_rows(joint, "dp", groups[0]), groups)]
    parts = all_after([dq, dk, dv], *[s.sent for s in sums])
    weights = [query_weight, key_weight, value_weight]

    def token_part(j):
        return sum(dot_nt(g[j * block : (j + 1) * block], w) for g, w in zip(parts, weights))

    sent = jnp.concatenate([token_part(j).astype(bf16) for j in (1, 3)], axis=0)
    got = near(sent)
    parts = all_after(parts, sent)
    mine, far_sent = token_part(0), token_part(2)
    got, mine, far_sent, feed_part = take_round(sums, got, mine, far_sent, feed_part)
    feed_part = after(feed_part, *[s.sent for s in sums])
    grad_feed = lax.all_gather(feed_part, "dp", axis=0, tiled=True)
    far_sent = (far_sent + got[block:].astype(f32)).astype(bf16)
    got_rows = far(far_sent)
    mine = grad_first + mine + got[:block].astype(f32)
    (got_rows,) = take_round(sums, got_rows)
    grad_tokens = mine + got_rows.astype(f32)
    while any(s.result is None for s in sums):
        take_round([s for s in sums if s.result is None])
    joint = sums[0].result.astype(f32)
    grad_gate, grad_up, grad_down = jnp.split(grad_feed.astype(f32), 3, axis=0)
    grad_joint = [joint[n * head_width : (n + 1) * head_width] for n in range(4)]
    grad_out = grad_joint.pop()
    small = joint[4 * head_width : 4 * head_width + 4]
    grad_joint = [g.T for g in grad_joint]
    return (
        encoded[None],
        grad_tokens[None],
        *grad_joint,
        grad_out,
        small[0],
        small[1],
        grad_gate,
        grad_up,
        grad_down,
        small[2],
        small[3],
    )


def solution(mesh):
    rows, cols, lead = P("dp", "tensor", None), P(None, "tensor"), P("tensor", None)
    return jax.shard_map(
        local,
        mesh=mesh,
        in_specs=(
            rows, P("dp", None), cols, cols, cols, lead, P(), P(), cols, cols, lead, P(), P(), rows,
        ),
        out_specs=(
            rows, rows, cols, cols, cols, lead, P(), P(), cols, cols, lead, P(), P(),
        ),
        check_vma=False,
    )
```

time: 383 us -> 359 us (0.937)
  other arithmetic: 33.1 us -> 15.8 us
  waiting for transfers between devices: 85.2 us -> 99.9 us
  Pallas kernels: 137 us -> 151 us
  local copies, waits for them, and re-layouts: 36.8 us -> 23.9 us
  matrix products: 21.5 us -> 9.49 us
  starting transfers between devices: 48.2 us -> 37.4 us
    ppermute x53 -> x37, starting transfers between devices: 47.9 us -> 37 us  [swap(): return lax.ppermute(value, axis, [(i, i ^ bit) for i in range(size)])]
    ppermute x53 -> x37, waiting for transfers between devices: 85.1 us -> 94.9 us  [swap(): return lax.ppermute(value, axis, [(i, i ^ bit) for i in range(size)])]
    pallas_call x7 -> x5, Pallas kernels: 90.3 us -> 99.8 us  [the longest x1 46.6 us: attend_back(): pl.pallas_call(functools.partial(attend_back_kernel, heads), grid=(length...]
    concatenate x13 -> x3, other arithmetic: 9.48 us -> 1.02 us  [the longest x1 0.87 us: join_rows(): return jnp.concatenate([pick(p) for p in range(len(parts))], axis=0)]
    convert_element_type x20 -> x4, other arithmetic: 12.8 us -> 5.13 us  [the longest x2 2.78 us: sum_steps(): value = sum((g.astype(f32) for g in got), parts[0].astype(f32)).astype(bf16)]
    dot_general x12, matrix products: 11.5 us -> 4.37 us  [dot_nt(): return lax.dot_general(a, b, NT, preferred_element_type=f32)]
    reshape x3 -> x0, local copies, waits for them, and re-layouts: 6.36 us -> none  [the longest x2 4.25 us: turned(): return jnp.concatenate([w, swapped], axis=-1).reshape(width, heads * WIDE)]
    unnamed x124 -> x84, local copies, waits for them, and re-layouts: 18.4 us -> 12.2 us
  transfers between devices with their start and end apart: 55 -> 40, of which waited for: 18 -> 17; matrix products, arithmetic and copies ran while one was open for 17% -> 8% of each run, Pallas kernels for 36% -> 43%
where the time goes in v3:
time: 359 us; the launch traced here: 353 us
  Pallas kernels  151 us (42%)
  waiting for transfers between devices  99.9 us (28%)
  starting transfers between devices  37.4 us (10%)
  local copies, waits for them, and re-layouts  23.9 us (7%)
  other arithmetic  15.8 us (4%)
  between operations  14.7 us (4%)
  matrix products  9.49 us (3%)
    ppermute x37, waiting for transfers between devices, swap(): return lax.ppermute(value, axis, [(i, i ^ bit) for i in range(size)])  94.9 us
    pallas_call x1, Pallas kernels, attend_back(): pl.pallas_call(functools.partial(attend_back_kernel, heads), grid=(length...  46.6 us
    ppermute x37, starting transfers between devices, swap(): return lax.ppermute(value, axis, [(i, i ^ bit) for i in range(size)])  37 us
    pallas_call x3, Pallas kernels, forward(): pl.pallas_call(functools.partial(forward_kernel, firsts, bool(last)), in_...  26.2 us
    pallas_call x1, Pallas kernels, weight_grads(): pl.pallas_call(weights_kernel, in_specs=[ANY] * 11, out_specs=ANY, out_sh...  20.7 us
    pallas_call x2, Pallas kernels, attend(): pl.pallas_call(functools.partial(attend_kernel, heads), grid=(count // bl...  20.4 us
    pallas_call x2, Pallas kernels, project(): pl.pallas_call(functools.partial(project_kernel, heads, start, len(pieces...  16.6 us
    pallas_call x1, Pallas kernels, backward(): pl.pallas_call(functools.partial(backward_kernel, firsts, where), in_spec...  15.8 us
  transfers between devices with their start and end apart: 40, of which 17 were waited for; matrix products, arithmetic and copies ran while one was open for 8% of the time, Pallas kernels for 43%

profile of v3, /device:TPU:0, one launch (start us, length us, event | category | flops | bytes accessed | tf_op | source)
XLA Modules:
  0.0 352.5 jit_solution(14120786612078680526)
XLA Ops:
  11.4 2.9 collective-permute-start
  16.0 9.0 %project.2 = (bf16[2048,768]{1,0:T(8,128)(2,1)}, bf16[3,2048,128]{2,1,0:T(8,128)(2,1)}, bf16[3,2048,128]{2,1,0:T(8,128)(2,1)}, bf16[3,2048,128]{2,1,0:T(8,128)(2...) custom-call(s32[1]{0:T(128)} %bitcast.1.me_ref, bf16[512,768]{1,0:T(8,128)(2,1)} %bitcast.51, ...), custom_call_target="tpu_custom_call" | custom-call | flops 1048576 | bytes 65536 | tf_op jit(solution)/shard_map/project/pallas_call | solution.py:202
  25.0 7.5 %collective-permute-done.refs_0_ = bf16[512,768]{1,0:T(8,128)(2,1)} collective-permute-done((bf16[512,768]{1,0:T(8,128)(2,1)}, bf16[512,768]{1,0:T(8,128)(2,1)}, u32[]{:S(2)}, u32[]{:S(2)}) %collective-permute-start) | collective-permute-done | bytes 786464 | tf_op jit(solution)/shard_map/ppermute | solution.py:42
  35.1 7.7 %project.3 = (bf16[2048,768]{1,0:T(8,128)(2,1)}, bf16[3,2048,128]{2,1,0:T(8,128)(2,1)}, bf16[3,2048,128]{2,1,0:T(8,128)(2,1)}, bf16[3,2048,128]{2,1,0:T(8,128)(2...) custom-call(s32[1]{0:T(128)} %bitcast.1.me_ref, ...), custom_call_target="tpu_custom_call", output_to_operand_aliasing={{0}: (8, {}), {1}: (9, {}), {2}: (10, {}), {3}: (11, {}), {... | custom-call | flops 1048576 | bytes 65536 | tf_op jit(solution)/shard_map/project/pallas_call | solution.py:202
  49.2 10.2 %attend.2 = (bf16[2048,192]{1,0:T(8,128)(2,1)S(1)}, bf16[3,2048,128]{2,1,0:T(8,128)(2,1)S(1)}) custom-call(bf16[3,2048,128]{2,1,0:T(8,128)(2,1)S(1)} %copy-done.2, bf16[3,2048,128]{2,1,0:T(8,128)(2,1)S(1)} %copy-done, bf16[3,2048,128]{2,1,0:T(8,128)(2,1)S(1)} %copy-done.1), custom_call_target="tpu_custom_call" | custom-call | flops 1048576 | bytes 65536 | tf_op jit(solution)/shard_map/attend/pallas_call | solution.py:255
  61.4 10.2 %attend.3 = (bf16[2048,192]{1,0:T(8,128)(2,1)S(1)}, bf16[3,2048,128]{2,1,0:T(8,128)(2,1)S(1)}) custom-call(bf16[3,2048,128]{2,1,0:T(8,128)(2,1)S(1)} %copy-done.2, bf16[3,2048,128]{2,1,0:T(8,128)(2,1)S(1)} %copy-done, bf16[3,2048,128]{2,1,0:T(8,128)(2,1)S(1)} %copy-done.1, ...), custom_call_target="tpu_custom_call", output_to_operand_aliasing={{0}: (3, {}), {1}: (4, {})} | custom-call | flops 1048576 | bytes 65536 | tf_op jit(solution)/shard_map/attend/pallas_call | solution.py:255
  76.8 4.9 %mix.1 = (f32[512,768]{1,0:T(8,128)}, f32[512,128]{1,0:T(8,128)}, bf16[512,768]{1,0:T(8,128)(2,1)}) custom-call(bf16[512,768]{1,0:T(8,128)(2,1)} %bitcast.52, bf16[512,192]{1,0:T(8,128)(2,1)} %get-tuple-element.231.refs_0_, bf16[512,192]{1,0:T(8,128)(2,1)} %copy-done.28, bf16[512,192]{1,0:T(8,128)(2,1)} %copy-done.24, bf16[512,192]{1,0:T(8,128)(2,1)} %copy-done.26, ...), custom_call_target="tpu_custom_call" | custom-call | flops 1048576 | bytes 65536 | tf_op jit(solution)/shard_map/mix/pallas_call | solution.py:391
  81.7 9.2 %feed_forward.3 = (bf16[512,1536]{1,0:T(8,128)(2,1)}, bf16[512,1536]{1,0:T(8,128)(2,1)}, f32[512,768]{1,0:T(8,128)}) custom-call(bf16[512,768]{1,0:T(8,128)(2,1)} %get-tuple-element.172.low_ref.refs_0_, bf16[768,768]{1,0:T(8,128)(2,1)} %refs_8_.1, bf16[768,768]{1,0:T(8,128)(2,1)} %refs_9_.1, bf16[768,768]{1,0:T(8,128)(2,1)} %refs_10_.1, ...), custom_call_target="tpu_custom_call" | custom-call | flops 1048576 | bytes 65536 | tf_op jit(solution)/shard_map/feed_forward/pallas_call | solution.py:522
  90.9 11.0 %collective-permute-done.13.refs_2_.refs_8_ = bf16[768,768]{1,0:T(8,128)(2,1)} collective-permute-done((bf16[768,768]{1,0:T(8,128)(2,1)}, bf16[768,768]{1,0:T(8,128)(2,1)}, u32[]{:S(2)}, u32[]{:S(2)}) %collective-permute-start.13) | collective-permute-done | bytes 1179680 | tf_op jit(solution)/shard_map/ppermute | solution.py:42
  103.9 7.0 %feed_forward.4 = (bf16[512,768]{1,0:T(8,128)(2,1)}, bf16[512,768]{1,0:T(8,128)(2,1)}, f32[512,768]{1,0:T(8,128)}) custom-call(bf16[512,768]{1,0:T(8,128)(2,1)} %get-tuple-element.172.low_ref.refs_0_, bf16[768,1536]{1,0:T(8,128)(2,1)} %all-gather.3.cloned.1.call-done.refs_0_.refs_1_.refs_6_.refs_7_, ...), custom_call_target="tpu_custom_call" | custom-call | flops 1048576 | bytes 65536 | tf_op jit(solution)/shard_map/feed_forward/pallas_call | solution.py:522
  112.4 9.9 %feed_forward.5 = (bf16[512,768]{1,0:T(8,128)(2,1)}, bf16[512,768]{1,0:T(8,128)(2,1)}, bf16[512,768]{1,0:T(8,128)(2,1)}, f32[512,768]{1,0:T(8,128)}, bf16[512,768]{1,0:T(8,128)(2,1)}, /*index=5*/f32[2,768]{1,0:T(2,128)}) custom-call(bf16[512,768]{1,0:T(8,128)(2,1)} %get-tuple-element.172.low_ref.refs_0_, bf16[768,1536]{1,0:T(8,128)(2,1)} %copy-done.5, ...), custom_call_target="tpu_custom_call" | custom-call | flops 1048576 | bytes 65536 | tf_op jit(solution)/shard_map/feed_forward/pallas_call | solution.py:522
  124.6 15.8 %feed_back.1 = (f32[512,768]{1,0:T(8,128)}, bf16[512,768]{1,0:T(8,128)(2,1)}, bf16[544,192]{1,0:T(8,128)(2,1)}, bf16[544,192]{1,0:T(8,128)(2,1)}, bf16[544,192]{1,0:T(8,128)(2,1)}, /*index=5*/bf16[544,192]{1,0:T(8,128)(2,1)}) custom-call(bf16[512,768]{1,0:T(8,128)(2,1)} %get-tuple-element.156.low2_ref.refs_4_, bf16[768,768]{1,0:T(8,128)(2,1)} %refs_8_.1, ...), custom_call_target="tpu_custom_call" | custom-call | flops 1048576 | bytes 65536 | tf_op jit(solution)/shard_map/feed_back/pallas_call | solution.py:603
  145.7 20.7 %feed_weights.1 = bf16[2304,768]{1,0:T(8,128)(2,1)} custom-call(bf16[512,768]{1,0:T(8,128)(2,1)} %get-tuple-element.172.low_ref.refs_0_, bf16[512,768]{1,0:T(8,128)(2,1)} %collective-permute-done.16.refs_1_, bf16[512,768]{1,0:T(8,128)(2,1)} %collective-permute-done.17.refs_2_, bf16[512,768]{1,0:T(8,128)(2,1)} %copy-done.32, ...), custom_call_target="tpu_custom_call" | custom-call | flops 1048576 | bytes 65536 | tf_op jit(solution)/shard_map/feed_weights/pallas_call | solution.py:674
  173.5 46.6 %attend_back.1 = (bf16[2048,192]{1,0:T(8,128)(2,1)}, bf16[2048,192]{1,0:T(8,128)(2,1)}, bf16[2048,192]{1,0:T(8,128)(2,1)}) custom-call(bf16[3,2048,128]{2,1,0:T(8,128)(2,1)} %copy-done.4, bf16[3,2048,128]{2,1,0:T(8,128)(2,1)} %get-tuple-element.129.ka_ref, bf16[3,2048,128]{2,1,0:T(8,128)(2,1)} %get-tuple-element.130.va_ref, ...), custom_call_target="tpu_custom_call" | custom-call | flops 1048576 | bytes 65536 | tf_op jit(solution)/shard_map/attend_back/pallas_call | solution.py:333
  234.2 16.0 %collective-permute-done.27 = bf16[416,768]{1,0:T(8,128)(2,1)S(1)} collective-permute-done((bf16[416,768]{1,0:T(8,128)(2,1)S(1)}, bf16[416,768]{1,0:T(8,128)(2,1)S(1)}, u32[]{:S(2)}, u32[]{:S(2)}) %collective-permute-start.27) | collective-permute-done | bytes 639008 | tf_op jit(solution)/shard_map/ppermute | solution.py:42
  262.2 5.7 %collective-permute-done.29 = bf16[104,768]{1,0:T(8,128)(2,1)} collective-permute-done((bf16[104,768]{1,0:T(8,128)(2,1)}, bf16[104,768]{1,0:T(8,128)(2,1)}, u32[]{:S(2)}, u32[]{:S(2)}) %collective-permute-start.29) | collective-permute-done | bytes 159776 | tf_op jit(solution)/shard_map/ppermute | solution.py:42
  267.9 11.5 %collective-permute-done.30 = bf16[104,768]{1,0:T(8,128)(2,1)} collective-permute-done((bf16[104,768]{1,0:T(8,128)(2,1)S(1)}, bf16[104,768]{1,0:T(8,128)(2,1)}, u32[]{:S(2)}, u32[]{:S(2)}) %collective-permute-start.30) | collective-permute-done | bytes 159776 | tf_op jit(solution)/shard_map/ppermute | solution.py:42
  280.7 9.0 %collective-permute-start.33 = (bf16[104,768]{1,0:T(8,128)(2,1)S(1)}, bf16[104,768]{1,0:T(8,128)(2,1)S(1)}, u32[]{:S(2)}, u32[]{:S(2)}) collective-permute-start(bf16[104,768]{1,0:T(8,128)(2,1)S(1)} %add_convert_fusion.6), channel_id=1, source_target_pairs={{0,8},{4,12},{8,0},{12,4},{16,24},{20,28},{24,16},{28,20},{1,9},{5... | collective-permute-start | bytes 479240 | tf_op jit(solution)/shard_map/ppermute | solution.py:42
  292.7 3.7 %collective-permute-done.33 = bf16[104,768]{1,0:T(8,128)(2,1)S(1)} collective-permute-done((bf16[104,768]{1,0:T(8,128)(2,1)S(1)}, bf16[104,768]{1,0:T(8,128)(2,1)S(1)}, u32[]{:S(2)}, u32[]{:S(2)}) %collective-permute-start.33) | collective-permute-done | bytes 159776 | tf_op jit(solution)/shard_map/ppermute | solution.py:42
  296.3 7.6 %collective-permute-done.34 = bf16[104,768]{1,0:T(8,128)(2,1)} collective-permute-done((bf16[104,768]{1,0:T(8,128)(2,1)S(1)}, bf16[104,768]{1,0:T(8,128)(2,1)}, u32[]{:S(2)}, u32[]{:S(2)}) %collective-permute-start.34) | collective-permute-done | bytes 159776 | tf_op jit(solution)/shard_map/ppermute | solution.py:42
  306.8 2.9 add_bitcast_fusion
  309.6 22.4 %collective-permute-done.36 = bf16[416,768]{1,0:T(8,128)(2,1)} collective-permute-done((bf16[416,768]{1,0:T(8,128)(2,1)}, bf16[416,768]{1,0:T(8,128)(2,1)}, u32[]{:S(2)}, u32[]{:S(2)}) %collective-permute-start.36) | collective-permute-done | bytes 639008 | tf_op jit(solution)/shard_map/ppermute | solution.py:42
  335.7 5.0 %all-gather.5.cloned.1.call-done = bf16[2304,768]{1,0:T(8,128)(2,1)} async-done(((bf16[288,768]{1,0:T(8,128)(2,1)}), bf16[2304,768]{1,0:T(8,128)(2,1)}) %all-gather.5.cloned.1.call-update) | async-done | bytes 3538960 | tf_op jit(solution)/shard_map/all_gather | solution.py:856
  340.7 5.1 %fusion.27 = (f32[768,768]{1,0:T(8,128)}, f32[768,768]{1,0:T(8,128)}, f32[768,768]{1,0:T(8,128)}) fusion(bf16[2304,768]{1,0:T(8,128)(2,1)} %all-gather.5.cloned.1.call-done), kind=kLoop, calls=%fused_computation.73 | loop fusion | bytes 14155776 | tf_op jit(solution)/shard_map/split | solution.py:865
  (207 shorter events, 76.2 us)
Async XLA Ops:
  7.2 94.8 %all-gather.3.cloned.1.call-start = ((), (), s32[]{:S(2)}) async-start(), calls=%async_computation.1 | async-start | bytes 2654208 | tf_op jit(solution)/shard_map/all_gather | solution.py:746
  11.4 21.0 %collective-permute-start = (bf16[512,768]{1,0:T(8,128)(2,1)}, bf16[512,768]{1,0:T(8,128)(2,1)}, u32[]{:S(2)}, u32[]{:S(2)}) collective-permute-start(bf16[512,768]{1,0:T(8,128)(2,1)} %bitcast.50), channel_id=1, source_target_pairs={{0,2},{1,3},{2,0},{3,1},{4,6},{5,7},{6,4},{7,5},{8,10},{9,11},{10,... | collective-permute-start | bytes 2359304 | tf_op jit(solution)/shard_map/ppermute | solution.py:42
  42.8 208.2 %reduce-scatter.2.cloned.1.call-start = ((), (), s32[]{:S(2)}) async-start(), calls=%async_computation.2 | async-start | bytes 3981312 | tf_op jit(solution)/shard_map/reduce_scatter | solution.py:824
  43.1 16.3 %collective-permute-start.8 = (bf16[192,768]{1,0:T(8,128)(2,1)}, bf16[192,768]{1,0:T(8,128)(2,1)S(1)}, u32[]{:S(2)}, u32[]{:S(2)}) collective-permute-start(bf16[192,768]{1,0:T(8,128)(2,1)} %refs_21_.1), channel_id=1, source_target_pairs={{0,2},{1,3},{2,0},{3,1},{4,6},{5,7},{6,4},{7,5},{8,10},{9,11},{10,... | collective-permute-start | bytes 884744 | tf_op jit(solution)/shard_map/ppermute | solution.py:42
  59.5 14.0 %collective-permute-start.9 = (bf16[192,768]{1,0:T(8,128)(2,1)S(1)}, bf16[192,768]{1,0:T(8,128)(2,1)S(1)}, u32[]{:S(2)}, u32[]{:S(2)}) collective-permute-start(bf16[192,768]{1,0:T(8,128)(2,1)S(1)} %collective-permute-done.8.refs_6_.refs_23_), channel_id=1, source_target_pairs={{0,1},{1,0},{2,3},{3,2},{4,5},{5,4},{6,7},{7,6},{8,9},{9,8},{10,11... | collective-permute-start | bytes 884744 | tf_op jit(solution)/shard_map/ppermute | solution.py:42
  73.4 28.5 %collective-permute-start.13 = (bf16[768,768]{1,0:T(8,128)(2,1)}, bf16[768,768]{1,0:T(8,128)(2,1)}, u32[]{:S(2)}, u32[]{:S(2)}) collective-permute-start(bf16[768,768]{1,0:T(8,128)(2,1)} %refs_10_.1), channel_id=1, source_target_pairs={{0,2},{1,3},{2,0},{3,1},{4,6},{5,7},{6,4},{7,5},{8,10},{9,11},{10,... | collective-permute-start | bytes 3538952 | tf_op jit(solution)/shard_map/ppermute | solution.py:42
  102.5 19.9 %collective-permute-start.16 = (bf16[512,768]{1,0:T(8,128)(2,1)}, bf16[512,768]{1,0:T(8,128)(2,1)}, u32[]{:S(2)}, u32[]{:S(2)}) collective-permute-start(bf16[512,768]{1,0:T(8,128)(2,1)} %get-tuple-element.172.low_ref.refs_0_), channel_id=1, source_target_pairs={{0,1},{1,0},{2,3},{3,2},{4,5},{5,4},{6,7},{7,6},{8,9},{9,8},{10,11... | collective-permute-start | bytes 2359304 | tf_op jit(solution)/shard_map/ppermute | solution.py:42
  102.5 20.3 %collective-permute-start.17 = (bf16[512,768]{1,0:T(8,128)(2,1)}, bf16[512,768]{1,0:T(8,128)(2,1)}, u32[]{:S(2)}, u32[]{:S(2)}) collective-permute-start(bf16[512,768]{1,0:T(8,128)(2,1)} %get-tuple-element.172.low_ref.refs_0_), channel_id=1, source_target_pairs={{0,2},{1,3},{2,0},{3,1},{4,6},{5,7},{6,4},{7,5},{8,10},{9,11},{10,... | collective-permute-start | bytes 2359304 | tf_op jit(solution)/shard_map/ppermute | solution.py:42
  122.7 17.8 %collective-permute-start.23 = (bf16[512,768]{1,0:T(8,128)(2,1)}, bf16[512,768]{1,0:T(8,128)(2,1)S(1)}, u32[]{:S(2)}, u32[]{:S(2)}) collective-permute-start(bf16[512,768]{1,0:T(8,128)(2,1)} %collective-permute-done.17.refs_2_), channel_id=1, source_target_pairs={{0,1},{1,0},{2,3},{3,2},{4,5},{5,4},{6,7},{7,6},{8,9},{9,8},{10,11... | collective-permute-start | bytes 2359304 | tf_op jit(solution)/shard_map/ppermute | solution.py:42
  122.7 17.8 %collective-permute-start.21 = (bf16[512,768]{1,0:T(8,128)(2,1)}, bf16[512,768]{1,0:T(8,128)(2,1)S(1)}, u32[]{:S(2)}, u32[]{:S(2)}) collective-permute-start(bf16[512,768]{1,0:T(8,128)(2,1)} %get-tuple-element.156.low2_ref.refs_4_), channel_id=1, source_target_pairs={{0,1},{1,0},{2,3},{3,2},{4,5},{5,4},{6,7},{7,6},{8,9},{9,8},{10,11... | collective-permute-start | bytes 2359304 | tf_op jit(solution)/shard_map/ppermute | solution.py:42
  123.3 19.7 %collective-permute-start.22 = (bf16[512,768]{1,0:T(8,128)(2,1)}, bf16[512,768]{1,0:T(8,128)(2,1)S(1)}, u32[]{:S(2)}, u32[]{:S(2)}) collective-permute-start(bf16[512,768]{1,0:T(8,128)(2,1)} %get-tuple-element.156.low2_ref.refs_4_), channel_id=1, source_target_pairs={{0,2},{1,3},{2,0},{3,1},{4,6},{5,7},{6,4},{7,5},{8,10},{9,11},{10,... | collective-permute-start | bytes 2359304 | tf_op jit(solution)/shard_map/ppermute | solution.py:42
  142.9 23.6 %collective-permute-start.18 = (bf16[544,192]{1,0:T(8,128)(2,1)}, bf16[544,192]{1,0:T(8,128)(2,1)}, u32[]{:S(2)}, u32[]{:S(2)}) collective-permute-start(bf16[544,192]{1,0:T(8,128)(2,1)} %get-tuple-element.169), channel_id=1, source_target_pairs={{0,1},{1,0},{2,3},{3,2},{4,5},{5,4},{6,7},{7,6},{8,9},{9,8},{10,11... | collective-permute-start | bytes 626696 | tf_op jit(solution)/shard_map/ppermute | solution.py:42
  143.4 23.1 %collective-permute-start.19 = (bf16[544,192]{1,0:T(8,128)(2,1)}, bf16[544,192]{1,0:T(8,128)(2,1)}, u32[]{:S(2)}, u32[]{:S(2)}) collective-permute-start(bf16[544,192]{1,0:T(8,128)(2,1)} %get-tuple-element.170), channel_id=1, source_target_pairs={{0,2},{1,3},{2,0},{3,1},{4,6},{5,7},{6,4},{7,5},{8,10},{9,11},{10,... | collective-permute-start | bytes 626696 | tf_op jit(solution)/shard_map/ppermute | solution.py:42
  145.0 21.5 %collective-permute-start.20 = (bf16[544,192]{1,0:T(8,128)(2,1)}, bf16[544,192]{1,0:T(8,128)(2,1)}, u32[]{:S(2)}, u32[]{:S(2)}) collective-permute-start(bf16[544,192]{1,0:T(8,128)(2,1)} %get-tuple-element.171), channel_id=1, source_target_pairs={{0,3},{1,2},{2,1},{3,0},{4,7},{5,6},{6,5},{7,4},{8,11},{9,10},{10,... | collective-permute-start | bytes 626696 | tf_op jit(solution)/shard_map/ppermute | solution.py:42
  166.6 174.1 %all-gather.5.cloned.1.call-start = ((), (), s32[]{:S(2)}) async-start(), calls=%async_computation.3 | async-start | bytes 3981312 | tf_op jit(solution)/shard_map/all_gather | solution.py:856
  171.8 52.5 %collective-permute-start.26 = (bf16[192,768]{1,0:T(8,128)(2,1)S(1)}, bf16[192,768]{1,0:T(8,128)(2,1)}, u32[]{:S(2)}, u32[]{:S(2)}) collective-permute-start(bf16[192,768]{1,0:T(8,128)(2,1)S(1)} %get-tuple-element.242), channel_id=1, source_target_pairs={{0,2},{1,3},{2,0},{3,1},{4,6},{5,7},{6,4},{7,5},{8,10},{9,11},{10,... | collective-permute-start | bytes 884744 | tf_op jit(solution)/shard_map/ppermute | solution.py:42
  229.9 21.0 %collective-permute-start.28 = (bf16[1024,768]{1,0:T(8,128)(2,1)S(1)}, bf16[1024,768]{1,0:T(8,128)(2,1)}, u32[]{:S(2)}, u32[]{:S(2)}) collective-permute-start(bf16[1024,768]{1,0:T(8,128)(2,1)S(1)} %pad_maximum_fusion), channel_id=1, source_target_pairs={{0,1},{1,0},{2,3},{3,2},{4,5},{5,4},{6,7},{7,6},{8,9},{9,8},{10,11... | collective-permute-start | bytes 4718600 | tf_op jit(solution)/shard_map/ppermute | solution.py:42
  230.0 20.1 %collective-permute-start.27 = (bf16[416,768]{1,0:T(8,128)(2,1)S(1)}, bf16[416,768]{1,0:T(8,128)(2,1)S(1)}, u32[]{:S(2)}, u32[]{:S(2)}) collective-permute-start(bf16[416,768]{1,0:T(8,128)(2,1)S(1)} %pad_dynamic-slice_fusion.1), channel_id=1, source_target_pairs={{0,4},{4,0},{8,12},{12,8},{16,20},{20,16},{24,28},{28,24},{1,5},{5... | collective-permute-start | bytes 1916936 | tf_op jit(solution)/shard_map/ppermute | solution.py:42
  256.3 23.2 %collective-permute-start.32 = (bf16[512,768]{1,0:T(8,128)(2,1)}, bf16[512,768]{1,0:T(8,128)(2,1)}, u32[]{:S(2)}, u32[]{:S(2)}) collective-permute-start(bf16[512,768]{1,0:T(8,128)(2,1)} %add_convert_fusion), channel_id=1, source_target_pairs={{0,2},{1,3},{2,0},{3,1},{4,6},{5,7},{6,4},{7,5},{8,10},{9,11},{10,... | collective-permute-start | bytes 2359304 | tf_op jit(solution)/shard_map/ppermute | solution.py:42
  259.2 20.2 %collective-permute-start.30 = (bf16[104,768]{1,0:T(8,128)(2,1)S(1)}, bf16[104,768]{1,0:T(8,128)(2,1)}, u32[]{:S(2)}, u32[]{:S(2)}) collective-permute-start(bf16[104,768]{1,0:T(8,128)(2,1)S(1)} %get-tuple-element.239), channel_id=1, source_target_pairs={{0,16},{4,20},{8,24},{12,28},{16,0},{20,4},{24,8},{28,12},{1,17},{... | collective-permute-start | bytes 479240 | tf_op jit(solution)/shard_map/ppermute | solution.py:42
  261.6 17.8 %collective-permute-start.31 = (bf16[104,768]{1,0:T(8,128)(2,1)S(1)}, bf16[104,768]{1,0:T(8,128)(2,1)}, u32[]{:S(2)}, u32[]{:S(2)}) collective-permute-start(bf16[104,768]{1,0:T(8,128)(2,1)S(1)} %get-tuple-element.238), channel_id=1, source_target_pairs={{0,24},{4,28},{8,16},{12,20},{16,8},{20,12},{24,0},{28,4},{1,25},{... | collective-permute-start | bytes 479240 | tf_op jit(solution)/shard_map/ppermute | solution.py:42
  280.7 15.6 %collective-permute-start.33 = (bf16[104,768]{1,0:T(8,128)(2,1)S(1)}, bf16[104,768]{1,0:T(8,128)(2,1)S(1)}, u32[]{:S(2)}, u32[]{:S(2)}) collective-permute-start(bf16[104,768]{1,0:T(8,128)(2,1)S(1)} %add_convert_fusion.6), channel_id=1, source_target_pairs={{0,8},{4,12},{8,0},{12,4},{16,24},{20,28},{24,16},{28,20},{1,9},{5... | collective-permute-start | bytes 479240 | tf_op jit(solution)/shard_map/ppermute | solution.py:42
  289.8 14.2 %collective-permute-start.34 = (bf16[104,768]{1,0:T(8,128)(2,1)S(1)}, bf16[104,768]{1,0:T(8,128)(2,1)}, u32[]{:S(2)}, u32[]{:S(2)}) collective-permute-start(bf16[104,768]{1,0:T(8,128)(2,1)S(1)} %add_convert_fusion.6), channel_id=1, source_target_pairs={{0,16},{4,20},{8,24},{12,28},{16,0},{20,4},{24,8},{28,12},{1,17},{... | collective-permute-start | bytes 479240 | tf_op jit(solution)/shard_map/ppermute | solution.py:42
  306.8 25.3 %collective-permute-start.36 = (bf16[416,768]{1,0:T(8,128)(2,1)}, bf16[416,768]{1,0:T(8,128)(2,1)}, u32[]{:S(2)}, u32[]{:S(2)}) collective-permute-start(bf16[416,768]{1,0:T(8,128)(2,1)} %pad_maximum_fusion.1), channel_id=1, source_target_pairs={{0,4},{4,0},{8,12},{12,8},{16,20},{20,16},{24,28},{28,24},{1,5},{5... | collective-permute-start | bytes 1916936 | tf_op jit(solution)/shard_map/ppermute | solution.py:42
  (58 other events, 612.6 us)
Sparse Core Ops, SparseCore 0:
  42.9 53.5 all-gather.2
  166.7 82.9 reduce-scatter.1
  254.2 86.4 all-gather.4
